TPU v7x, 128 devices: a whole 4x4x4 slice. The times are simulated.
128 devices in a mesh: ctx: 32 (over y, z, core), tp: 4 (over x).
Axes of the slice: x: 4, y: 4, z: 4, core: 2. Of those that a mesh axis runs over, the one named last changes fastest.
Arguments:
- query_proj: bfloat16 [4096, 8192], P('ctx', 'tp'), may hold values from -6 to 6
- key_proj: bfloat16 [4096, 8192], P('ctx', 'tp'), may hold values from -6 to 6
- value_proj: bfloat16 [4096, 8192], P('ctx', 'tp'), may hold values from -6 to 6
- short_filter: float32 [3, 3, 8192], P(None, None, 'tp'), may hold values from -3 to 3
- skip_gain: float32 [8192], P('tp'), may hold values from -4 to 4
- pole_rates: float32 [8192, 16], P('tp'), as said below
- pole_residues: float32 [8192, 16], P('tp'), as said below
Outputs:
- mixer_out: bfloat16 [4096, 8192], P('ctx', 'tp')
Inputs may be any that keep to these rules, and one draw needn't show every extreme that they name: `pole_rates`: every decay rate lies between 0.3 / 4096 and 1 / 30. `pole_residues`: residues are real numbers of either sign.
All inputs are finite; a program needn't handle non-finite values.
Results may differ from a plain program's by a relative error of at most 0.02.
Values may be sent and summed in bfloat16 or wider, within the bound.
No kernel may reach another device: no remote copies, remote signals or barrier semaphores. Data moves between devices by JAX's collectives and lax.ppermute only.
A program may use at most 64 MiB of HBM per device.

v0:
```python
import math

import jax
import jax.numpy as jnp
from jax import lax
from jax.sharding import PartitionSpec as P

two_pi = 2.0 * math.pi
maximum_precision = lax.Precision.HIGHEST


def shifted(value, axis, by):
    size = lax.axis_size(axis)
    pairs = [(i, i + by) for i in range(size) if 0 <= i + by < size]
    return lax.ppermute(value, axis, pairs)


def angle_table(first_idx, second_idx, modulus):
    return (
        two_pi * (first_idx[:, None] * second_idx[None, :] % modulus).astype(jnp.float32) / modulus
    )


def featurize(signal, prior_rows, tap_weights):
    values = signal.astype(jnp.float32)
    extended = jnp.concatenate([prior_rows.astype(jnp.float32), values], 0)
    output_values = (
        tap_weights[0] * values + tap_weights[1] * extended[1:-1] + tap_weights[2] * extended[:-2]
    )
    return output_values.astype(jnp.bfloat16)


def fine_weights(length, sign_top):
    inner_idx = jnp.arange(length, dtype=jnp.int32)
    fine_angles = angle_table(inner_idx, inner_idx, length)
    cos_fine = jnp.cos(fine_angles)
    sin_fine = jnp.sin(fine_angles)
    upper = jnp.concatenate([cos_fine, sign_top * sin_fine], 1)
    lower = jnp.concatenate([-sign_top * sin_fine, cos_fine], 1)
    return jnp.concatenate([upper, lower], 0)


def forward(signal):
    blocks, chan_count, length = signal.shape
    entire_extent = 2 * blocks * length
    outer_idx = jnp.arange(2 * blocks, dtype=jnp.int32)
    block_number = jnp.arange(blocks, dtype=jnp.int32)
    inner_idx = jnp.arange(length, dtype=jnp.int32)
    coarse_angles = angle_table(outer_idx, block_number, 2 * blocks)
    transfer_matrix = jnp.stack([jnp.cos(coarse_angles), -jnp.sin(coarse_angles)])
    section_one = jnp.einsum("cap,pgs->cags", transfer_matrix, signal, precision=maximum_precision)
    twiddle = angle_table(outer_idx, inner_idx, entire_extent)[:, None, :]
    cosine = jnp.cos(twiddle)
    sine_part = jnp.sin(twiddle)
    real_part = section_one[0] * cosine + section_one[1] * sine_part
    imag_part = section_one[1] * cosine - section_one[0] * sine_part
    joined = jnp.concatenate([real_part, imag_part], -1).reshape(-1, 2 * length)
    result = jnp.dot(joined, fine_weights(length, -1.0), precision=maximum_precision)
    result = result.reshape(2 * blocks, chan_count, 2 * length)
    return (result[..., :length], result[..., length:])


def inverse(real_part, imag_part):
    twoblocks, chan_count, length = real_part.shape
    blocks = twoblocks // 2
    entire_extent = twoblocks * length
    outer_idx = jnp.arange(twoblocks, dtype=jnp.int32)
    block_number = jnp.arange(blocks, dtype=jnp.int32)
    inner_idx = jnp.arange(length, dtype=jnp.int32)
    joined = jnp.concatenate([real_part, imag_part], -1).reshape(-1, 2 * length)
    result = jnp.dot(joined, fine_weights(length, 1.0), precision=maximum_precision)
    result = result.reshape(twoblocks, chan_count, 2 * length)
    twiddle = angle_table(outer_idx, inner_idx, entire_extent)[:, None, :]
    cosine = jnp.cos(twiddle)
    sine_part = jnp.sin(twiddle)
    turned_real = result[..., :length] * cosine - result[..., length:] * sine_part
    turned_imag = result[..., :length] * sine_part + result[..., length:] * cosine
    coarse_angles = angle_table(block_number, outer_idx, twoblocks)
    transfer_matrix = jnp.stack([jnp.cos(coarse_angles), -jnp.sin(coarse_angles)])
    stacked_rows = jnp.stack([turned_real, turned_imag])
    return (
        jnp.einsum("nrm,nmez->rez", transfer_matrix, stacked_rows, precision=maximum_precision)
        / entire_extent
    )


def filter_rows(pole_rates, pole_residues, positions):

    def add_pole(pole_idx, running):
        decay_rate = lax.dynamic_slice_in_dim(pole_rates, pole_idx, 1, 1)
        residue = lax.dynamic_slice_in_dim(pole_residues, pole_idx, 1, 1)
        return running + residue * jnp.exp(-decay_rate * positions[None, :])

    empty_sum = jnp.zeros((pole_rates.shape[0], positions.shape[0]), jnp.float32)
    return lax.fori_loop(0, pole_rates.shape[1], add_pole, empty_sum)


def spectral(signal_in, side_in):
    data_real, data_imag = forward(signal_in.astype(jnp.float32))
    filt_real, filt_imag = forward(side_in)
    prod_real = data_real * filt_real - data_imag * filt_imag
    prod_imag = data_real * filt_imag + data_imag * filt_real
    return inverse(prod_real, prod_imag).astype(jnp.bfloat16)


def on_device(query_proj, key_proj, value_proj, short_filter, skip_gain, pole_rates, pole_residues):
    row_count, channels = query_proj.shape
    rim_rows = jnp.stack([query_proj[-2:], key_proj[-2:], value_proj[-2:]])
    before = shifted(rim_rows, "ctx", 1)
    query_feat = featurize(query_proj, before[0], short_filter[0])
    key_feat = featurize(key_proj, before[1], short_filter[1])
    value_feat = featurize(value_proj, before[2], short_filter[2])
    product = (key_feat.astype(jnp.float32) * value_feat.astype(jnp.float32)).astype(jnp.bfloat16)
    ctx_count = lax.axis_size("ctx")
    tp_count = lax.axis_size("tp")
    positions = (lax.axis_index("ctx") * row_count + jnp.arange(row_count, dtype=jnp.int32)).astype(
        jnp.float32
    )
    side_data = filter_rows(pole_rates, pole_residues, positions)
    columns = product.T
    side_width = side_data.shape[1]
    groups = ctx_count * tp_count
    per_group = channels // groups
    signal_in = lax.all_to_all(
        columns.reshape(groups, per_group, row_count),
        ("ctx", "tp"),
        split_axis=0,
        concat_axis=0,
        tiled=True,
    )
    side_in = lax.all_to_all(
        side_data.reshape(groups, per_group, side_width),
        ("ctx", "tp"),
        split_axis=0,
        concat_axis=0,
        tiled=True,
    )
    spread = spectral(
        signal_in.reshape(ctx_count, -1, row_count), side_in.reshape(ctx_count, -1, side_width)
    )
    returned = lax.all_to_all(
        spread.reshape(groups, per_group, row_count),
        ("ctx", "tp"),
        split_axis=0,
        concat_axis=0,
        tiled=True,
    )
    convolved = returned.reshape(channels, row_count).T
    mixer_out = query_feat.astype(jnp.float32) * (
        convolved.astype(jnp.float32) + skip_gain * product.astype(jnp.float32)
    )
    return mixer_out.astype(jnp.bfloat16)


def solution(mesh):
    placed = (
        P("ctx", "tp"),
        P("ctx", "tp"),
        P("ctx", "tp"),
        P(None, None, "tp"),
        P("tp"),
        P("tp", None),
        P("tp", None),
    )
    return jax.shard_map(
        on_device, mesh=mesh, in_specs=placed, out_specs=P("ctx", "tp"), check_vma=False
    )
```

profile of v0, /device:TPU:0, one launch (start us, length us, event | category | flops | bytes accessed | tf_op | source)
XLA Modules:
  0.0 162.3 jit_solution(6202109316691906075)
XLA Ops:
  1.6 1.3 collective-permute-start
  2.9 1.0 fusion.97
  4.0 1.3 copy.30
  5.3 1.3 copy.32
  6.8 1.1 copy.33
  7.9 1.1 bitcast_convert_fusion
  9.0 1.1 copy.31
  10.0 1.1 bitcast_convert_fusion.1
  11.1 4.2 %multiply_convert_fusion = bf16[128,2048]{0,1:T(8,128)(2,1)} fusion(f32[128,2048]{0,1:T(8,128)S(1)} %convert_element_type.168, f32[2,2048]{0,1:T(8,128)S(1)} %bitcast_convert_fusion, f32[2048]{0:T(1024)S(1)} %bitcast.120, f32[2048]{0:T(1024)S(1)} %bitcast.121, f32[2048]{0:T(1024)S(1)} %bitcast.116, f32[128,2048]{0,1:T(8,128)S(1)} %convert_element_type.163, ...), kind=kLoop, calls=%fused_computation.67 | loop fusion | flops 5242880 | bytes 2703360 | tf_op jit(solution)/shard_map/convert_element_type | solution.py:113
  15.4 12.9 %all-to-all-start = ((bf16[128,16,128]{2,1,0:T(8,128)(2,1)}), bf16[128,16,128]{2,1,0:T(8,128)(2,1)S(1)}, u32[]{:S(2)}, u32[]{:S(2)}) async-start(bf16[128,16,128]{2,1,0:T(8,128)(2,1)} %bitcast.19), calls=%async_computation | async-start | bytes 1048576 | tf_op jit(solution)/shard_map/all_to_all | solution.py:124
  28.3 54.2 %while.14 = (s32[]{:T(128)}, f32[2048,128]{1,0:T(8,128)}, f32[2048,16]{0,1:T(8,128)}, f32[2048,16]{0,1:T(8,128)}, s32[]{:T(128)}, /*index=5*/s32[]{:T(128)}, s32[]{:T(128)}) while((s32[]{:T(128)}, f32[2048,128]{1,0:T(8,128)}, f32[2048,16]{0,1:T(8,128)}, f32[2048,16]{0,1:T(8,128)}, s32[]{:T(128)}, /*index=5*/s32[]{:T(128)}, ...), condition=%wide.region_1.0_spmd.clone, body=%wide.region_0.0_spmd.clone.sunk | while | flops 1050883 | bytes 2147423 | solution.py:95
  28.4 0.9 dynamic-slice_negate_fusion.2
  29.3 1.5 select_add_fusion.2
  30.8 0.9 dynamic-slice_negate_fusion.2
  31.7 2.5 %select_add_fusion.2 = f32[2048,128]{1,0:T(8,128)} fusion(f32[2048,128]{1,0:T(8,128)} %get-tuple-element.208, f32[128]{0:T(128)S(1)} %add_convert_fusion.2, f32[2048]{0:T(1024)S(1)} %bitcast.111, f32[2048]{0:T(1024)S(1)} %bitcast.112, pred[]{:T(512)S(6)} %compare.30), kind=kLoop, calls=%fused_computation.1.clone.1 | loop fusion | flops 1048576 | bytes 2114049 | tf_op jit(solution)/shard_map/while/body/eval_jaxpr/add | solution.py:92
  34.2 0.9 dynamic-slice_negate_fusion.2
  35.2 2.5 %select_add_fusion.2 = f32[2048,128]{1,0:T(8,128)} fusion(f32[2048,128]{1,0:T(8,128)} %get-tuple-element.208, f32[128]{0:T(128)S(1)} %add_convert_fusion.2, f32[2048]{0:T(1024)S(1)} %bitcast.111, f32[2048]{0:T(1024)S(1)} %bitcast.112, pred[]{:T(512)S(6)} %compare.30), kind=kLoop, calls=%fused_computation.1.clone.1 | loop fusion | flops 1048576 | bytes 2114049 | tf_op jit(solution)/shard_map/while/body/eval_jaxpr/add | solution.py:92
  37.7 0.9 dynamic-slice_negate_fusion.2
  38.6 2.5 %select_add_fusion.2 = f32[2048,128]{1,0:T(8,128)} fusion(f32[2048,128]{1,0:T(8,128)} %get-tuple-element.208, f32[128]{0:T(128)S(1)} %add_convert_fusion.2, f32[2048]{0:T(1024)S(1)} %bitcast.111, f32[2048]{0:T(1024)S(1)} %bitcast.112, pred[]{:T(512)S(6)} %compare.30), kind=kLoop, calls=%fused_computation.1.clone.1 | loop fusion | flops 1048576 | bytes 2114049 | tf_op jit(solution)/shard_map/while/body/eval_jaxpr/add | solution.py:92
  41.1 0.9 dynamic-slice_negate_fusion.2
  42.0 2.5 %select_add_fusion.2 = f32[2048,128]{1,0:T(8,128)} fusion(f32[2048,128]{1,0:T(8,128)} %get-tuple-element.208, f32[128]{0:T(128)S(1)} %add_convert_fusion.2, f32[2048]{0:T(1024)S(1)} %bitcast.111, f32[2048]{0:T(1024)S(1)} %bitcast.112, pred[]{:T(512)S(6)} %compare.30), kind=kLoop, calls=%fused_computation.1.clone.1 | loop fusion | flops 1048576 | bytes 2114049 | tf_op jit(solution)/shard_map/while/body/eval_jaxpr/add | solution.py:92
  44.6 0.9 dynamic-slice_negate_fusion.2
  45.5 2.5 %select_add_fusion.2 = f32[2048,128]{1,0:T(8,128)} fusion(f32[2048,128]{1,0:T(8,128)} %get-tuple-element.208, f32[128]{0:T(128)S(1)} %add_convert_fusion.2, f32[2048]{0:T(1024)S(1)} %bitcast.111, f32[2048]{0:T(1024)S(1)} %bitcast.112, pred[]{:T(512)S(6)} %compare.30), kind=kLoop, calls=%fused_computation.1.clone.1 | loop fusion | flops 1048576 | bytes 2114049 | tf_op jit(solution)/shard_map/while/body/eval_jaxpr/add | solution.py:92
  48.9 2.5 %select_add_fusion.2 = f32[2048,128]{1,0:T(8,128)} fusion(f32[2048,128]{1,0:T(8,128)} %get-tuple-element.208, f32[128]{0:T(128)S(1)} %add_convert_fusion.2, f32[2048]{0:T(1024)S(1)} %bitcast.111, f32[2048]{0:T(1024)S(1)} %bitcast.112, pred[]{:T(512)S(6)} %compare.30), kind=kLoop, calls=%fused_computation.1.clone.1 | loop fusion | flops 1048576 | bytes 2114049 | tf_op jit(solution)/shard_map/while/body/eval_jaxpr/add | solution.py:92
  52.4 2.5 %select_add_fusion.2 = f32[2048,128]{1,0:T(8,128)} fusion(f32[2048,128]{1,0:T(8,128)} %get-tuple-element.208, f32[128]{0:T(128)S(1)} %add_convert_fusion.2, f32[2048]{0:T(1024)S(1)} %bitcast.111, f32[2048]{0:T(1024)S(1)} %bitcast.112, pred[]{:T(512)S(6)} %compare.30), kind=kLoop, calls=%fused_computation.1.clone.1 | loop fusion | flops 1048576 | bytes 2114049 | tf_op jit(solution)/shard_map/while/body/eval_jaxpr/add | solution.py:92
  55.8 2.5 %select_add_fusion.2 = f32[2048,128]{1,0:T(8,128)} fusion(f32[2048,128]{1,0:T(8,128)} %get-tuple-element.208, f32[128]{0:T(128)S(1)} %add_convert_fusion.2, f32[2048]{0:T(1024)S(1)} %bitcast.111, f32[2048]{0:T(1024)S(1)} %bitcast.112, pred[]{:T(512)S(6)} %compare.30), kind=kLoop, calls=%fused_computation.1.clone.1 | loop fusion | flops 1048576 | bytes 2114049 | tf_op jit(solution)/shard_map/while/body/eval_jaxpr/add | solution.py:92
  58.4 0.9 dynamic-slice_negate_fusion.2
  59.3 2.5 %select_add_fusion.2 = f32[2048,128]{1,0:T(8,128)} fusion(f32[2048,128]{1,0:T(8,128)} %get-tuple-element.208, f32[128]{0:T(128)S(1)} %add_convert_fusion.2, f32[2048]{0:T(1024)S(1)} %bitcast.111, f32[2048]{0:T(1024)S(1)} %bitcast.112, pred[]{:T(512)S(6)} %compare.30), kind=kLoop, calls=%fused_computation.1.clone.1 | loop fusion | flops 1048576 | bytes 2114049 | tf_op jit(solution)/shard_map/while/body/eval_jaxpr/add | solution.py:92
  62.7 2.5 %select_add_fusion.2 = f32[2048,128]{1,0:T(8,128)} fusion(f32[2048,128]{1,0:T(8,128)} %get-tuple-element.208, f32[128]{0:T(128)S(1)} %add_convert_fusion.2, f32[2048]{0:T(1024)S(1)} %bitcast.111, f32[2048]{0:T(1024)S(1)} %bitcast.112, pred[]{:T(512)S(6)} %compare.30), kind=kLoop, calls=%fused_computation.1.clone.1 | loop fusion | flops 1048576 | bytes 2114049 | tf_op jit(solution)/shard_map/while/body/eval_jaxpr/add | solution.py:92
  66.2 2.5 %select_add_fusion.2 = f32[2048,128]{1,0:T(8,128)} fusion(f32[2048,128]{1,0:T(8,128)} %get-tuple-element.208, f32[128]{0:T(128)S(1)} %add_convert_fusion.2, f32[2048]{0:T(1024)S(1)} %bitcast.111, f32[2048]{0:T(1024)S(1)} %bitcast.112, pred[]{:T(512)S(6)} %compare.30), kind=kLoop, calls=%fused_computation.1.clone.1 | loop fusion | flops 1048576 | bytes 2114049 | tf_op jit(solution)/shard_map/while/body/eval_jaxpr/add | solution.py:92
  69.6 2.5 %select_add_fusion.2 = f32[2048,128]{1,0:T(8,128)} fusion(f32[2048,128]{1,0:T(8,128)} %get-tuple-element.208, f32[128]{0:T(128)S(1)} %add_convert_fusion.2, f32[2048]{0:T(1024)S(1)} %bitcast.111, f32[2048]{0:T(1024)S(1)} %bitcast.112, pred[]{:T(512)S(6)} %compare.30), kind=kLoop, calls=%fused_computation.1.clone.1 | loop fusion | flops 1048576 | bytes 2114049 | tf_op jit(solution)/shard_map/while/body/eval_jaxpr/add | solution.py:92
  73.1 2.5 %select_add_fusion.2 = f32[2048,128]{1,0:T(8,128)} fusion(f32[2048,128]{1,0:T(8,128)} %get-tuple-element.208, f32[128]{0:T(128)S(1)} %add_convert_fusion.2, f32[2048]{0:T(1024)S(1)} %bitcast.111, f32[2048]{0:T(1024)S(1)} %bitcast.112, pred[]{:T(512)S(6)} %compare.30), kind=kLoop, calls=%fused_computation.1.clone.1 | loop fusion | flops 1048576 | bytes 2114049 | tf_op jit(solution)/shard_map/while/body/eval_jaxpr/add | solution.py:92
  76.5 2.5 %select_add_fusion.2 = f32[2048,128]{1,0:T(8,128)} fusion(f32[2048,128]{1,0:T(8,128)} %get-tuple-element.208, f32[128]{0:T(128)S(1)} %add_convert_fusion.2, f32[2048]{0:T(1024)S(1)} %bitcast.111, f32[2048]{0:T(1024)S(1)} %bitcast.112, pred[]{:T(512)S(6)} %compare.30), kind=kLoop, calls=%fused_computation.1.clone.1 | loop fusion | flops 1048576 | bytes 2114049 | tf_op jit(solution)/shard_map/while/body/eval_jaxpr/add | solution.py:92
  80.0 2.5 %select_add_fusion.2 = f32[2048,128]{1,0:T(8,128)} fusion(f32[2048,128]{1,0:T(8,128)} %get-tuple-element.208, f32[128]{0:T(128)S(1)} %add_convert_fusion.2, f32[2048]{0:T(1024)S(1)} %bitcast.111, f32[2048]{0:T(1024)S(1)} %bitcast.112, pred[]{:T(512)S(6)} %compare.30), kind=kLoop, calls=%fused_computation.1.clone.1 | loop fusion | flops 1048576 | bytes 2114049 | tf_op jit(solution)/shard_map/while/body/eval_jaxpr/add | solution.py:92
  82.5 9.9 %all-to-all-start.1 = ((f32[128,16,128]{2,1,0:T(8,128)}), f32[128,16,128]{2,1,0:T(8,128)S(1)}, u32[]{:S(2)}, u32[]{:S(2)}) async-start(f32[128,16,128]{2,1,0:T(8,128)} %bitcast.26), calls=%async_computation.1 | async-start | bytes 2097152 | tf_op jit(solution)/shard_map/all_to_all | solution.py:131
  93.3 3.8 %fusion.45 = f32[2,64,64,128]{3,1,2,0:T(8,128)} fusion(bf16[32,64,128]{2,1,0:T(8,128)(2,1)S(1)} %bitcast.110, f32[1,64,32]{1,2,0:T(8,128)S(1)} %get-tuple-element.157, f32[1,64,32]{1,2,0:T(8,128)S(1)} %get-tuple-element.158), kind=kOutput, calls=%fused_computation.71 | convolution fusion | flops 402657280 | bytes 4734976 | tf_op jit(solution)/shard_map/cap,pgs->cags/dot_general | solution.py:51
  97.1 14.1 %all-to-all-done.1 = f32[128,16,128]{2,1,0:T(8,128)S(1)} async-done(((f32[128,16,128]{2,1,0:T(8,128)}), f32[128,16,128]{2,1,0:T(8,128)S(1)}, u32[]{:S(2)}, u32[]{:S(2)}) %all-to-all-start.1) | async-done | bytes 1048608 | tf_op jit(solution)/shard_map/all_to_all | solution.py:131
  111.2 3.7 %fusion.42 = f32[2,64,64,128]{3,1,2,0:T(8,128)S(1)} fusion(f32[32,64,128]{2,1,0:T(8,128)S(1)} %bitcast.109, f32[1,64,32]{1,2,0:T(8,128)S(1)} %get-tuple-element.157, f32[1,64,32]{1,2,0:T(8,128)S(1)} %get-tuple-element.158), kind=kOutput, calls=%fused_computation.64 | convolution fusion | flops 402657280 | bytes 5259264 | tf_op jit(solution)/shard_map/cap,pgs->cags/dot_general | solution.py:51
  114.9 2.0 %multiply_add_fusion.2 = (f32[64,64,128]{2,0,1:T(8,128)S(1)}, f32[64,64,128]{2,0,1:T(8,128)S(1)}, f32[64,64,128]{2,0,1:T(8,128)S(1)}, f32[64,64,128]{2,0,1:T(8,128)S(1)}) fusion(f32[2,64,64,128]{3,1,2,0:T(8,128)S(1)} %copy-done, f32[64,128]{1,0:T(8,128)S(1)} %get-tuple-element.159, f32[64,128]{1,0:T(8,128)S(1)} %get-tuple-element.160, ...), kind=kLoop, calls=%fused_computation.35 | loop fusion | flops 6291456 | bytes 16842752 | tf_op jit(solution)/shard_map/add | solution.py:55
  117.7 5.9 %fusion.10 = f32[64,64,256]{2,1,0:T(8,128)S(1)} fusion(f32[64,64,256]{2,0,1:T(8,128)S(1)} %pad_maximum_fusion, f32[128,128]{1,0:T(8,128)S(1)} %fusion.71, f32[128,128]{1,0:T(8,128)S(1)} %get-tuple-element.162, f32[128,128]{1,0:T(8,128)S(1)} %get-tuple-element.161), kind=kOutput, calls=%fused_computation.16 | convolution fusion | flops 3221422080 | bytes 8585216 | tf_op jit(solution)/shard_map/dot_general | solution.py:58
  123.6 5.7 %fusion.8 = f32[64,64,256]{2,1,0:T(8,128)S(1)} fusion(f32[64,64,256]{2,0,1:T(8,128)S(1)} %pad_maximum_fusion.1, f32[128,128]{1,0:T(8,128)S(1)} %fusion.71, f32[128,128]{1,0:T(8,128)S(1)} %get-tuple-element.162, f32[128,128]{1,0:T(8,128)S(1)} %get-tuple-element.161), kind=kOutput, calls=%fused_computation.14 | convolution fusion | flops 3221422080 | bytes 8585216 | tf_op jit(solution)/shard_map/dot_general | solution.py:58
  130.3 5.8 %fusion.6 = f32[64,64,256]{2,0,1:T(8,128)S(1)} fusion(f32[64,64,256]{2,1,0:T(8,128)S(1)} %pad_maximum_fusion.2, f32[128,128]{1,0:T(8,128)S(1)} %fusion.71, f32[128,128]{1,0:T(8,128)S(1)} %get-tuple-element.161, f32[128,128]{1,0:T(8,128)S(1)} %get-tuple-element.162), kind=kOutput, calls=%fused_computation.12 | convolution fusion | flops 3221422080 | bytes 8585216 | tf_op jit(solution)/shard_map/dot_general | solution.py:71
  136.8 2.2 %fusion.18 = bf16[32,64,128]{2,0,1:T(8,128)(2,1)S(1)} fusion(f32[1,64,64,128]{3,1,2,0:T(8,128)S(1)} %get-tuple-element.136, f32[1,64,64,128]{3,1,2,0:T(8,128)S(1)} %get-tuple-element.135, f32[1,32,64]{2,1,0:T(8,128)S(1)} %get-tuple-element.163, f32[1,32,64]{2,1,0:T(8,128)S(1)} %get-tuple-element.164), kind=kOutput, calls=%fused_computation.38 | convolution fusion | flops 404230144 | bytes 4734976 | tf_op jit(solution)/shard_map/nrm,nmez->rez/dot_general | solution.py:82
  139.0 1.0 copy.41
  140.0 4.6 %all-to-all-start.2 = ((bf16[128,16,128]{2,1,0:T(8,128)(2,1)}), bf16[128,16,128]{2,1,0:T(8,128)(2,1)S(1)}, u32[]{:S(2)}, u32[]{:S(2)}) async-start(bf16[128,16,128]{2,1,0:T(8,128)(2,1)} %bitcast.36), calls=%async_computation.2 | async-start | bytes 1048576 | tf_op jit(solution)/shard_map/all_to_all | solution.py:141
  145.4 12.5 %all-to-all-done.2 = bf16[128,16,128]{2,1,0:T(8,128)(2,1)S(1)} async-done(((bf16[128,16,128]{2,1,0:T(8,128)(2,1)}), bf16[128,16,128]{2,1,0:T(8,128)(2,1)S(1)}, u32[]{:S(2)}, u32[]{:S(2)}) %all-to-all-start.2) | async-done | bytes 524320 | tf_op jit(solution)/shard_map/all_to_all | solution.py:141
  157.9 3.3 %fusion.41 = bf16[128,2048]{0,1:T(8,128)(2,1)S(1)} fusion(bf16[128,2048]{0,1:T(8,128)(2,1)} %multiply_convert_fusion, f32[128,2048]{0,1:T(8,128)S(1)} %convert_element_type.156, f32[2,2048]{0,1:T(8,128)S(1)} %bitcast_convert_fusion.2, bf16[128,16,128]{2,1,0:T(8,128)(2,1)S(1)} %all-to-all-done.2, f32[2048]{0:T(1024)S(1)} %copy-done.2, f32[2048]{0:T(1024)S(1)} %bitcast.114, ...), kind=kLoop, calls=%fused_computation.63 | loop fusion | flops 3932160 | bytes 2670592 | tf_op jit(solution)/shard_map/convert_element_type | solution.py:152
  161.3 1.0 copy.42
  (54 shorter events, 13.9 us)
Async XLA Ops:
  1.6 5.2 %collective-permute-start = (bf16[3,2,2048]{2,1,0:T(2,128)(2,1)S(1)}, bf16[3,2,2048]{2,1,0:T(2,128)(2,1)S(1)}, u32[]{:S(2)}, u32[]{:S(2)}) collective-permute-start(bf16[3,2,2048]{2,1,0:T(2,128)(2,1)S(1)} %pad_maximum_fusion.11), channel_id=1, source_target_pairs={{0,4},{4,8},{8,12},{12,16},{16,20},{20,24},{24,28},{28,32},{32,36}... | collective-permute-start | bytes 73736 | tf_op jit(solution)/shard_map/ppermute | solution.py:15
  15.4 67.1 %all-to-all-start = ((bf16[128,16,128]{2,1,0:T(8,128)(2,1)}), bf16[128,16,128]{2,1,0:T(8,128)(2,1)S(1)}, u32[]{:S(2)}, u32[]{:S(2)}) async-start(bf16[128,16,128]{2,1,0:T(8,128)(2,1)} %bitcast.19), calls=%async_computation | async-start | bytes 1048576 | tf_op jit(solution)/shard_map/all_to_all | solution.py:124
  82.5 28.7 %all-to-all-start.1 = ((f32[128,16,128]{2,1,0:T(8,128)}), f32[128,16,128]{2,1,0:T(8,128)S(1)}, u32[]{:S(2)}, u32[]{:S(2)}) async-start(f32[128,16,128]{2,1,0:T(8,128)} %bitcast.26), calls=%async_computation.1 | async-start | bytes 2097152 | tf_op jit(solution)/shard_map/all_to_all | solution.py:131
  111.2 3.7 %copy-start = (f32[2,64,64,128]{3,1,2,0:T(8,128)S(1)}, f32[2,64,64,128]{3,1,2,0:T(8,128)}, u32[]{:S(2)}) copy-start(f32[2,64,64,128]{3,1,2,0:T(8,128)} %fusion.45) | copy-start | bytes 12582916
  139.0 5.6 %copy-start.1 = (bf16[128,2048]{1,0:T(8,128)(2,1)S(1)}, bf16[128,2048]{1,0:T(8,128)(2,1)}, u32[]{:S(2)}) copy-start(bf16[128,2048]{1,0:T(8,128)(2,1)} %param.9) | copy-start | bytes 1572868
  140.0 17.9 %all-to-all-start.2 = ((bf16[128,16,128]{2,1,0:T(8,128)(2,1)}), bf16[128,16,128]{2,1,0:T(8,128)(2,1)S(1)}, u32[]{:S(2)}, u32[]{:S(2)}) async-start(bf16[128,16,128]{2,1,0:T(8,128)(2,1)} %bitcast.36), calls=%async_computation.2 | async-start | bytes 1048576 | tf_op jit(solution)/shard_map/all_to_all | solution.py:141
  144.9 13.0 %copy-start.2 = (f32[2048]{0:T(1024)S(1)}, f32[2048]{0:T(1024)}, u32[]{:S(2)}) copy-start(f32[2048]{0:T(1024)} %param.13) | copy-start | bytes 24580
where the time goes:
time: 165 us; the launch traced here: 162 us
  other arithmetic  69.3 us (42%)
  starting transfers between devices  28.8 us (17%)
  matrix products  27 us (16%)
  waiting for transfers between devices  26.6 us (16%)
  local copies, waits for them, and re-layouts  9.98 us (6%)
    add x16, other arithmetic, add_pole(): return running + residue * jnp.exp(-decay_rate * positions[None, :])  39.6 us
    neg x16, other arithmetic, add_pole(): return running + residue * jnp.exp(-decay_rate * positions[None, :])  14.2 us
    all_to_all x1, waiting for transfers between devices, on_device(): lax.all_to_all(side_data.reshape(groups, per_group, side_width), ('ctx',...  14.1 us
    all_to_all x1, starting transfers between devices, on_device(): lax.all_to_all(columns.reshape(groups, per_group, row_count), ('ctx', 'tp...  12.9 us
    all_to_all x1, waiting for transfers between devices, on_device(): lax.all_to_all(spread.reshape(groups, per_group, row_count), ('ctx', 'tp'...  12.5 us
    dot_general x2, matrix products, forward(): jnp.dot(joined, fine_weights(length, -1.0), precision=maximum_precision)  11.5 us
    all_to_all x1, starting transfers between devices, on_device(): lax.all_to_all(side_data.reshape(groups, per_group, side_width), ('ctx',...  9.94 us
    dot_general x2, matrix products, forward(): jnp.einsum('cap,pgs->cags', transfer_matrix, signal, precision=maximum_pr...  7.47 us
  transfers between devices with their start and end apart: 4, of which 2 were waited for; matrix products, arithmetic and copies ran while one was open for 39% of the time, Pallas kernels for 0%

commit v1 on v0

v1 whole, which is shorter than its diff:
```python
import functools

import jax
import jax.numpy as jnp
import numpy as np
from jax import lax
from jax.experimental import pallas as pl
from jax.experimental.pallas import tpu as pltpu
from jax.sharding import PartitionSpec as P

import ml_dtypes

RATE_MIN, RATE_MAX = 0.3 / 4096, 1.0 / 30.0
SHIFT = 1.2e-3
NODES = 24
RANK = 8
PAD = 80
F32 = jnp.float32
BF16 = jnp.bfloat16


def split_np(values):
    high = values.astype(np.float32).astype(ml_dtypes.bfloat16)
    low = (values - high.astype(np.float64)).astype(np.float32).astype(ml_dtypes.bfloat16)
    return high, low


def log_range():
    low, high = np.log(RATE_MIN + SHIFT), np.log(RATE_MAX + SHIFT)
    return (low + high) / 2, (high - low) / 2


@functools.lru_cache(maxsize=None)
def tables(block, devices):
    mid, half = log_range()
    order = np.arange(NODES)
    node_x = np.cos((2 * order + 1) * np.pi / (2 * NODES))
    nodes = np.exp(mid + half * node_x) - SHIFT
    weights = np.full(NODES, 2.0 / NODES)
    weights[0] = 1.0 / NODES
    to_nodes = np.cos(order[None, :] * np.arccos(node_x)[:, None]) * weights[None, :]

    lags = np.arange(block)
    rates = np.linspace(RATE_MIN, RATE_MAX, 1500)
    basis = np.linalg.svd(np.exp(-np.outer(rates, lags)), full_matrices=False)[2][:RANK]
    shares = np.exp(-np.outer(nodes, lags)) @ basis.T
    mix = np.concatenate([to_nodes, shares.T @ to_nodes], 0).astype(np.float32)

    lag = lags[:, None] - lags[None, :]
    toeplitz = np.where(lag >= 0, basis[:, np.maximum(lag, 0)], 0.0).reshape(RANK * block, block)
    toeplitz = np.concatenate(split_np(toeplitz), 1)
    reverse = basis[:, ::-1]
    moment = np.concatenate(split_np(reverse), 1)
    first = np.zeros((RANK, 128), np.float32)
    first[:, :2] = reverse[:, :2]

    gap = np.arange(devices)[:, None] - 1 - np.arange(devices)[None, :]
    decay = np.where(
        gap[:, None, :] >= 0, np.exp(-nodes[None, :, None] * block * np.maximum(gap, 0)[:, None, :]), 0.0
    )
    carry = (decay[:, :, :, None] * shares[None, :, None, :]).reshape(devices, NODES, devices * RANK)
    carry = np.concatenate(split_np(carry), 1).reshape(devices * 2 * NODES, devices * RANK)

    parts = [np.exp(-np.outer(lags + 1 - by, nodes)) * (lags >= by - 1)[:, None] for by in (0, 1, 2)]
    spread = np.concatenate(parts + [np.zeros((block, PAD - 3 * NODES))], 1)
    high, low = split_np(spread)
    spread = np.concatenate([high, low, high], 1)
    return mix, toeplitz, moment, first, carry, spread


def split(values):
    high = values.astype(BF16)
    return high, (values - high.astype(F32)).astype(BF16)


def dot(left, right):
    return jnp.dot(left, right, preferred_element_type=F32)


def taps_of(values, taps):
    return taps[0:1] * values + taps[1:2] * pltpu.roll(values, 1, 0) + taps[2:3] * pltpu.roll(values, 2, 0)


def rounded(values):
    return values.astype(BF16).astype(F32)


def local_kernel(k_ref, v_ref, taps_ref, rates_ref, residues_ref, mix_ref, toeplitz_ref, moment_ref,
                 product_ref, local_ref, part_ref, weight_ref, cheb_ref):
    mid, half = log_range()
    x = (jnp.log(rates_ref[...] + SHIFT) - mid) * (1.0 / half)
    before = residues_ref[...]
    now = before * x
    cheb_ref[0:1] = jnp.sum(before, 0, keepdims=True)
    cheb_ref[1:2] = jnp.sum(now, 0, keepdims=True)
    twice = 2.0 * x
    for order in range(2, NODES):
        before, now = now, twice * now - before
        cheb_ref[order : order + 1] = jnp.sum(now, 0, keepdims=True)
    mixed = jnp.dot(mix_ref[...], cheb_ref[...], preferred_element_type=F32, precision=lax.Precision.HIGHEST)
    weight_ref[...] = mixed[:NODES]

    key_feat = rounded(taps_of(k_ref[...].astype(F32), taps_ref[1]))
    value_feat = rounded(taps_of(v_ref[...].astype(F32), taps_ref[2]))
    product = key_feat * value_feat
    row = lax.broadcasted_iota(jnp.int32, product.shape, 0)
    product = jnp.where(row < 2, 0.0, product).astype(BF16)
    product_ref[...] = product
    block = product.shape[0]
    twin = jnp.concatenate([product, product], 0)
    part_ref[...] = dot(moment_ref[...], twin)
    for half_idx in range(product.shape[1] // 256):
        cols = slice(half_idx * 256, half_idx * 256 + 256)
        total = None
        for k in range(RANK):
            term = mixed[NODES + k : NODES + k + 1, cols] * dot(
                toeplitz_ref[k * block : (k + 1) * block], twin[:, cols]
            )
            total = term if total is None else total + term
        local_ref[:, cols] = total


def edge_kernel(k_ref, v_ref, edge_ref, taps_ref, part_ref, first_ref, sent_ref, rows_ref):
    edge = edge_ref[...].astype(F32)

    def two_rows(values, tail, taps):
        row0 = taps[0:1] * values[0:1] + taps[1:2] * tail[1:2] + taps[2:3] * tail[0:1]
        row1 = taps[0:1] * values[1:2] + taps[1:2] * values[0:1] + taps[2:3] * tail[1:2]
        return rounded(row0), rounded(row1)

    key0, key1 = two_rows(k_ref[...].astype(F32), edge[2:4], taps_ref[1])
    value0, value1 = two_rows(v_ref[...].astype(F32), edge[4:6], taps_ref[2])
    row0, row1 = rounded(key0 * value0), rounded(key1 * value1)
    rows_ref[...] = jnp.concatenate([row0, row1, jnp.zeros((6, row0.shape[1]), F32)], 0)
    first = first_ref[...]
    whole = part_ref[...] + first[:, 0:1] * row0 + first[:, 1:2] * row1
    copies = 16 // RANK
    pair = jnp.concatenate([whole] * copies, 0).astype(BF16)
    for idx in range(sent_ref.shape[0] // 16):
        sent_ref[idx * 16 : idx * 16 + 16] = pair


def out_kernel(idx_ref, q_ref, edge_ref, taps_ref, skip_ref, product_ref, local_ref, rows_ref, weight_ref,
               got_ref, carry_ref, spread_ref, out_ref):
    state = dot(carry_ref[...], got_ref[...])
    state = state[:NODES] + state[NODES:]
    weight = weight_ref[...]
    row0, row1 = rows_ref[0:1], rows_ref[1:2]
    columns = weight.shape[1]
    stacked = jnp.concatenate(
        [weight * state, weight * row0, weight * row1, jnp.zeros((PAD - 3 * NODES, columns), F32)], 0
    )
    high, low = split(stacked)
    convolved = local_ref[...] + dot(spread_ref[...], jnp.concatenate([high, high, low], 0))

    values = q_ref[...].astype(F32)
    edge = edge_ref[...].astype(F32)
    taps = taps_ref[0]
    row = lax.broadcasted_iota(jnp.int32, values.shape, 0)
    one = jnp.where(row == 0, edge[1:2], pltpu.roll(values, 1, 0))
    two = jnp.where(row == 0, edge[0:1], jnp.where(row == 1, edge[1:2], pltpu.roll(values, 2, 0)))
    query_feat = rounded(taps[0:1] * values + taps[1:2] * one + taps[2:3] * two)
    product = product_ref[...].astype(F32)
    product = jnp.where(row == 0, row0, jnp.where(row == 1, row1, product))
    out_ref[...] = (query_feat * (rounded(convolved) + skip_ref[...] * product)).astype(BF16)


def on_device(query_proj, key_proj, value_proj, short_filter, skip_gain, pole_rates, pole_residues):
    block, channels = query_proj.shape
    devices = lax.axis_size("ctx")
    mix, toeplitz, moment, first, carry, spread = tables(block, devices)
    width = min(512, channels)
    grid = (channels // width,)

    def cols(rows):
        return pl.BlockSpec((rows, width), lambda i, *_: (0, i))

    def fixed(array):
        return pl.BlockSpec(array.shape, lambda i, *_: (0,) * array.ndim)

    taps_spec = pl.BlockSpec((3, 3, width), lambda i, *_: (0, 0, i))
    params = pltpu.CompilerParams(vmem_limit_bytes=48 * 1024 * 1024)

    tails = jnp.concatenate([query_proj[-2:], key_proj[-2:], value_proj[-2:]], 0)
    edge = lax.ppermute(tails, "ctx", [(i, i + 1) for i in range(devices - 1)])

    poles = pole_rates.shape[1]
    product, local, part, weight = pl.pallas_call(
        local_kernel,
        grid=grid,
        in_specs=[cols(block), cols(block), taps_spec, cols(poles), cols(poles), fixed(mix), fixed(toeplitz),
                  fixed(moment)],
        out_specs=[cols(block), cols(block), cols(RANK), cols(NODES)],
        out_shape=[
            jax.ShapeDtypeStruct((block, channels), BF16),
            jax.ShapeDtypeStruct((block, channels), F32),
            jax.ShapeDtypeStruct((RANK, channels), F32),
            jax.ShapeDtypeStruct((NODES, channels), F32),
        ],
        scratch_shapes=[pltpu.VMEM((NODES, width), F32)],
        compiler_params=params,
        cost_estimate=pl.CostEstimate(
            flops=2 * toeplitz.size * channels, bytes_accessed=4 * block * channels * 3, transcendentals=0
        ),
        name="local",
    )(key_proj, value_proj, short_filter, pole_rates.T, pole_residues.T, jnp.asarray(mix),
      jnp.asarray(toeplitz), jnp.asarray(moment))

    sent, rows = pl.pallas_call(
        edge_kernel,
        grid=grid,
        in_specs=[cols(16), cols(16), cols(6), taps_spec, cols(RANK), fixed(first)],
        out_specs=[cols(devices * RANK), cols(8)],
        out_shape=[
            jax.ShapeDtypeStruct((devices * RANK, channels), BF16),
            jax.ShapeDtypeStruct((8, channels), F32),
        ],
        compiler_params=params,
        name="edge",
    )(key_proj, value_proj, edge, short_filter, part, jnp.asarray(first))

    got = lax.all_to_all(sent, "ctx", 0, 0, tiled=True)

    place = lax.axis_index("ctx").astype(jnp.int32).reshape(1)
    return pl.pallas_call(
        out_kernel,
        grid_spec=pltpu.PrefetchScalarGridSpec(
            num_scalar_prefetch=1,
            grid=grid,
            in_specs=[
                cols(block), cols(6), taps_spec, cols(1), cols(block), cols(block), cols(8), cols(NODES),
                cols(devices * RANK),
                pl.BlockSpec((2 * NODES, devices * RANK), lambda i, idx: (idx[0], 0)),
                fixed(spread),
            ],
            out_specs=cols(block),
        ),
        out_shape=jax.ShapeDtypeStruct((block, channels), BF16),
        compiler_params=params,
        name="output",
    )(place, query_proj, edge, short_filter, skip_gain.reshape(1, -1), product, local, rows, weight, got,
      jnp.asarray(carry), jnp.asarray(spread))


def solution(mesh):
    placed = (
        P("ctx", "tp"),
        P("ctx", "tp"),
        P("ctx", "tp"),
        P(None, None, "tp"),
        P("tp"),
        P("tp", None),
        P("tp", None),
    )
    return jax.shard_map(
        on_device, mesh=mesh, in_specs=placed, out_specs=P("ctx", "tp"), check_vma=False
    )
```

time: 165 us -> 51.5 us (0.31)
  the two profiles are of different devices: /device:TPU:0 before, /device:TPU:1 now
where the time goes in v1:
time: 51.5 us; the launch traced here: 50.7 us
  waiting for transfers between devices  16.9 us (33%)
  starting transfers between devices  12.8 us (25%)
  local copies, waits for them, and re-layouts  12.4 us (24%)
  Pallas kernels  8.49 us (16%)
    all_to_all x1, waiting for transfers between devices, on_device(): got = lax.all_to_all(sent, 'ctx', 0, 0, tiled=True)  16.9 us
    unnamed x38, local copies, waits for them, and re-layouts  10 us
    all_to_all x1, starting transfers between devices, on_device(): got = lax.all_to_all(sent, 'ctx', 0, 0, tiled=True)  7.89 us
    ppermute x1, starting transfers between devices, on_device(): edge = lax.ppermute(tails, 'ctx', [(i, i + 1) for i in range(devices - 1)])  4.94 us
    pallas_call x1, Pallas kernels, on_device(): pl.pallas_call(local_kernel, grid=grid, in_specs=[cols(block), cols(block...  3.88 us
    pallas_call x1, Pallas kernels, on_device(): pl.pallas_call(out_kernel, grid_spec=pltpu.PrefetchScalarGridSpec(num_sca...  2.8 us
    pallas_call x1, Pallas kernels, on_device(): pl.pallas_call(edge_kernel, grid=grid, in_specs=[cols(16), cols(16), cols...  1.8 us
  transfers between devices with their start and end apart: 2, of which 1 were waited for; matrix products, arithmetic and copies ran while one was open for 0% of the time, Pallas kernels for 8%

profile of v1, /device:TPU:1, one launch (start us, length us, event | category | flops | bytes accessed | tf_op | source)
XLA Modules:
  0.0 50.7 jit_solution(6006964983665899833)
XLA Ops:
  0.0 0.0 copy-start.18
  0.0 0.0 copy-start.17
  0.0 0.0 copy-start.6
  0.0 0.8 %slice.10 = bf16[2,2048]{1,0:T(2,128)(2,1)S(1)} slice(bf16[128,2048]{1,0:T(8,128)(2,1)} %k_ref.3), slice={[126:128], [0:2048]} | slice | bytes 16384 | tf_op jit(solution)/shard_map/slice | solution.py:184
  0.8 0.8 %slice.11 = bf16[2,2048]{1,0:T(2,128)(2,1)S(1)} slice(bf16[128,2048]{1,0:T(8,128)(2,1)} %v_ref.3), slice={[126:128], [0:2048]} | slice | bytes 16384 | tf_op jit(solution)/shard_map/slice | solution.py:184
  1.6 0.8 %slice.9 = bf16[2,2048]{1,0:T(2,128)(2,1)S(1)} slice(bf16[128,2048]{1,0:T(8,128)(2,1)} %q_ref.1), slice={[126:128], [0:2048]} | slice | bytes 16384 | tf_op jit(solution)/shard_map/slice | solution.py:184
  2.4 4.9 %collective-permute-start = (bf16[6,2048]{1,0:T(8,128)(2,1)S(1)}, bf16[6,2048]{1,0:T(8,128)(2,1)S(1)}, u32[]{:S(2)}, u32[]{:S(2)}) collective-permute-start(bf16[6,2048]{1,0:T(8,128)(2,1)S(1)} %pad_maximum_fusion), channel_id=1, source_target_pairs={{0,4},{4,8},{8,12},{12,16},{16,20},{20,24},{24,28},{28,32},{32,36}... | collective-permute-start | bytes 73736 | tf_op jit(solution)/shard_map/ppermute | solution.py:185
  7.4 0.0 copy-done.18
  7.4 0.0 copy-done.17
  7.4 0.0 copy-done.6
  7.4 0.0 copy-start.2
  7.4 1.0 %copy-done.2 = bf16[128,2048]{1,0:T(8,128)(2,1)S(1)} copy-done((bf16[128,2048]{1,0:T(8,128)(2,1)S(1)}, bf16[128,2048]{1,0:T(8,128)(2,1)}, u32[]{:S(2)}) %copy-start.2) | copy-done | bytes 524312
  8.4 0.0 copy-start.3
  8.4 1.0 %copy-done.3 = bf16[128,2048]{1,0:T(8,128)(2,1)S(1)} copy-done((bf16[128,2048]{1,0:T(8,128)(2,1)S(1)}, bf16[128,2048]{1,0:T(8,128)(2,1)}, u32[]{:S(2)}) %copy-start.3) | copy-done | bytes 524312
  9.5 0.0 copy-start.14
  9.5 0.9 %copy-done.14 = f32[2048,16]{0,1:T(8,128)S(1)} copy-done((f32[2048,16]{0,1:T(8,128)S(1)}, f32[2048,16]{0,1:T(8,128)}, u32[]{:S(2)}) %copy-start.14) | copy-done | bytes 131096
  10.4 0.0 copy-start.15
  10.4 0.9 %copy-done.15 = f32[2048,16]{0,1:T(8,128)S(1)} copy-done((f32[2048,16]{0,1:T(8,128)S(1)}, f32[2048,16]{0,1:T(8,128)}, u32[]{:S(2)}) %copy-start.15) | copy-done | bytes 131096
  11.3 0.0 copy-start.16
  11.3 1.0 %copy-done.16 = bf16[1024,256]{1,0:T(8,128)(2,1)S(1)} copy-done((bf16[1024,256]{1,0:T(8,128)(2,1)S(1)}, bf16[1024,256]{1,0:T(8,128)(2,1)}, u32[]{:S(2)}) %copy-start.16) | copy-done | bytes 524312
  12.3 0.0 copy-start.13
  12.3 3.9 %local.1 = (bf16[128,2048]{1,0:T(8,128)(2,1)S(1)}, f32[128,2048]{1,0:T(8,128)S(1)}, f32[8,2048]{1,0:T(8,128)S(1)}, f32[24,2048]{1,0:T(8,128)S(1)}) custom-call(bf16[128,2048]{1,0:T(8,128)(2,1)S(1)} %copy-done.3, bf16[128,2048]{1,0:T(8,128)(2,1)S(1)} %copy-done.2, f32[3,3,2048]{2,1,0:T(4,128)S(1)} %copy-done.6, f32[16,2048]{1,0:T(8,128)S(1)} %bitcast.8, ...), custom_call_target="tpu_custom_call" | custom-call | flops 1073741824 | bytes 3145728 | tf_op jit(solution)/shard_map/local/pallas_call | solution.py:188
  16.2 0.0 copy-start.4
  16.2 0.8 %copy-done.4 = bf16[128,2048]{1,0:T(8,128)(2,1)} copy-done((bf16[128,2048]{1,0:T(8,128)(2,1)}, bf16[128,2048]{1,0:T(8,128)(2,1)S(1)}, u32[]{:S(2)}) %copy-start.4) | copy-done | bytes 524312
  17.0 0.0 copy-start.7
  17.0 0.0 collective-permute-done.edge_ref
  17.0 0.0 copy-done.13
  17.0 1.8 %edge.1 = (bf16[256,2048]{1,0:T(8,128)(2,1)}, f32[8,2048]{1,0:T(8,128)S(1)}) custom-call(bf16[128,2048]{1,0:T(8,128)(2,1)S(1)} %copy-done.3, bf16[128,2048]{1,0:T(8,128)(2,1)S(1)} %copy-done.2, bf16[6,2048]{1,0:T(8,128)(2,1)S(1)} %collective-permute-done.edge_ref, f32[3,3,2048]{2,1,0:T(4,128)S(1)} %copy-done.6, f32[8,2048]{1,0:T(8,128)S(1)} %get-tuple-element.13.part_ref, ...), custom_call_target="tpu_custom_call" | custom-call | tf_op jit(solution)/shard_map/edge/pallas_call | solution.py:209
  18.8 0.0 copy-done.7
  18.8 0.0 copy-start.10
  18.8 0.6 %copy-done.10 = f32[8,2048]{1,0:T(8,128)} copy-done((f32[8,2048]{1,0:T(8,128)}, f32[8,2048]{1,0:T(8,128)S(1)}, u32[]{:S(2)}) %copy-start.10) | copy-done | bytes 65560
  19.5 0.0 copy-start
  19.5 0.0 copy-start.1
  19.5 7.9 %all-to-all-start = ((bf16[32,8,2048]{2,1,0:T(8,128)(2,1)}), bf16[32,8,2048]{2,1,0:T(8,128)(2,1)S(1)}, u32[]{:S(2)}, u32[]{:S(2)}) async-start(bf16[32,8,2048]{2,1,0:T(8,128)(2,1)} %bitcast.4), calls=%async_computation | async-start | bytes 2097152 | tf_op jit(solution)/shard_map/all_to_all | solution.py:222
  27.4 0.0 copy-start.12
  27.4 16.9 %all-to-all-done = bf16[32,8,2048]{2,1,0:T(8,128)(2,1)S(1)} async-done(((bf16[32,8,2048]{2,1,0:T(8,128)(2,1)}), bf16[32,8,2048]{2,1,0:T(8,128)(2,1)S(1)}, u32[]{:S(2)}, u32[]{:S(2)}) %all-to-all-start) | async-done | bytes 1048608 | tf_op jit(solution)/shard_map/all_to_all | solution.py:222
  44.3 0.0 copy-done
  44.3 0.0 copy-done.1
  44.3 0.0 copy-done.12
  44.3 0.0 copy-start.5
  44.3 1.0 %copy-done.5 = bf16[128,2048]{1,0:T(8,128)(2,1)S(1)} copy-done((bf16[128,2048]{1,0:T(8,128)(2,1)S(1)}, bf16[128,2048]{1,0:T(8,128)(2,1)}, u32[]{:S(2)}) %copy-start.5) | copy-done | bytes 524312
  45.3 0.0 copy-start.8
  45.3 0.9 %copy-done.8 = f32[24,2048]{1,0:T(8,128)S(1)} copy-done((f32[24,2048]{1,0:T(8,128)S(1)}, f32[24,2048]{1,0:T(8,128)}, u32[]{:S(2)}) %copy-start.8) | copy-done | bytes 196632
  46.2 0.0 copy-start.9
  46.2 0.8 %copy-done.9 = bf16[128,240]{1,0:T(8,128)(2,1)S(1)} copy-done((bf16[128,240]{1,0:T(8,128)(2,1)S(1)}, bf16[128,240]{1,0:T(8,128)(2,1)}, u32[]{:S(2)}) %copy-start.9) | copy-done | bytes 61464
  47.1 0.0 copy-start.11
  47.1 0.8 %copy-done.11 = f32[8,2048]{1,0:T(8,128)S(1)} copy-done((f32[8,2048]{1,0:T(8,128)S(1)}, f32[8,2048]{1,0:T(8,128)}, u32[]{:S(2)}) %copy-start.11) | copy-done | bytes 65560
  47.9 2.8 %output.1 = bf16[128,2048]{1,0:T(8,128)(2,1)} custom-call(s32[1]{0:T(128)} %bitcast.idx_ref, bf16[128,2048]{1,0:T(8,128)(2,1)S(1)} %copy-done.1, bf16[6,2048]{1,0:T(8,128)(2,1)S(1)} %collective-permute-done.edge_ref, f32[3,3,2048]{2,1,0:T(4,128)S(1)} %copy-done.6, f32[1,2048]{1,0:T(1,128)S(1)} %bitcast.7, bf16[128,2048]{1,0:T(8,128)(2,1)S(1)} %copy-done.5, ...), custom_call_target="tpu_custom_call" | custom-call | tf_op jit(solution)/shard_map/output/pallas_call | solution.py:225
  (1 shorter events, 0.0 us)
Async XLA Ops:
  0.0 7.4 %copy-start.18 = (bf16[8,256]{1,0:T(8,128)(2,1)S(1)}, bf16[8,256]{1,0:T(8,128)(2,1)}, u32[]{:S(2)}) copy-start(bf16[8,256]{1,0:T(8,128)(2,1)} %constant.20.clone.moment_ref) | copy-start | bytes 12292
  0.0 7.4 %copy-start.17 = (f32[32,24]{1,0:T(8,128)S(1)}, f32[32,24]{1,0:T(8,128)}, u32[]{:S(2)}) copy-start(f32[32,24]{1,0:T(8,128)} %constant.18.clone.mix_ref) | copy-start | bytes 9220
  0.0 7.4 %copy-start.6 = (f32[3,3,2048]{2,1,0:T(4,128)S(1)}, f32[3,3,2048]{2,1,0:T(4,128)}, u32[]{:S(2)}) copy-start(f32[3,3,2048]{2,1,0:T(4,128)} %taps_ref.5) | copy-start | bytes 221188
  2.4 14.6 %collective-permute-start = (bf16[6,2048]{1,0:T(8,128)(2,1)S(1)}, bf16[6,2048]{1,0:T(8,128)(2,1)S(1)}, u32[]{:S(2)}, u32[]{:S(2)}) collective-permute-start(bf16[6,2048]{1,0:T(8,128)(2,1)S(1)} %pad_maximum_fusion), channel_id=1, source_target_pairs={{0,4},{4,8},{8,12},{12,16},{16,20},{20,24},{24,28},{28,32},{32,36}... | collective-permute-start | bytes 73736 | tf_op jit(solution)/shard_map/ppermute | solution.py:185
  7.4 1.0 %copy-start.2 = (bf16[128,2048]{1,0:T(8,128)(2,1)S(1)}, bf16[128,2048]{1,0:T(8,128)(2,1)}, u32[]{:S(2)}) copy-start(bf16[128,2048]{1,0:T(8,128)(2,1)} %v_ref.3) | copy-start | bytes 1572868
  8.4 1.0 %copy-start.3 = (bf16[128,2048]{1,0:T(8,128)(2,1)S(1)}, bf16[128,2048]{1,0:T(8,128)(2,1)}, u32[]{:S(2)}) copy-start(bf16[128,2048]{1,0:T(8,128)(2,1)} %k_ref.3) | copy-start | bytes 1572868
  9.5 0.9 %copy-start.14 = (f32[2048,16]{0,1:T(8,128)S(1)}, f32[2048,16]{0,1:T(8,128)}, u32[]{:S(2)}) copy-start(f32[2048,16]{0,1:T(8,128)} %param.18) | copy-start | bytes 393220
  10.4 0.9 %copy-start.15 = (f32[2048,16]{0,1:T(8,128)S(1)}, f32[2048,16]{0,1:T(8,128)}, u32[]{:S(2)}) copy-start(f32[2048,16]{0,1:T(8,128)} %param.19) | copy-start | bytes 393220
  11.3 1.0 %copy-start.16 = (bf16[1024,256]{1,0:T(8,128)(2,1)S(1)}, bf16[1024,256]{1,0:T(8,128)(2,1)}, u32[]{:S(2)}) copy-start(bf16[1024,256]{1,0:T(8,128)(2,1)} %constant.19.clone.toeplitz_ref) | copy-start | bytes 1572868
  12.3 4.7 %copy-start.13 = (f32[8,128]{1,0:T(8,128)S(1)}, f32[8,128]{1,0:T(8,128)}, u32[]{:S(2)}) copy-start(f32[8,128]{1,0:T(8,128)} %constant.21.clone.first_ref) | copy-start | bytes 12292
  16.2 0.8 %copy-start.4 = (bf16[128,2048]{1,0:T(8,128)(2,1)}, bf16[128,2048]{1,0:T(8,128)(2,1)S(1)}, u32[]{:S(2)}) copy-start(bf16[128,2048]{1,0:T(8,128)(2,1)S(1)} %get-tuple-element.11.product_ref) | copy-start | bytes 1572868
  17.0 1.8 %copy-start.7 = (f32[24,2048]{1,0:T(8,128)}, f32[24,2048]{1,0:T(8,128)S(1)}, u32[]{:S(2)}) copy-start(f32[24,2048]{1,0:T(8,128)S(1)} %get-tuple-element.15.weight_ref) | copy-start | bytes 589828
  18.8 0.6 %copy-start.10 = (f32[8,2048]{1,0:T(8,128)}, f32[8,2048]{1,0:T(8,128)S(1)}, u32[]{:S(2)}) copy-start(f32[8,2048]{1,0:T(8,128)S(1)} %get-tuple-element.14.rows_ref) | copy-start | bytes 196612
  19.5 24.8 %copy-start = (bf16[1536,256]{1,0:T(8,128)(2,1)S(1)}, bf16[1536,256]{1,0:T(8,128)(2,1)}, u32[]{:S(2)}) copy-start(bf16[1536,256]{1,0:T(8,128)(2,1)} %constant.22.clone.carry_ref) | copy-start | bytes 2359300
  19.5 24.8 %copy-start.1 = (bf16[128,2048]{1,0:T(8,128)(2,1)S(1)}, bf16[128,2048]{1,0:T(8,128)(2,1)}, u32[]{:S(2)}) copy-start(bf16[128,2048]{1,0:T(8,128)(2,1)} %q_ref.1) | copy-start | bytes 1572868
  19.5 24.8 %all-to-all-start = ((bf16[32,8,2048]{2,1,0:T(8,128)(2,1)}), bf16[32,8,2048]{2,1,0:T(8,128)(2,1)S(1)}, u32[]{:S(2)}, u32[]{:S(2)}) async-start(bf16[32,8,2048]{2,1,0:T(8,128)(2,1)} %bitcast.4), calls=%async_computation | async-start | bytes 2097152 | tf_op jit(solution)/shard_map/all_to_all | solution.py:222
  27.4 16.9 %copy-start.12 = (f32[2048]{0:T(1024)S(1)}, f32[2048]{0:T(1024)}, u32[]{:S(2)}) copy-start(f32[2048]{0:T(1024)} %param.17) | copy-start | bytes 24580
  44.3 1.0 %copy-start.5 = (bf16[128,2048]{1,0:T(8,128)(2,1)S(1)}, bf16[128,2048]{1,0:T(8,128)(2,1)}, u32[]{:S(2)}) copy-start(bf16[128,2048]{1,0:T(8,128)(2,1)} %copy-done.4) | copy-start | bytes 1572868
  45.3 0.9 %copy-start.8 = (f32[24,2048]{1,0:T(8,128)S(1)}, f32[24,2048]{1,0:T(8,128)}, u32[]{:S(2)}) copy-start(f32[24,2048]{1,0:T(8,128)} %copy-done.7) | copy-start | bytes 589828
  46.2 0.8 %copy-start.9 = (bf16[128,240]{1,0:T(8,128)(2,1)S(1)}, bf16[128,240]{1,0:T(8,128)(2,1)}, u32[]{:S(2)}) copy-start(bf16[128,240]{1,0:T(8,128)(2,1)} %constant.23.clone.spread_ref) | copy-start | bytes 184324
  47.1 0.8 %copy-start.11 = (f32[8,2048]{1,0:T(8,128)S(1)}, f32[8,2048]{1,0:T(8,128)}, u32[]{:S(2)}) copy-start(f32[8,2048]{1,0:T(8,128)} %copy-done.10) | copy-start | bytes 196612

commit v2 on v1

v2 whole, which is shorter than its diff:
```python
import functools

import jax
import jax.numpy as jnp
import ml_dtypes
import numpy as np
from jax import lax
from jax.experimental import pallas as pl
from jax.experimental.pallas import tpu as pltpu
from jax.sharding import PartitionSpec as P

RATE_MIN, RATE_MAX = 0.3 / 4096, 1.0 / 30.0
SHIFT = 1.2e-3
NODES = 24
RANK = 8
PAD = 80
F32 = jnp.float32
BF16 = jnp.bfloat16
MIB = 1024 * 1024


def split_np(values):
    high = values.astype(np.float32).astype(ml_dtypes.bfloat16)
    low = (values - high.astype(np.float64)).astype(np.float32).astype(ml_dtypes.bfloat16)
    return high, low


def log_range():
    low, high = np.log(RATE_MIN + SHIFT), np.log(RATE_MAX + SHIFT)
    return (low + high) / 2, (high - low) / 2


def basis_of(count):
    rates = np.linspace(RATE_MIN, RATE_MAX, 1500)
    basis = np.linalg.svd(np.exp(-np.outer(rates, np.arange(count))), full_matrices=False)[2][:RANK]
    return basis * np.sign(basis[:, :1])


@functools.lru_cache(maxsize=None)
def tables(block, devices):
    mid, half = log_range()
    order = np.arange(NODES)
    node_x = np.cos((2 * order + 1) * np.pi / (2 * NODES))
    nodes = np.exp(mid + half * node_x) - SHIFT
    weights = np.full(NODES, 2.0 / NODES)
    weights[0] = 1.0 / NODES
    to_nodes = np.cos(order[None, :] * np.arccos(node_x)[:, None]) * weights[None, :]

    lags = np.arange(block)
    near, wide = basis_of(block), basis_of(2 * block)
    near_share = np.exp(-np.outer(nodes, lags)) @ near.T
    wide_share = np.exp(-np.outer(nodes, np.arange(2 * block))) @ wide.T
    mix = np.concatenate([to_nodes, near_share.T @ to_nodes], 0).astype(np.float32)

    lag = lags[:, None] - lags[None, :]
    toeplitz = np.where(lag >= 0, near[:, np.maximum(lag, 0)], 0.0).reshape(RANK * block, block)
    toeplitz = np.concatenate(split_np(toeplitz), 1)
    near_back, wide_back = near[:, ::-1], wide[:, ::-1]
    moment = np.concatenate([wide_back[:, :block], near_back, wide_back[:, block:], near_back], 0)
    moment = np.concatenate(split_np(moment), 1)
    first = np.zeros((2 * RANK, 128), np.float32)
    first[:RANK, 0:2] = wide_back[:, :2]
    first[:RANK, 2:4] = wide_back[:, block : block + 2]
    first[RANK:, 0:2] = near_back[:, :2]

    chips = devices // 2
    place = np.arange(devices)
    gap = (place // 2)[:, None] - 1 - np.arange(chips)[None, :]
    lead = (2 * np.maximum(gap, 0) + (place % 2)[:, None]) * block
    decay = np.where(gap[:, None, :] >= 0, np.exp(-nodes[None, :, None] * lead[:, None, :]), 0.0)
    carry = (decay[:, :, :, None] * wide_share[None, :, None, :]).reshape(devices, NODES, chips * RANK)
    carry = np.concatenate(split_np(carry), 1).reshape(devices * 2 * NODES, chips * RANK)

    parts = [np.exp(-np.outer(lags + 1 - by, nodes)) * (lags >= by - 1)[:, None] for by in (0, 1, 2)]
    spread = np.concatenate(parts + [np.zeros((block, PAD - 3 * NODES))], 1)
    high, low = split_np(spread)
    spread = np.concatenate([high, low, high], 1)
    return mix, toeplitz, moment, first, near_share.astype(np.float32), carry, spread


def split(values):
    high = values.astype(BF16)
    return high, (values - high.astype(F32)).astype(BF16)


def dot(left, right):
    return jnp.dot(left, right, preferred_element_type=F32)


def exact_dot(left, right):
    return jnp.dot(left, right, preferred_element_type=F32, precision=lax.Precision.HIGHEST)


def rounded(values):
    return values.astype(BF16).astype(F32)


def zeros(rows, columns):
    return jnp.zeros((rows, columns), F32)


def edge_kernel(q_ref, k_ref, v_ref, tails_ref, edges_ref, held, sems):
    block, columns = q_ref.shape
    copies = []
    for idx, (ref, start) in enumerate(
        ((q_ref, block - 16), (k_ref, block - 16), (v_ref, block - 16), (k_ref, 0), (v_ref, 0))
    ):
        copies.append(pltpu.make_async_copy(ref.at[pl.ds(start, 16)], held.at[idx], sems.at[idx]))
    for copy in copies:
        copy.start()
    for copy in copies:
        copy.wait()
    rows = [held[idx].astype(F32)[14:16] for idx in range(3)]
    rows += [held[idx].astype(F32)[0:2] for idx in (3, 4)]
    tails_ref[...] = jnp.concatenate(rows[:3] + [zeros(2, columns)], 0).astype(BF16)
    edges_ref[...] = jnp.concatenate(rows + [zeros(6, columns)], 0).astype(BF16)


def featurize(values, taps):
    return rounded(
        taps[0:1] * values + taps[1:2] * pltpu.roll(values, 1, 0) + taps[2:3] * pltpu.roll(values, 2, 0)
    )


def moment_kernel(order_ref, k_ref, v_ref, taps_hbm, moment_hbm, parts_ref, held, taps_ref, moment_ref, sems):
    block, columns = k_ref.shape
    width = held.shape[-1]
    steps = columns // width
    copies = []
    for step in range(steps):
        cols = pl.ds(step * width, width)
        copies.append(
            [
                pltpu.make_async_copy(ref.at[:, cols], held.at[idx, step], sems.at[2 * step + idx])
                for idx, ref in enumerate((k_ref, v_ref))
            ]
        )
    copies[0].append(pltpu.make_async_copy(taps_hbm, taps_ref, sems.at[2 * steps]))
    copies[0].append(pltpu.make_async_copy(moment_hbm, moment_ref, sems.at[2 * steps + 1]))
    for group in copies:
        for copy in group:
            copy.start()
    core = lax.rem(lax.axis_index("ctx"), 2)
    row = lax.broadcasted_iota(jnp.int32, (block, width), 0)
    for step in range(steps):
        cols = slice(step * width, (step + 1) * width)
        for copy in copies[step]:
            copy.wait()
        moment = moment_ref[pl.ds(pl.multiple_of(core * 2 * RANK, 2 * RANK), 2 * RANK)]
        key_feat = featurize(held[0, step].astype(F32), taps_ref[1, :, cols])
        value_feat = featurize(held[1, step].astype(F32), taps_ref[2, :, cols])
        product = jnp.where(row < 2, 0.0, key_feat * value_feat).astype(BF16)
        parts_ref[:, cols] = dot(moment, jnp.concatenate([product, product], 0))


def merge_kernel(mine_ref, other_ref, halo_ref, halo_other_ref, parts_ref, parts_other_ref, taps_ref, first_ref,
                 sent_ref, side_ref, held, sem):
    lower = lax.rem(lax.axis_index("ctx"), 2) == 0
    mine, other = mine_ref[...].astype(F32), other_ref[...].astype(F32)
    before = halo_ref[...].astype(F32) + halo_other_ref[...].astype(F32)
    edges0, edges1 = jnp.where(lower, mine, other), jnp.where(lower, other, mine)
    parts, parts_other = parts_ref[...], parts_other_ref[...]
    parts0, parts1 = jnp.where(lower, parts, parts_other), jnp.where(lower, parts_other, parts)

    def two_rows(head, tail, taps):
        row0 = taps[0:1] * head[0:1] + taps[1:2] * tail[1:2] + taps[2:3] * tail[0:1]
        row1 = taps[0:1] * head[1:2] + taps[1:2] * head[0:1] + taps[2:3] * tail[1:2]
        return rounded(row0), rounded(row1)

    def product_rows(edges, tails):
        key = two_rows(edges[6:8], tails[2:4], taps_ref[1])
        value = two_rows(edges[8:10], tails[4:6], taps_ref[2])
        return rounded(key[0] * value[0]), rounded(key[1] * value[1])

    a0, a1 = product_rows(edges0, before)
    b0, b1 = product_rows(edges1, edges0)
    first = first_ref[...]
    wide, close = first[:RANK], first[RANK:]
    near = parts0[RANK:] + close[:, 0:1] * a0 + close[:, 1:2] * a1
    columns = near.shape[1]
    held[...] = jnp.concatenate(
        [
            jnp.where(lower, a0, b0),
            jnp.where(lower, a1, b1),
            jnp.where(lower, before[0:2], edges0[0:2]),
            zeros(4, columns),
            jnp.where(lower, 0.0, near),
        ],
        0,
    )
    copy = pltpu.make_async_copy(held, side_ref, sem)
    copy.start()
    whole = parts0[:RANK] + parts1[:RANK]
    whole += wide[:, 0:1] * a0 + wide[:, 1:2] * a1 + wide[:, 2:3] * b0 + wide[:, 3:4] * b1
    pair = jnp.concatenate([whole, whole], 0).astype(BF16)
    for idx in range(sent_ref.shape[0] // 16):
        sent_ref[idx * 16 : idx * 16 + 16] = pair
    copy.wait()


def local_kernel(q_ref, k_ref, v_ref, side_ref, taps_ref, skip_ref, rates_ref, residues_ref, mix_ref, toeplitz_ref,
                 near_ref, spread_ref, feat_ref, full_ref, local_ref, weight_ref, cheb_ref):
    mid, half = log_range()
    x = (jnp.log(rates_ref[...] + SHIFT) - mid) * (1.0 / half)
    before = residues_ref[...]
    now = before * x
    cheb_ref[0:1] = jnp.sum(before, 0, keepdims=True)
    cheb_ref[1:2] = jnp.sum(now, 0, keepdims=True)
    twice = 2.0 * x
    for order in range(2, NODES):
        before, now = now, twice * now - before
        cheb_ref[order : order + 1] = jnp.sum(now, 0, keepdims=True)
    mixed = exact_dot(mix_ref[...], cheb_ref[...])
    weight = mixed[:NODES]

    side = side_ref[...]
    row0, row1, edge = side[0:1], side[1:2], side[2:4]
    columns = side.shape[1]
    weight_ref[...] = jnp.concatenate([weight, skip_ref[...], zeros(7, columns)], 0)
    stacked = jnp.concatenate(
        [weight * exact_dot(near_ref[...], side[8:]), weight * row0, weight * row1,
         zeros(PAD - 3 * NODES, columns)], 0
    )
    high, low = split(stacked)
    stacked = jnp.concatenate([high, high, low], 0)
    block = q_ref.shape[0]
    row = lax.broadcasted_iota(jnp.int32, (block, columns), 0)
    product = featurize(k_ref[...].astype(F32), taps_ref[1]) * featurize(v_ref[...].astype(F32), taps_ref[2])
    full_ref[...] = jnp.where(row == 0, row0, jnp.where(row == 1, row1, product)).astype(BF16)
    product = jnp.where(row < 2, 0.0, product).astype(BF16)
    twin = jnp.concatenate([product, product], 0)
    for half_idx in range(columns // 256):
        cols = slice(half_idx * 256, half_idx * 256 + 256)
        total = dot(spread_ref[...], stacked[:, cols])
        for k in range(RANK):
            total += mixed[NODES + k : NODES + k + 1, cols] * dot(
                toeplitz_ref[k * block : (k + 1) * block], twin[:, cols]
            )
        local_ref[:, cols] = total

    values = q_ref[...].astype(F32)
    taps = taps_ref[0]
    one = jnp.where(row == 0, edge[1:2], pltpu.roll(values, 1, 0))
    two = jnp.where(row == 0, edge[0:1], jnp.where(row == 1, edge[1:2], pltpu.roll(values, 2, 0)))
    feat_ref[...] = (taps[0:1] * values + taps[1:2] * one + taps[2:3] * two).astype(BF16)


def out_kernel(feat_ref, full_ref, local_ref, weight_ref, got_ref, carry_ref, spread_ref, out_ref, held, sems):
    place = lax.axis_index("ctx")
    carry = carry_ref[pl.ds(pl.multiple_of(place * 2 * NODES, 2 * NODES), 2 * NODES)]
    width = held.shape[-1]
    copies = []
    for step in range(held.shape[0]):
        cols = slice(step * width, (step + 1) * width)
        state = dot(carry, got_ref[:, cols])
        state = weight_ref[:NODES, cols] * (state[:NODES] + state[NODES:])
        high, low = split(jnp.concatenate([state, zeros(PAD - NODES, width)], 0))
        convolved = local_ref[:, cols] + dot(spread_ref[...], jnp.concatenate([high, high, low], 0))
        skip = weight_ref[NODES : NODES + 1, cols]
        held[step] = (
            feat_ref[:, cols].astype(F32) * (rounded(convolved) + skip * full_ref[:, cols].astype(F32))
        ).astype(BF16)
        copies.append(pltpu.make_async_copy(held.at[step], out_ref.at[:, pl.ds(step * width, width)], sems.at[step]))
        copies[-1].start()
    for copy in copies:
        copy.wait()


def on_device(query_proj, key_proj, value_proj, short_filter, skip_gain, pole_rates, pole_residues):
    block, channels = query_proj.shape
    devices = lax.axis_size("ctx")
    poles = pole_rates.shape[1]
    mix, toeplitz, moment, first, near, carry, spread = (jnp.asarray(table) for table in tables(block, devices))
    width = 512
    grid = (channels // width,)

    def cols(rows):
        return pl.BlockSpec((rows, width), lambda i: (0, i))

    def fixed(array):
        return pl.BlockSpec(array.shape, lambda i: (0,) * array.ndim)

    taps_spec = pl.BlockSpec((3, 3, width), lambda i: (0, 0, i))
    hbm = pl.BlockSpec(memory_space=pltpu.HBM)
    vmem = pl.BlockSpec(memory_space=pltpu.VMEM)
    params = pltpu.CompilerParams(vmem_limit_bytes=32 * MIB)
    keep = functools.partial(pltpu.with_memory_space_constraint, memory_space=pltpu.HBM)
    query_proj, key_proj, value_proj = keep(query_proj), keep(key_proj), keep(value_proj)
    swap = [(i, i ^ 1) for i in range(devices)]

    tails, edges = pl.pallas_call(
        edge_kernel,
        in_specs=[hbm, hbm, hbm],
        out_specs=[vmem, vmem],
        out_shape=[pltpu.VMEM((8, channels), BF16), pltpu.VMEM((16, channels), BF16)],
        scratch_shapes=[pltpu.VMEM((5, 16, channels), BF16), pltpu.SemaphoreType.DMA((5,))],
        compiler_params=params,
        name="edges",
    )(query_proj, key_proj, value_proj)
    halo = lax.ppermute(tails, "ctx", [(i, i + 1) for i in range(1, devices - 1, 2)])
    edges_other = lax.ppermute(edges, "ctx", swap)

    parts = pl.pallas_call(
        moment_kernel,
        in_specs=[pl.BlockSpec(memory_space=pl.ANY), hbm, hbm, hbm, hbm],
        out_specs=vmem,
        out_shape=pltpu.VMEM((2 * RANK, channels), F32),
        scratch_shapes=[
            pltpu.VMEM((2, channels // width, block, width), BF16),
            pltpu.VMEM(short_filter.shape, F32),
            pltpu.VMEM(moment.shape, BF16),
            pltpu.SemaphoreType.DMA((2 * (channels // width) + 2,)),
        ],
        compiler_params=params,
        cost_estimate=pl.CostEstimate(
            flops=1, bytes_accessed=1, transcendentals=0
        ),
        name="moments",
    )(edges, key_proj, value_proj, keep(short_filter), keep(moment))
    parts, halo = lax.optimization_barrier((parts, halo))
    parts_other = lax.ppermute(parts, "ctx", swap)
    halo_other = lax.ppermute(halo, "ctx", swap)

    sent, side = pl.pallas_call(
        merge_kernel,
        in_specs=[vmem] * 8,
        out_specs=[vmem, hbm],
        out_shape=[
            pltpu.VMEM((devices // 2 * RANK, channels), BF16),
            pltpu.HBM((2 * RANK, channels), F32),
        ],
        scratch_shapes=[pltpu.VMEM((2 * RANK, channels), F32), pltpu.SemaphoreType.DMA],
        compiler_params=params,
        name="merge",
    )(edges, edges_other, halo, halo_other, parts, parts_other, short_filter, first)

    groups = [list(range(core, devices, 2)) for core in range(2)]
    got = lax.all_to_all(sent, "ctx", 0, 0, axis_index_groups=groups, tiled=True)

    local_args = (query_proj, key_proj, value_proj, side, short_filter, skip_gain.reshape(1, -1), pole_rates.T,
                  pole_residues.T, mix, toeplitz, near, spread)
    feat, full, local, weight = pl.pallas_call(
        local_kernel,
        grid=grid,
        in_specs=[cols(block), cols(block), cols(block), cols(2 * RANK), taps_spec, cols(1), cols(poles), cols(poles),
                  fixed(mix), fixed(toeplitz), fixed(near), fixed(spread)],
        out_specs=[cols(block), cols(block), cols(block), cols(NODES + 8)],
        out_shape=[
            pltpu.VMEM((block, channels), BF16),
            pltpu.VMEM((block, channels), BF16),
            pltpu.VMEM((block, channels), F32),
            pltpu.VMEM((NODES + 8, channels), F32),
        ],
        scratch_shapes=[pltpu.VMEM((NODES, width), F32)],
        compiler_params=params,
        cost_estimate=pl.CostEstimate(
            flops=8 * toeplitz.size * channels, bytes_accessed=16 * block * channels, transcendentals=0
        ),
        name="local",
    )(*(keep(arg) for arg in local_args))

    return pl.pallas_call(
        out_kernel,
        in_specs=[vmem] * 7,
        out_specs=hbm,
        out_shape=pltpu.HBM((block, channels), BF16),
        scratch_shapes=[
            pltpu.VMEM((channels // width, block, width), BF16),
            pltpu.SemaphoreType.DMA((channels // width,)),
        ],
        compiler_params=params,
        name="output",
    )(feat, full, local, weight, got, carry, spread)


def solution(mesh):
    placed = (
        P("ctx", "tp"),
        P("ctx", "tp"),
        P("ctx", "tp"),
        P(None, None, "tp"),
        P("tp"),
        P("tp", None),
        P("tp", None),
    )
    return jax.shard_map(
        on_device, mesh=mesh, in_specs=placed, out_specs=P("ctx", "tp"), check_vma=False
    )
```

time: 51.5 us -> 32.6 us (0.63)
  the two profiles are of different devices: /device:TPU:1 before, /device:TPU:0 now
where the time goes in v2:
time: 32.6 us; the launch traced here: 32.3 us
  Pallas kernels  13 us (40%)
  starting transfers between devices  12.2 us (37%)
  waiting for transfers between devices  6.92 us (21%)
    all_to_all x1, starting transfers between devices, on_device(): lax.all_to_all(sent, 'ctx', 0, 0, axis_index_groups=groups, tiled=True)  7.61 us
    all_to_all x1, waiting for transfers between devices, on_device(): lax.all_to_all(sent, 'ctx', 0, 0, axis_index_groups=groups, tiled=True)  6.05 us
    pallas_call x1, Pallas kernels, on_device(): pl.pallas_call(local_kernel, grid=grid, in_specs=[cols(block), cols(block...  5.92 us
    ppermute x1, starting transfers between devices, on_device(): parts_other = lax.ppermute(parts, 'ctx', swap)  3.44 us
    pallas_call x1, Pallas kernels, on_device(): pl.pallas_call(moment_kernel, in_specs=[pl.BlockSpec(memory_space=pl.ANY)...  2.66 us
    pallas_call x1, Pallas kernels, on_device(): pl.pallas_call(merge_kernel, in_specs=[vmem] * 8, out_specs=[vmem, hbm],...  1.71 us
    pallas_call x1, Pallas kernels, on_device(): pl.pallas_call(out_kernel, in_specs=[vmem] * 7, out_specs=hbm, out_shape=...  1.69 us
    pallas_call x1, Pallas kernels, on_device(): pl.pallas_call(edge_kernel, in_specs=[hbm, hbm, hbm], out_specs=[vmem, vm...  1.04 us
  transfers between devices with their start and end apart: 5, of which 3 were waited for; matrix products, arithmetic and copies ran while one was open for 0% of the time, Pallas kernels for 27%

profile of v2, /device:TPU:0, one launch (start us, length us, event | category | flops | bytes accessed | tf_op | source)
XLA Modules:
  0.0 32.3 jit_solution(13921185750394034643)
XLA Ops:
  0.0 1.0 %edges.1 = (bf16[8,2048]{1,0:T(8,128)(2,1)S(1)}, bf16[16,2048]{1,0:T(8,128)(2,1)S(1)}) custom-call(bf16[128,2048]{1,0:T(8,128)(2,1)} %q_ref.3, bf16[128,2048]{1,0:T(8,128)(2,1)} %k_ref.5, bf16[128,2048]{1,0:T(8,128)(2,1)} %v_ref.5), custom_call_target="tpu_custom_call" | custom-call | tf_op jit(solution)/shard_map/edges/pallas_call | solution.py:291
  1.1 0.7 %collective-permute-start.1 = (bf16[8,2048]{1,0:T(8,128)(2,1)S(1)}, bf16[8,2048]{1,0:T(8,128)(2,1)S(1)}, u32[]{:S(2)}, u32[]{:S(2)}) collective-permute-start(bf16[8,2048]{1,0:T(8,128)(2,1)S(1)} %get-tuple-element.16), channel_id=1, source_target_pairs={{4,8},{12,16},{20,24},{28,32},{36,40},{44,48},{52,56},{60,64},{68,... | collective-permute-start | bytes 98312 | tf_op jit(solution)/shard_map/ppermute | solution.py:300
  1.7 0.0 copy-start.1
  1.7 0.0 copy-start.3
  1.7 2.7 %moments.1.parts_ref = f32[16,2048]{1,0:T(8,128)S(1)} custom-call(bf16[16,2048]{1,0:T(8,128)(2,1)S(1)} %get-tuple-element.15.order_ref.mine_ref, bf16[128,2048]{1,0:T(8,128)(2,1)} %k_ref.5, bf16[128,2048]{1,0:T(8,128)(2,1)} %v_ref.5, f32[3,3,2048]{2,1,0:T(4,128)} %taps_ref.3, bf16[32,256]{1,0:T(8,128)(2,1)} %constant.16.clone.moment_hbm), custom_call_target="tpu_custom_call" | custom-call | flops 1 | bytes 1 | tf_op jit(solution)/shard_map/moments/pallas_call | solution.py:303
  4.4 0.0 collective-permute-done.1.halo_ref
  4.4 3.4 %collective-permute-start.3 = (f32[16,2048]{1,0:T(8,128)S(1)}, f32[16,2048]{1,0:T(8,128)S(1)}, u32[]{:S(2)}, u32[]{:S(2)}) collective-permute-start(f32[16,2048]{1,0:T(8,128)S(1)} %moments.1.parts_ref), channel_id=1, source_target_pairs={{0,4},{4,0},{8,12},{12,8},{16,20},{20,16},{24,28},{28,24},{32,36},... | collective-permute-start | bytes 393224 | tf_op jit(solution)/shard_map/ppermute | solution.py:321
  7.9 0.1 collective-permute-start
  8.0 0.4 %collective-permute-start.2 = (bf16[8,2048]{1,0:T(8,128)(2,1)S(1)}, bf16[8,2048]{1,0:T(8,128)(2,1)S(1)}, u32[]{:S(2)}, u32[]{:S(2)}) collective-permute-start(bf16[8,2048]{1,0:T(8,128)(2,1)S(1)} %collective-permute-done.1.halo_ref), channel_id=1, source_target_pairs={{0,4},{4,0},{8,12},{12,8},{16,20},{20,16},{24,28},{28,24},{32,36},... | collective-permute-start | bytes 98312 | tf_op jit(solution)/shard_map/ppermute | solution.py:322
  8.4 0.7 %collective-permute-done.other_ref = bf16[16,2048]{1,0:T(8,128)(2,1)S(1)} collective-permute-done((bf16[16,2048]{1,0:T(8,128)(2,1)S(1)}, bf16[16,2048]{1,0:T(8,128)(2,1)S(1)}, u32[]{:S(2)}, u32[]{:S(2)}) %collective-permute-start) | collective-permute-done | bytes 65568 | tf_op jit(solution)/shard_map/ppermute | solution.py:301
  9.1 0.1 collective-permute-done.2.halo_other_ref
  9.2 0.0 collective-permute-done.3.parts_other_ref
  9.2 0.0 copy-done.1
  9.2 0.0 copy-done.3
  9.2 1.7 %merge.1 = (bf16[128,2048]{1,0:T(8,128)(2,1)}, f32[16,2048]{1,0:T(8,128)}) custom-call(bf16[16,2048]{1,0:T(8,128)(2,1)S(1)} %get-tuple-element.15.order_ref.mine_ref, bf16[16,2048]{1,0:T(8,128)(2,1)S(1)} %collective-permute-done.other_ref, bf16[8,2048]{1,0:T(8,128)(2,1)S(1)} %collective-permute-done.1.halo_ref, ...), custom_call_target="tpu_custom_call" | custom-call | tf_op jit(solution)/shard_map/merge/pallas_call | solution.py:324
  11.0 7.6 %all-to-all-start = ((bf16[16,8,2048]{2,1,0:T(8,128)(2,1)}), bf16[16,8,2048]{2,1,0:T(8,128)(2,1)S(1)}, u32[]{:S(2)}, u32[]{:S(2)}) async-start(bf16[16,8,2048]{2,1,0:T(8,128)(2,1)} %bitcast.3), calls=%async_computation | async-start | bytes 1048576 | tf_op jit(solution)/shard_map/all_to_all | solution.py:338
  18.6 0.0 copy-start
  18.6 0.0 copy-start.2
  18.6 5.9 %local.1 = (bf16[128,2048]{1,0:T(8,128)(2,1)S(1)}, bf16[128,2048]{1,0:T(8,128)(2,1)S(1)}, f32[128,2048]{1,0:T(8,128)S(1)}, f32[32,2048]{1,0:T(8,128)S(1)}) custom-call(bf16[128,2048]{1,0:T(8,128)(2,1)} %q_ref.3, bf16[128,2048]{1,0:T(8,128)(2,1)} %k_ref.5, bf16[128,2048]{1,0:T(8,128)(2,1)} %v_ref.5, f32[16,2048]{1,0:T(8,128)} %get-tuple-element.19.side_ref, ...), custom_call_target="tpu_custom_call" | custom-call | flops 4294967296 | bytes 4194304 | tf_op jit(solution)/shard_map/local/pallas_call | solution.py:342
  24.5 6.1 %all-to-all-done = bf16[16,8,2048]{2,1,0:T(8,128)(2,1)S(1)} async-done(((bf16[16,8,2048]{2,1,0:T(8,128)(2,1)}), bf16[16,8,2048]{2,1,0:T(8,128)(2,1)S(1)}, u32[]{:S(2)}, u32[]{:S(2)}) %all-to-all-start) | async-done | bytes 524320 | tf_op jit(solution)/shard_map/all_to_all | solution.py:338
  30.6 0.0 copy-done
  30.6 0.0 copy-done.2
  30.6 1.7 %output.1 = bf16[128,2048]{1,0:T(8,128)(2,1)} custom-call(bf16[128,2048]{1,0:T(8,128)(2,1)S(1)} %get-tuple-element.20.feat_ref, bf16[128,2048]{1,0:T(8,128)(2,1)S(1)} %get-tuple-element.21.full_ref, f32[128,2048]{1,0:T(8,128)S(1)} %get-tuple-element.22.local_ref, f32[32,2048]{1,0:T(8,128)S(1)} %get-tuple-element.23.weight_ref, ...), custom_call_target="tpu_custom_call" | custom-call | tf_op jit(solution)/shard_map/output/pallas_call | solution.py:362
Async XLA Ops:
  1.1 3.4 %collective-permute-start.1 = (bf16[8,2048]{1,0:T(8,128)(2,1)S(1)}, bf16[8,2048]{1,0:T(8,128)(2,1)S(1)}, u32[]{:S(2)}, u32[]{:S(2)}) collective-permute-start(bf16[8,2048]{1,0:T(8,128)(2,1)S(1)} %get-tuple-element.16), channel_id=1, source_target_pairs={{4,8},{12,16},{20,24},{28,32},{36,40},{44,48},{52,56},{60,64},{68,... | collective-permute-start | bytes 98312 | tf_op jit(solution)/shard_map/ppermute | solution.py:300
  1.7 7.5 %copy-start.1 = (f32[3,3,2048]{2,1,0:T(4,128)S(1)}, f32[3,3,2048]{2,1,0:T(4,128)}, u32[]{:S(2)}) copy-start(f32[3,3,2048]{2,1,0:T(4,128)} %taps_ref.3) | copy-start | bytes 221188
  1.7 7.5 %copy-start.3 = (f32[16,128]{1,0:T(8,128)S(1)}, f32[16,128]{1,0:T(8,128)}, u32[]{:S(2)}) copy-start(f32[16,128]{1,0:T(8,128)} %constant.17.clone.first_ref) | copy-start | bytes 24580
  4.4 4.8 %collective-permute-start.3 = (f32[16,2048]{1,0:T(8,128)S(1)}, f32[16,2048]{1,0:T(8,128)S(1)}, u32[]{:S(2)}, u32[]{:S(2)}) collective-permute-start(f32[16,2048]{1,0:T(8,128)S(1)} %moments.1.parts_ref), channel_id=1, source_target_pairs={{0,4},{4,0},{8,12},{12,8},{16,20},{20,16},{24,28},{28,24},{32,36},... | collective-permute-start | bytes 393224 | tf_op jit(solution)/shard_map/ppermute | solution.py:321
  7.9 1.3 %collective-permute-start = (bf16[16,2048]{1,0:T(8,128)(2,1)S(1)}, bf16[16,2048]{1,0:T(8,128)(2,1)S(1)}, u32[]{:S(2)}, u32[]{:S(2)}) collective-permute-start(bf16[16,2048]{1,0:T(8,128)(2,1)S(1)} %get-tuple-element.15.order_ref.mine_ref), channel_id=1, source_target_pairs={{0,4},{4,0},{8,12},{12,8},{16,20},{20,16},{24,28},{28,24},{32,36},... | collective-permute-start | bytes 196616 | tf_op jit(solution)/shard_map/ppermute | solution.py:301
  8.0 1.3 %collective-permute-start.2 = (bf16[8,2048]{1,0:T(8,128)(2,1)S(1)}, bf16[8,2048]{1,0:T(8,128)(2,1)S(1)}, u32[]{:S(2)}, u32[]{:S(2)}) collective-permute-start(bf16[8,2048]{1,0:T(8,128)(2,1)S(1)} %collective-permute-done.1.halo_ref), channel_id=1, source_target_pairs={{0,4},{4,0},{8,12},{12,8},{16,20},{20,16},{24,28},{28,24},{32,36},... | collective-permute-start | bytes 98312 | tf_op jit(solution)/shard_map/ppermute | solution.py:322
  11.0 19.6 %all-to-all-start = ((bf16[16,8,2048]{2,1,0:T(8,128)(2,1)}), bf16[16,8,2048]{2,1,0:T(8,128)(2,1)S(1)}, u32[]{:S(2)}, u32[]{:S(2)}) async-start(bf16[16,8,2048]{2,1,0:T(8,128)(2,1)} %bitcast.3), calls=%async_computation | async-start | bytes 1048576 | tf_op jit(solution)/shard_map/all_to_all | solution.py:338
  18.6 12.0 %copy-start = (bf16[1536,128]{1,0:T(8,128)(2,1)S(1)}, bf16[1536,128]{1,0:T(8,128)(2,1)}, u32[]{:S(2)}) copy-start(bf16[1536,128]{1,0:T(8,128)(2,1)} %constant.19.clone.carry_ref) | copy-start | bytes 1179652
  18.6 12.0 %copy-start.2 = (bf16[128,240]{1,0:T(8,128)(2,1)S(1)}, bf16[128,240]{1,0:T(8,128)(2,1)}, u32[]{:S(2)}) copy-start(bf16[128,240]{1,0:T(8,128)(2,1)} %constant.20.clone.spread_ref) | copy-start | bytes 184324

commit v3 on v2

v3 whole, which is shorter than its diff:
```python
import functools

import jax
import jax.numpy as jnp
import ml_dtypes
import numpy as np
from jax import lax
from jax.experimental import pallas as pl
from jax.experimental.pallas import tpu as pltpu
from jax.sharding import PartitionSpec as P

RATE_MIN, RATE_MAX = 0.3 / 4096, 1.0 / 30.0
SHIFT = 1.2e-3
NODES = 24
RANK = 8
PAD = 80
F32 = jnp.float32
BF16 = jnp.bfloat16
MIB = 1024 * 1024


def split_np(values):
    high = values.astype(np.float32).astype(ml_dtypes.bfloat16)
    low = (values - high.astype(np.float64)).astype(np.float32).astype(ml_dtypes.bfloat16)
    return high, low


def log_range():
    low, high = np.log(RATE_MIN + SHIFT), np.log(RATE_MAX + SHIFT)
    return (low + high) / 2, (high - low) / 2


def basis_of(count):
    rates = np.linspace(RATE_MIN, RATE_MAX, 1500)
    basis = np.linalg.svd(np.exp(-np.outer(rates, np.arange(count))), full_matrices=False)[2][:RANK]
    return basis * np.sign(basis[:, :1])


def chip_order(chips):
    return list(range(chips))[::-1]


@functools.lru_cache(maxsize=None)
def tables(block, devices):
    mid, half = log_range()
    order = np.arange(NODES)
    node_x = np.cos((2 * order + 1) * np.pi / (2 * NODES))
    nodes = np.exp(mid + half * node_x) - SHIFT
    weights = np.full(NODES, 2.0 / NODES)
    weights[0] = 1.0 / NODES
    to_nodes = np.cos(order[None, :] * np.arccos(node_x)[:, None]) * weights[None, :]

    lags = np.arange(block)
    near, wide = basis_of(block), basis_of(2 * block + 2)
    near_share = np.exp(-np.outer(nodes, lags)) @ near.T
    wide_share = np.exp(-np.outer(nodes, np.arange(2 * block + 2))) @ wide.T
    mix = np.concatenate([to_nodes, near_share.T @ to_nodes], 0).astype(np.float32)

    lag = lags[:, None] - lags[None, :]
    toeplitz = np.where(lag >= 0, near[:, np.maximum(lag, 0)], 0.0).reshape(RANK * block, block)
    toeplitz = np.concatenate(split_np(toeplitz), 1)
    near_back = near[:, ::-1]
    moment = np.concatenate(split_np(near_back), 1)
    first = np.zeros((2 * RANK, 128), np.float32)
    first[:RANK, 0:2] = near_back[:, :2]
    first[:RANK, 2:4] = near_back[:, -2:]
    first[RANK:, 0:2] = wide[:, 1::-1]
    widen = np.concatenate([wide[:, block + 2 :] @ near.T, wide[:, 2 : block + 2] @ near.T], 1)
    high, low = split_np(widen)
    widen = np.concatenate([high, low, high, np.zeros_like(high)], 1)

    chips = devices // 2
    place = np.arange(devices)
    gap = (place // 2)[:, None] - 1 - np.array(chip_order(chips))[None, :]
    lead = 2 * block * np.maximum(gap, 0) + (place % 2)[:, None] * (block - 2)
    decay = np.where(gap[:, None, :] >= 0, np.exp(-nodes[None, :, None] * lead[:, None, :]), 0.0)
    carry = (decay[:, :, :, None] * wide_share[None, :, None, :]).reshape(devices, NODES, chips * RANK)
    carry = np.concatenate(split_np(carry), 1).reshape(devices * 2 * NODES, chips * RANK)

    upper = [np.exp(-np.outer(lags + 1 - by, nodes)) * (lags >= by - 1)[:, None] for by in (0, 1, 2)]
    lower = [np.exp(-np.outer(lags - 1, nodes)), np.zeros((block, NODES)), -np.exp(nodes)[None, :] * (lags == 0)[:, None]]
    spread = []
    for parts in (lower, upper):
        high, low = split_np(np.concatenate(parts + [np.zeros((block, PAD - 3 * NODES))], 1))
        spread.append(np.concatenate([high, low, high], 1))
    spread = np.concatenate(spread, 0)
    high, low = split_np(near_share)
    near_share = np.concatenate([high, low, high, np.zeros_like(high)], 1)
    return mix, toeplitz, moment, first, widen, near_share, carry, spread


def split(values):
    high = values.astype(BF16)
    return high, (values - high.astype(F32)).astype(BF16)


def dot(left, right):
    return jnp.dot(left, right, preferred_element_type=F32)


def exact_dot(left, right):
    return jnp.dot(left, right, preferred_element_type=F32, precision=lax.Precision.HIGHEST)


def rounded(values):
    return values.astype(BF16).astype(F32)


def zeros(rows, columns):
    return jnp.zeros((rows, columns), F32)


def edge_kernel(q_ref, k_ref, v_ref, edges_ref, outer_ref, held, sems):
    block, columns = q_ref.shape
    copies = []
    for idx, (ref, start) in enumerate(
        ((q_ref, block - 16), (k_ref, block - 16), (v_ref, block - 16), (k_ref, 0), (v_ref, 0))
    ):
        copies.append(pltpu.make_async_copy(ref.at[pl.ds(start, 16)], held.at[idx], sems.at[idx]))
    for copy in copies:
        copy.start()
    for copy in copies:
        copy.wait()
    tails = [held[idx].astype(F32)[14:16] for idx in range(3)]
    heads = [held[idx].astype(F32)[0:2] for idx in (3, 4)]
    edges_ref[...] = jnp.concatenate(tails + heads + [zeros(6, columns)], 0).astype(BF16)
    lower = lax.rem(lax.axis_index("ctx"), 2) == 0
    outer = jnp.where(
        lower, jnp.concatenate(heads + [zeros(4, columns)], 0), jnp.concatenate(tails + [zeros(2, columns)], 0)
    )
    outer_ref[...] = outer.astype(BF16)


def featurize(values, taps):
    row = lax.broadcasted_iota(jnp.int32, values.shape, 0)
    one = jnp.where(row < 1, 0.0, pltpu.roll(values, 1, 0))
    two = jnp.where(row < 2, 0.0, pltpu.roll(values, 2, 0))
    return rounded(taps[0:1] * values + taps[1:2] * one + taps[2:3] * two)


def moment_kernel(edges_ref, k_ref, v_ref, taps_hbm, moment_hbm, near_ref, inner_ref, held, taps_ref, moment_ref,
                  sems):
    block, columns = k_ref.shape
    width = held.shape[-1]
    steps = columns // width
    copies = []
    for step in range(steps):
        cols = pl.ds(step * width, width)
        copies.append(
            [
                pltpu.make_async_copy(ref.at[:, cols], held.at[idx, step], sems.at[2 * step + idx])
                for idx, ref in enumerate((k_ref, v_ref))
            ]
        )
    copies[0].append(pltpu.make_async_copy(taps_hbm, taps_ref, sems.at[2 * steps]))
    copies[0].append(pltpu.make_async_copy(moment_hbm, moment_ref, sems.at[2 * steps + 1]))
    for group in copies:
        for copy in group:
            copy.start()
    row = lax.broadcasted_iota(jnp.int32, (block, width), 0)
    place = lax.axis_index("ctx")
    lower = lax.rem(place, 2) == 0
    first_row = jnp.where(place == 0, 0, 2)
    for step in range(steps):
        cols = slice(step * width, (step + 1) * width)
        for copy in copies[step]:
            copy.wait()
        key_feat = featurize(held[0, step].astype(F32), taps_ref[1, :, cols])
        value_feat = featurize(held[1, step].astype(F32), taps_ref[2, :, cols])
        product = jnp.where(row < first_row, 0.0, key_feat * value_feat).astype(BF16)
        near = dot(moment_ref[...], jnp.concatenate([product, product], 0))
        near_ref[:, cols] = near
        edges = edges_ref[:, cols].astype(F32)
        for_upper = jnp.concatenate([edges[0:6], zeros(2, width)], 0)
        for_lower = jnp.concatenate([edges[6:10], edges[2:6]], 0)
        inner_ref[:, cols] = jnp.concatenate([near, jnp.where(lower, for_upper, for_lower)], 0).astype(BF16)


def two_rows(head, tail, taps):
    row0 = taps[0:1] * head[0:1] + taps[1:2] * tail[1:2] + taps[2:3] * tail[0:1]
    row1 = taps[0:1] * head[1:2] + taps[1:2] * head[0:1] + taps[2:3] * tail[1:2]
    return rounded(row0), rounded(row1)


def product_rows(heads, tails, taps_ref):
    key = two_rows(heads[0:2], tails[0:2], taps_ref[1])
    value = two_rows(heads[2:4], tails[2:4], taps_ref[2])
    return rounded(key[0] * value[0]), rounded(key[1] * value[1])


def merge_kernel(edges_ref, inner_ref, outer_ref, outer_more_ref, near_ref, taps_ref, first_ref, widen_ref, sent_ref,
                 side_ref, held, sems):
    place = lax.axis_index("ctx")
    lower = lax.rem(place, 2) == 0
    edges, inner = edges_ref[...].astype(F32), inner_ref[...].astype(F32)
    outer, outer_more = outer_ref[...].astype(F32), outer_more_ref[...].astype(F32)
    a0, a1 = product_rows(edges[6:10], outer[2:6], taps_ref)
    b0, b1 = product_rows(
        jnp.where(lower, inner[8:12], edges[6:10]), jnp.where(lower, edges[2:6], inner[10:14]), taps_ref
    )
    c0, c1 = product_rows(
        jnp.where(lower, outer_more[0:4], outer[0:4]), jnp.where(lower, inner[12:16], edges[2:6]), taps_ref
    )
    near, near_other = near_ref[...], inner[:RANK]
    first, last = first_ref[:RANK], first_ref[RANK:]
    near0 = jnp.where(lower, near, near_other)
    near1 = jnp.where(lower, near_other, near) + first[:, 0:1] * b0 + first[:, 1:2] * b1
    high, low = split(jnp.concatenate([near0, near1], 0))
    whole = dot(widen_ref[...], jnp.concatenate([high, high, low, jnp.zeros_like(low)], 0))
    whole += last[:, 0:1] * c0 + last[:, 1:2] * c1
    held[...] = jnp.concatenate([whole, whole], 0).astype(BF16)
    copies = [
        pltpu.make_async_copy(held, sent_ref.at[pl.ds(idx * 16, 16)], sems.at[idx])
        for idx in range(sent_ref.shape[0] // 16)
    ]
    for copy in copies:
        copy.start()
    start = jnp.where(place == 0, first[:, 2:3] * a0 + first[:, 3:4] * a1, 0.0)
    side_ref[...] = jnp.concatenate(
        [
            jnp.where(lower, a0, b0),
            jnp.where(lower, a1, b1),
            jnp.where(lower, outer[0:2], inner[8:10]),
            zeros(4, a0.shape[1]),
            jnp.where(lower, start, near0),
        ],
        0,
    )
    for copy in copies:
        copy.wait()


def local_kernel(side_ref, q_hbm, k_hbm, v_hbm, taps_hbm, skip_hbm, rates_hbm, residues_hbm, mix_hbm, toeplitz_hbm,
                 near_hbm, spread_hbm, feat_ref, full_ref, local_ref, weight_ref, q_ref, k_ref, v_ref, taps_ref,
                 skip_ref, rates_ref, residues_ref, mix_ref, toeplitz_ref, near_ref, spread_ref, cheb_ref, sems):
    block, channels = q_ref.shape
    width = cheb_ref.shape[1]
    steps = channels // width
    count = 0

    def load(source, target):
        nonlocal count
        copy = pltpu.make_async_copy(source, target, sems.at[count])
        copy.start()
        count += 1
        return copy

    filters = [load(rates_hbm, rates_ref), load(residues_hbm, residues_ref), load(mix_hbm, mix_ref),
               load(skip_hbm, skip_ref)]
    rows = [load(taps_hbm, taps_ref), load(near_hbm, near_ref)]
    signals = []
    for step in range(steps):
        at = (slice(None), pl.ds(step * width, width))
        signals.append([load(k_hbm.at[at], k_ref.at[at]), load(v_hbm.at[at], v_ref.at[at])])
        if step == 0:
            matrices = [load(spread_hbm, spread_ref), load(toeplitz_hbm, toeplitz_ref)]
    queries = []
    for step in range(steps):
        at = (slice(None), pl.ds(step * width, width))
        queries.append(load(q_hbm.at[at], q_ref.at[at]))

    mid, half = log_range()
    core = lax.rem(lax.axis_index("ctx"), 2)
    row = lax.broadcasted_iota(jnp.int32, (block, width), 0)
    for copy in filters:
        copy.wait()
    for step in range(steps):
        cols = slice(step * width, (step + 1) * width)
        x = (jnp.log(rates_ref[:, cols] + SHIFT) - mid) * (1.0 / half)
        before = residues_ref[:, cols]
        now = before * x
        cheb_ref[0:1] = jnp.sum(before, 0, keepdims=True)
        cheb_ref[1:2] = jnp.sum(now, 0, keepdims=True)
        twice = 2.0 * x
        for order in range(2, NODES):
            before, now = now, twice * now - before
            cheb_ref[order : order + 1] = jnp.sum(now, 0, keepdims=True)
        mixed = exact_dot(mix_ref[...], cheb_ref[...])
        weight = mixed[:NODES]
        weight_ref[:, cols] = jnp.concatenate([weight, skip_ref[:, cols], zeros(7, width)], 0)

        if step == 0:
            for copy in rows:
                copy.wait()
        side = side_ref[:, cols]
        row0, row1, edge, moment = side[0:1], side[1:2], side[2:4], side[8:]
        high, low = split(moment)
        state = dot(near_ref[...], jnp.concatenate([high, high, low, jnp.zeros_like(low)], 0))
        stacked = jnp.concatenate(
            [weight * state, weight * row0, weight * row1, zeros(PAD - 3 * NODES, width)], 0
        )
        high, low = split(stacked)
        stacked = jnp.concatenate([high, high, low], 0)

        for copy in signals[step]:
            copy.wait()
        product = featurize(k_ref[:, cols].astype(F32), taps_ref[1, :, cols]) * featurize(
            v_ref[:, cols].astype(F32), taps_ref[2, :, cols]
        )
        full_ref[:, cols] = jnp.where(row == 0, row0, jnp.where(row == 1, row1, product)).astype(BF16)
        product = jnp.where(row < 2, 0.0, product).astype(BF16)
        twin = jnp.concatenate([product, product], 0)
        if step == 0:
            for copy in matrices:
                copy.wait()
        for part in range(width // 256):
            inner = slice(part * 256, part * 256 + 256)
            total = dot(spread_ref[pl.ds(pl.multiple_of(core * block, block), block)], stacked[:, inner])
            for k in range(RANK):
                total += mixed[NODES + k : NODES + k + 1, inner] * dot(
                    toeplitz_ref[k * block : (k + 1) * block], twin[:, inner]
                )
            local_ref[:, step * width + part * 256 : step * width + part * 256 + 256] = total

        queries[step].wait()
        values = q_ref[:, cols].astype(F32)
        taps = taps_ref[0, :, cols]
        one = jnp.where(row == 0, edge[1:2], pltpu.roll(values, 1, 0))
        two = jnp.where(row == 0, edge[0:1], jnp.where(row == 1, edge[1:2], pltpu.roll(values, 2, 0)))
        feat_ref[:, cols] = (taps[0:1] * values + taps[1:2] * one + taps[2:3] * two).astype(BF16)


def out_kernel(feat_ref, full_ref, local_ref, weight_ref, got_ref, carry_ref, spread_ref, out_ref, held, sems):
    place = lax.axis_index("ctx")
    carry = carry_ref[pl.ds(pl.multiple_of(place * 2 * NODES, 2 * NODES), 2 * NODES)]
    _, block, width = held.shape
    spread = spread_ref[pl.ds(pl.multiple_of(lax.rem(place, 2) * block, block), block)]
    copies = []
    for step in range(held.shape[0]):
        cols = slice(step * width, (step + 1) * width)
        state = dot(carry, got_ref[:, cols])
        state = weight_ref[:NODES, cols] * (state[:NODES] + state[NODES:])
        high, low = split(jnp.concatenate([state, zeros(PAD - NODES, width)], 0))
        convolved = local_ref[:, cols] + dot(spread, jnp.concatenate([high, high, low], 0))
        skip = weight_ref[NODES : NODES + 1, cols]
        held[step] = (
            feat_ref[:, cols].astype(F32) * (rounded(convolved) + skip * full_ref[:, cols].astype(F32))
        ).astype(BF16)
        copies.append(pltpu.make_async_copy(held.at[step], out_ref.at[:, pl.ds(step * width, width)], sems.at[step]))
        copies[-1].start()
    for copy in copies:
        copy.wait()


def on_device(query_proj, key_proj, value_proj, short_filter, skip_gain, pole_rates, pole_residues):
    block, channels = query_proj.shape
    devices = lax.axis_size("ctx")
    poles = pole_rates.shape[1]
    mix, toeplitz, moment, first, widen, near, carry, spread = (jnp.asarray(table) for table in tables(block, devices))
    width = 512
    grid = (channels // width,)

    def cols(rows):
        return pl.BlockSpec((rows, width), lambda i: (0, i))

    def fixed(array):
        return pl.BlockSpec(array.shape, lambda i: (0,) * array.ndim)

    taps_spec = pl.BlockSpec((3, 3, width), lambda i: (0, 0, i))
    hbm = pl.BlockSpec(memory_space=pltpu.HBM)
    vmem = pl.BlockSpec(memory_space=pltpu.VMEM)
    params = pltpu.CompilerParams(vmem_limit_bytes=32 * MIB)
    keep = functools.partial(pltpu.with_memory_space_constraint, memory_space=pltpu.HBM)
    query_proj, key_proj, value_proj = keep(query_proj), keep(key_proj), keep(value_proj)
    swap = [(i, i ^ 1) for i in range(devices)]

    edges, outer = pl.pallas_call(
        edge_kernel,
        in_specs=[hbm, hbm, hbm],
        out_specs=[vmem, vmem],
        out_shape=[pltpu.VMEM((16, channels), BF16), pltpu.VMEM((8, channels), BF16)],
        scratch_shapes=[pltpu.VMEM((5, 16, channels), BF16), pltpu.SemaphoreType.DMA((5,))],
        compiler_params=params,
        name="edges",
    )(query_proj, key_proj, value_proj)
    between = [(i, i + 1) for i in range(1, devices - 1, 2)]
    outer = lax.ppermute(outer, "ctx", between + [(j, i) for i, j in between])

    near_sums, inner = pl.pallas_call(
        moment_kernel,
        in_specs=[vmem, hbm, hbm, hbm, hbm],
        out_specs=[vmem, vmem],
        out_shape=[pltpu.VMEM((RANK, channels), F32), pltpu.VMEM((2 * RANK, channels), BF16)],
        scratch_shapes=[
            pltpu.VMEM((2, channels // width, block, width), BF16),
            pltpu.VMEM(short_filter.shape, F32),
            pltpu.VMEM(moment.shape, BF16),
            pltpu.SemaphoreType.DMA((2 * (channels // width) + 2,)),
        ],
        compiler_params=params,
        cost_estimate=pl.CostEstimate(
            flops=1, bytes_accessed=1, transcendentals=0
        ),
        name="moments",
    )(edges, key_proj, value_proj, keep(short_filter), keep(moment))
    inner, outer = lax.optimization_barrier((inner, outer))
    inner = lax.ppermute(inner, "ctx", swap)
    outer_more = lax.ppermute(outer, "ctx", swap)

    sent, side = pl.pallas_call(
        merge_kernel,
        in_specs=[vmem] * 8,
        out_specs=[hbm, vmem],
        out_shape=[
            pltpu.HBM((devices // 2 * RANK, channels), BF16),
            pltpu.VMEM((2 * RANK, channels), F32),
        ],
        scratch_shapes=[pltpu.VMEM((16, channels), BF16), pltpu.SemaphoreType.DMA((devices // 2 * RANK // 16,))],
        compiler_params=params,
        name="merge",
    )(edges, inner, outer, outer_more, near_sums, short_filter, first, widen)

    groups = [[2 * chip + core for chip in chip_order(devices // 2)] for core in range(2)]
    got = lax.all_to_all(sent, "ctx", 0, 0, axis_index_groups=groups, tiled=True)

    local_args = tuple(
        keep(arg)
        for arg in (query_proj, key_proj, value_proj, short_filter, skip_gain.reshape(1, -1), pole_rates.T,
                    pole_residues.T, mix, toeplitz, near, spread)
    )
    feat, full, local, weight = pl.pallas_call(
        local_kernel,
        in_specs=[vmem] + [hbm] * len(local_args),
        out_specs=[vmem] * 4,
        out_shape=[
            pltpu.VMEM((block, channels), BF16),
            pltpu.VMEM((block, channels), BF16),
            pltpu.VMEM((block, channels), F32),
            pltpu.VMEM((NODES + 8, channels), F32),
        ],
        scratch_shapes=[pltpu.VMEM(arg.shape, arg.dtype) for arg in local_args]
        + [pltpu.VMEM((NODES, width), F32), pltpu.SemaphoreType.DMA((9 + 3 * (channels // width),))],
        compiler_params=params,
        cost_estimate=pl.CostEstimate(
            flops=8 * toeplitz.size * channels, bytes_accessed=16 * block * channels, transcendentals=0
        ),
        name="local",
    )(side, *local_args)

    return pl.pallas_call(
        out_kernel,
        in_specs=[vmem] * 7,
        out_specs=hbm,
        out_shape=pltpu.HBM((block, channels), BF16),
        scratch_shapes=[
            pltpu.VMEM((channels // width, block, width), BF16),
            pltpu.SemaphoreType.DMA((channels // width,)),
        ],
        compiler_params=params,
        name="output",
    )(feat, full, local, weight, got, carry, spread)


def solution(mesh):
    placed = (
        P("ctx", "tp"),
        P("ctx", "tp"),
        P("ctx", "tp"),
        P(None, None, "tp"),
        P("tp"),
        P("tp", None),
        P("tp", None),
    )
    return jax.shard_map(
        on_device, mesh=mesh, in_specs=placed, out_specs=P("ctx", "tp"), check_vma=False
    )
```

time: 32.6 us -> 29.5 us (0.905)
  waiting for transfers between devices: 6.92 us -> 2.82 us
  starting transfers between devices: 12.2 us -> 13.6 us
    all_to_all x1, waiting for transfers between devices: 6.05 us -> 1.7 us  [on_device(): lax.all_to_all(sent, 'ctx', 0, 0, axis_index_groups=groups, tiled=True)]
    all_to_all x1, starting transfers between devices: 7.61 us -> 9.42 us  [on_device(): lax.all_to_all(sent, 'ctx', 0, 0, axis_index_groups=groups, tiled=True)]
    ppermute x4 -> x3, starting transfers between devices: 4.61 us -> 4.2 us  [the longest x1 3.44 us: on_device(): inner = lax.ppermute(inner, 'ctx', swap)]
    pallas_call x3, Pallas kernels: 10.3 us -> 9.92 us  [the longest x1 6 us: on_device(): pl.pallas_call(local_kernel, in_specs=[vmem] + [hbm] * len(local_args), o...]
    ppermute x4 -> x3, waiting for transfers between devices: 0.86 us -> 1.12 us  [the longest x1 1.11 us: on_device(): outer_more = lax.ppermute(outer, 'ctx', swap)]
  transfers between devices with their start and end apart: 5 -> 4, of which waited for: 3 -> 2; matrix products, arithmetic and copies ran while one was open for 0% -> 0% of each run, Pallas kernels for 27% -> 30%
where the time goes in v3:
time: 29.5 us; the launch traced here: 29.2 us
  starting transfers between devices  13.6 us (46%)
  Pallas kernels  12.7 us (43%)
  waiting for transfers between devices  2.82 us (10%)
    all_to_all x1, starting transfers between devices, on_device(): lax.all_to_all(sent, 'ctx', 0, 0, axis_index_groups=groups, tiled=True)  9.42 us
    pallas_call x1, Pallas kernels, on_device(): pl.pallas_call(local_kernel, in_specs=[vmem] + [hbm] * len(local_args), o...  6 us
    ppermute x1, starting transfers between devices, on_device(): inner = lax.ppermute(inner, 'ctx', swap)  3.44 us
    pallas_call x1, Pallas kernels, on_device(): pl.pallas_call(moment_kernel, in_specs=[vmem, hbm, hbm, hbm, hbm], out_sp...  2.7 us
    all_to_all x1, waiting for transfers between devices, on_device(): lax.all_to_all(sent, 'ctx', 0, 0, axis_index_groups=groups, tiled=True)  1.7 us
    pallas_call x1, Pallas kernels, on_device(): pl.pallas_call(out_kernel, in_specs=[vmem] * 7, out_specs=hbm, out_shape=...  1.69 us
    pallas_call x1, Pallas kernels, on_device(): pl.pallas_call(merge_kernel, in_specs=[vmem] * 8, out_specs=[hbm, vmem],...  1.21 us
    ppermute x1, waiting for transfers between devices, on_device(): outer_more = lax.ppermute(outer, 'ctx', swap)  1.11 us
  transfers between devices with their start and end apart: 4, of which 2 were waited for; matrix products, arithmetic and copies ran while one was open for 0% of the time, Pallas kernels for 30%

profile of v3, /device:TPU:0, one launch (start us, length us, event | category | flops | bytes accessed | tf_op | source)
XLA Modules:
  0.0 29.2 jit_solution(4974772648525939437)
XLA Ops:
  0.0 1.1 %edges.1 = (bf16[16,2048]{1,0:T(8,128)(2,1)S(1)}, bf16[8,2048]{1,0:T(8,128)(2,1)S(1)}) custom-call(bf16[128,2048]{1,0:T(8,128)(2,1)} %q_hbm.1, bf16[128,2048]{1,0:T(8,128)(2,1)} %k_hbm.1, bf16[128,2048]{1,0:T(8,128)(2,1)} %v_hbm.1), custom_call_target="tpu_custom_call" | custom-call | tf_op jit(solution)/shard_map/edges/pallas_call | solution.py:367
  1.1 0.7 %collective-permute-start = (bf16[8,2048]{1,0:T(8,128)(2,1)S(1)}, bf16[8,2048]{1,0:T(8,128)(2,1)S(1)}, u32[]{:S(2)}, u32[]{:S(2)}) collective-permute-start(bf16[8,2048]{1,0:T(8,128)(2,1)S(1)} %get-tuple-element.19), channel_id=1, source_target_pairs={{4,8},{12,16},{20,24},{28,32},{36,40},{44,48},{52,56},{60,64},{68,... | collective-permute-start | bytes 98312 | tf_op jit(solution)/shard_map/ppermute | solution.py:377
  1.7 0.0 copy-start
  1.7 0.0 copy-start.3
  1.8 2.7 %moments.1 = (f32[8,2048]{1,0:T(8,128)S(1)}, bf16[16,2048]{1,0:T(8,128)(2,1)S(1)}) custom-call(bf16[16,2048]{1,0:T(8,128)(2,1)S(1)} %get-tuple-element.17.edges_ref, bf16[128,2048]{1,0:T(8,128)(2,1)} %k_hbm.1, bf16[128,2048]{1,0:T(8,128)(2,1)} %v_hbm.1, f32[3,3,2048]{2,1,0:T(4,128)} %taps_hbm.3, bf16[8,256]{1,0:T(8,128)(2,1)} %constant.18.clone.moment_hbm), custom_call_target="tpu_custom_call" | custom-call | flops 1 | bytes 1 | tf_op jit(solution)/shard_map/moments/pallas_call | solution.py:379
  4.5 0.0 copy-start.4
  4.5 0.0 collective-permute-done.outer_ref
  4.5 3.4 %collective-permute-start.1 = (bf16[16,2048]{1,0:T(8,128)(2,1)S(1)}, bf16[16,2048]{1,0:T(8,128)(2,1)S(1)}, u32[]{:S(2)}, u32[]{:S(2)}) collective-permute-start(bf16[16,2048]{1,0:T(8,128)(2,1)S(1)} %get-tuple-element.20), channel_id=1, source_target_pairs={{0,4},{4,0},{8,12},{12,8},{16,20},{20,16},{24,28},{28,24},{32,36},... | collective-permute-start | bytes 196616 | tf_op jit(solution)/shard_map/ppermute | solution.py:397
  7.9 0.1 collective-permute-start.2
  8.0 1.1 %collective-permute-done.2.outer_more_ref = bf16[8,2048]{1,0:T(8,128)(2,1)S(1)} collective-permute-done((bf16[8,2048]{1,0:T(8,128)(2,1)S(1)}, bf16[8,2048]{1,0:T(8,128)(2,1)S(1)}, u32[]{:S(2)}, u32[]{:S(2)}) %collective-permute-start.2) | collective-permute-done | bytes 32800 | tf_op jit(solution)/shard_map/ppermute | solution.py:398
  9.1 0.0 collective-permute-done.1.inner_ref
  9.1 0.0 copy-done
  9.1 0.0 copy-done.3
  9.1 0.0 copy-done.4
  9.2 1.2 %merge.1 = (bf16[128,2048]{1,0:T(8,128)(2,1)}, f32[16,2048]{1,0:T(8,128)S(1)}) custom-call(bf16[16,2048]{1,0:T(8,128)(2,1)S(1)} %get-tuple-element.17.edges_ref, bf16[16,2048]{1,0:T(8,128)(2,1)S(1)} %collective-permute-done.1.inner_ref, bf16[8,2048]{1,0:T(8,128)(2,1)S(1)} %collective-permute-done.outer_ref, ...), custom_call_target="tpu_custom_call" | custom-call | tf_op jit(solution)/shard_map/merge/pallas_call | solution.py:400
  10.4 9.4 %all-to-all-start = ((bf16[16,8,2048]{2,1,0:T(8,128)(2,1)}), bf16[16,8,2048]{2,1,0:T(8,128)(2,1)S(1)}, u32[]{:S(2)}, u32[]{:S(2)}) async-start(bf16[16,8,2048]{2,1,0:T(8,128)(2,1)} %bitcast.6), calls=%async_computation | async-start | bytes 1048576 | tf_op jit(solution)/shard_map/all_to_all | solution.py:414
  19.8 0.0 copy-start.1
  19.8 0.0 copy-start.2
  19.8 6.0 %local.1 = (bf16[128,2048]{1,0:T(8,128)(2,1)S(1)}, bf16[128,2048]{1,0:T(8,128)(2,1)S(1)}, f32[128,2048]{1,0:T(8,128)S(1)}, f32[32,2048]{1,0:T(8,128)S(1)}) custom-call(f32[16,2048]{1,0:T(8,128)S(1)} %get-tuple-element.23.side_ref, bf16[128,2048]{1,0:T(8,128)(2,1)} %q_hbm.1, bf16[128,2048]{1,0:T(8,128)(2,1)} %k_hbm.1, bf16[128,2048]{1,0:T(8,128)(2,1)} %v_hbm.1, ...), custom_call_target="tpu_custom_call" | custom-call | flops 4294967296 | bytes 4194304 | tf_op jit(solution)/shard_map/local/pallas_call | solution.py:421
  25.8 1.7 %all-to-all-done = bf16[16,8,2048]{2,1,0:T(8,128)(2,1)S(1)} async-done(((bf16[16,8,2048]{2,1,0:T(8,128)(2,1)}), bf16[16,8,2048]{2,1,0:T(8,128)(2,1)S(1)}, u32[]{:S(2)}, u32[]{:S(2)}) %all-to-all-start) | async-done | bytes 524320 | tf_op jit(solution)/shard_map/all_to_all | solution.py:414
  27.5 0.0 copy-done.1
  27.5 0.0 copy-done.2
  27.5 1.7 %output.1 = bf16[128,2048]{1,0:T(8,128)(2,1)} custom-call(bf16[128,2048]{1,0:T(8,128)(2,1)S(1)} %get-tuple-element.24.feat_ref, bf16[128,2048]{1,0:T(8,128)(2,1)S(1)} %get-tuple-element.25.full_ref, f32[128,2048]{1,0:T(8,128)S(1)} %get-tuple-element.26.local_ref, f32[32,2048]{1,0:T(8,128)S(1)} %get-tuple-element.27.weight_ref, ...), custom_call_target="tpu_custom_call" | custom-call | tf_op jit(solution)/shard_map/output/pallas_call | solution.py:440
Async XLA Ops:
  1.1 3.4 %collective-permute-start = (bf16[8,2048]{1,0:T(8,128)(2,1)S(1)}, bf16[8,2048]{1,0:T(8,128)(2,1)S(1)}, u32[]{:S(2)}, u32[]{:S(2)}) collective-permute-start(bf16[8,2048]{1,0:T(8,128)(2,1)S(1)} %get-tuple-element.19), channel_id=1, source_target_pairs={{4,8},{12,16},{20,24},{28,32},{36,40},{44,48},{52,56},{60,64},{68,... | collective-permute-start | bytes 98312 | tf_op jit(solution)/shard_map/ppermute | solution.py:377
  1.7 7.4 %copy-start = (f32[3,3,2048]{2,1,0:T(4,128)S(1)}, f32[3,3,2048]{2,1,0:T(4,128)}, u32[]{:S(2)}) copy-start(f32[3,3,2048]{2,1,0:T(4,128)} %taps_hbm.3) | copy-start | bytes 221188
  1.7 7.4 %copy-start.3 = (f32[16,128]{1,0:T(8,128)S(1)}, f32[16,128]{1,0:T(8,128)}, u32[]{:S(2)}) copy-start(f32[16,128]{1,0:T(8,128)} %constant.19.clone.first_ref) | copy-start | bytes 24580
  4.5 4.7 %copy-start.4 = (bf16[8,64]{1,0:T(8,128)(2,1)S(1)}, bf16[8,64]{1,0:T(8,128)(2,1)}, u32[]{:S(2)}) copy-start(bf16[8,64]{1,0:T(8,128)(2,1)} %constant.20.clone.widen_ref) | copy-start | bytes 3076
  4.5 4.7 %collective-permute-start.1 = (bf16[16,2048]{1,0:T(8,128)(2,1)S(1)}, bf16[16,2048]{1,0:T(8,128)(2,1)S(1)}, u32[]{:S(2)}, u32[]{:S(2)}) collective-permute-start(bf16[16,2048]{1,0:T(8,128)(2,1)S(1)} %get-tuple-element.20), channel_id=1, source_target_pairs={{0,4},{4,0},{8,12},{12,8},{16,20},{20,16},{24,28},{28,24},{32,36},... | collective-permute-start | bytes 196616 | tf_op jit(solution)/shard_map/ppermute | solution.py:397
  7.9 1.2 %collective-permute-start.2 = (bf16[8,2048]{1,0:T(8,128)(2,1)S(1)}, bf16[8,2048]{1,0:T(8,128)(2,1)S(1)}, u32[]{:S(2)}, u32[]{:S(2)}) collective-permute-start(bf16[8,2048]{1,0:T(8,128)(2,1)S(1)} %collective-permute-done.outer_ref), channel_id=1, source_target_pairs={{0,4},{4,0},{8,12},{12,8},{16,20},{20,16},{24,28},{28,24},{32,36},... | collective-permute-start | bytes 98312 | tf_op jit(solution)/shard_map/ppermute | solution.py:398
  10.4 17.2 %all-to-all-start = ((bf16[16,8,2048]{2,1,0:T(8,128)(2,1)}), bf16[16,8,2048]{2,1,0:T(8,128)(2,1)S(1)}, u32[]{:S(2)}, u32[]{:S(2)}) async-start(bf16[16,8,2048]{2,1,0:T(8,128)(2,1)} %bitcast.6), calls=%async_computation | async-start | bytes 1048576 | tf_op jit(solution)/shard_map/all_to_all | solution.py:414
  19.8 7.7 %copy-start.1 = (bf16[1536,128]{1,0:T(8,128)(2,1)S(1)}, bf16[1536,128]{1,0:T(8,128)(2,1)}, u32[]{:S(2)}) copy-start(bf16[1536,128]{1,0:T(8,128)(2,1)} %constant.22.clone.carry_ref) | copy-start | bytes 1179652
  19.8 7.7 %copy-start.2 = (bf16[256,240]{1,0:T(8,128)(2,1)S(1)}, bf16[256,240]{1,0:T(8,128)(2,1)}, u32[]{:S(2)}) copy-start(bf16[256,240]{1,0:T(8,128)(2,1)} %constant.23.clone.spread_hbm.spread_ref) | copy-start | bytes 368644

commit v4 on v3

--- a/solution.py
+++ b/solution.py
@@ -14,6 +14,7 @@
 NODES = 24
 RANK = 8
 PAD = 80
+ROW = 4
 F32 = jnp.float32
 BF16 = jnp.bfloat16
 MIB = 1024 * 1024
@@ -36,8 +37,15 @@
     return basis * np.sign(basis[:, :1])
 
 
+def shift_of(chip):
+    return 0 if chip % ROW == 0 else 2
+
+
+ORDER = (10, 14, 11, 15, 6, 7, 13, 9, 3, 2, 5, 8, 12, 1, 4, 0)
+
+
 def chip_order(chips):
-    return list(range(chips))[::-1]
+    return ORDER if chips == len(ORDER) else tuple(range(chips))
 
 
 @functools.lru_cache(maxsize=None)
@@ -63,17 +71,23 @@
     moment = np.concatenate(split_np(near_back), 1)
     first = np.zeros((2 * RANK, 128), np.float32)
     first[:RANK, 0:2] = near_back[:, :2]
-    first[:RANK, 2:4] = near_back[:, -2:]
     first[RANK:, 0:2] = wide[:, 1::-1]
-    widen = np.concatenate([wide[:, block + 2 :] @ near.T, wide[:, 2 : block + 2] @ near.T], 1)
-    high, low = split_np(widen)
+    widen = [
+        np.concatenate([wide[:, by + block : by + 2 * block] @ near.T, wide[:, by : by + block] @ near.T], 1)
+        for by in (0, 2)
+    ]
+    blank = np.zeros_like(widen[0])
+    high, low = split_np(np.concatenate([widen[0], blank, widen[1], blank], 0))
     widen = np.concatenate([high, low, high, np.zeros_like(high)], 1)
 
     chips = devices // 2
     place = np.arange(devices)
-    gap = (place // 2)[:, None] - 1 - np.array(chip_order(chips))[None, :]
-    lead = 2 * block * np.maximum(gap, 0) + (place % 2)[:, None] * (block - 2)
-    decay = np.where(gap[:, None, :] >= 0, np.exp(-nodes[None, :, None] * lead[:, None, :]), 0.0)
+    sources = np.array(chip_order(chips))
+    starts = np.array([2 * block * (i // 2) + (block if i % 2 else shift_of(i // 2)) for i in place])
+    ends = np.array([2 * block * (chip + 1) + shift_of(chip + 1) for chip in sources])
+    lead = np.maximum(starts[:, None] - ends[None, :], 0)
+    before = (place // 2)[:, None] > sources[None, :]
+    decay = np.where(before[:, None, :], np.exp(-nodes[None, :, None] * lead[:, None, :]), 0.0)
     carry = (decay[:, :, :, None] * wide_share[None, :, None, :]).reshape(devices, NODES, chips * RANK)
     carry = np.concatenate(split_np(carry), 1).reshape(devices * 2 * NODES, chips * RANK)
 
@@ -110,25 +124,23 @@
     return jnp.zeros((rows, columns), F32)
 
 
-def edge_kernel(q_ref, k_ref, v_ref, edges_ref, outer_ref, held, sems):
+def edge_kernel(q_ref, k_ref, v_ref, heads_ref, tails_ref, outer_ref, held, sems):
     block, columns = q_ref.shape
     copies = []
-    for idx, (ref, start) in enumerate(
-        ((q_ref, block - 16), (k_ref, block - 16), (v_ref, block - 16), (k_ref, 0), (v_ref, 0))
-    ):
-        copies.append(pltpu.make_async_copy(ref.at[pl.ds(start, 16)], held.at[idx], sems.at[idx]))
+    for idx, ref in enumerate((k_ref, v_ref, q_ref)):
+        copies.append(pltpu.make_async_copy(ref.at[pl.ds(0, 16)], held.at[idx], sems.at[idx]))
+        copies.append(pltpu.make_async_copy(ref.at[pl.ds(block - 16, 16)], held.at[idx + 3], sems.at[idx + 3]))
     for copy in copies:
         copy.start()
     for copy in copies:
         copy.wait()
-    tails = [held[idx].astype(F32)[14:16] for idx in range(3)]
-    heads = [held[idx].astype(F32)[0:2] for idx in (3, 4)]
-    edges_ref[...] = jnp.concatenate(tails + heads + [zeros(6, columns)], 0).astype(BF16)
-    lower = lax.rem(lax.axis_index("ctx"), 2) == 0
-    outer = jnp.where(
-        lower, jnp.concatenate(heads + [zeros(4, columns)], 0), jnp.concatenate(tails + [zeros(2, columns)], 0)
-    )
-    outer_ref[...] = outer.astype(BF16)
+    heads = [held[idx].astype(F32)[0:2] for idx in range(3)]
+    tails = [held[idx + 3].astype(F32)[14:16] for idx in range(3)]
+    heads = jnp.concatenate(heads + [zeros(2, columns)], 0)
+    tails = jnp.concatenate(tails + [zeros(2, columns)], 0)
+    heads_ref[...] = heads.astype(BF16)
+    tails_ref[...] = tails.astype(BF16)
+    outer_ref[...] = jnp.where(lax.rem(lax.axis_index("ctx"), 2) == 0, heads, tails).astype(BF16)
 
 
 def featurize(values, taps):
@@ -138,42 +150,19 @@
     return rounded(taps[0:1] * values + taps[1:2] * one + taps[2:3] * two)
 
 
-def moment_kernel(edges_ref, k_ref, v_ref, taps_hbm, moment_hbm, near_ref, inner_ref, held, taps_ref, moment_ref,
-                  sems):
+def moment_kernel(heads_ref, tails_ref, k_ref, v_ref, taps_ref, moment_ref, near_ref, inner_ref, *, width):
     block, columns = k_ref.shape
-    width = held.shape[-1]
     steps = columns // width
-    copies = []
-    for step in range(steps):
-        cols = pl.ds(step * width, width)
-        copies.append(
-            [
-                pltpu.make_async_copy(ref.at[:, cols], held.at[idx, step], sems.at[2 * step + idx])
-                for idx, ref in enumerate((k_ref, v_ref))
-            ]
-        )
-    copies[0].append(pltpu.make_async_copy(taps_hbm, taps_ref, sems.at[2 * steps]))
-    copies[0].append(pltpu.make_async_copy(moment_hbm, moment_ref, sems.at[2 * steps + 1]))
-    for group in copies:
-        for copy in group:
-            copy.start()
     row = lax.broadcasted_iota(jnp.int32, (block, width), 0)
-    place = lax.axis_index("ctx")
-    lower = lax.rem(place, 2) == 0
-    first_row = jnp.where(place == 0, 0, 2)
     for step in range(steps):
         cols = slice(step * width, (step + 1) * width)
-        for copy in copies[step]:
-            copy.wait()
-        key_feat = featurize(held[0, step].astype(F32), taps_ref[1, :, cols])
-        value_feat = featurize(held[1, step].astype(F32), taps_ref[2, :, cols])
-        product = jnp.where(row < first_row, 0.0, key_feat * value_feat).astype(BF16)
+        key_feat = featurize(k_ref[:, cols].astype(F32), taps_ref[1, :, cols])
+        value_feat = featurize(v_ref[:, cols].astype(F32), taps_ref[2, :, cols])
+        product = jnp.where(row < 2, 0.0, key_feat * value_feat).astype(BF16)
         near = dot(moment_ref[...], jnp.concatenate([product, product], 0))
         near_ref[:, cols] = near
-        edges = edges_ref[:, cols].astype(F32)
-        for_upper = jnp.concatenate([edges[0:6], zeros(2, width)], 0)
-        for_lower = jnp.concatenate([edges[6:10], edges[2:6]], 0)
-        inner_ref[:, cols] = jnp.concatenate([near, jnp.where(lower, for_upper, for_lower)], 0).astype(BF16)
+        rows = [tails_ref[:, cols].astype(F32), heads_ref[:, cols].astype(F32), zeros(8, width)]
+        inner_ref[:, cols] = jnp.concatenate([near] + rows, 0).astype(BF16)
 
 
 def two_rows(head, tail, taps):
@@ -188,25 +177,29 @@
     return rounded(key[0] * value[0]), rounded(key[1] * value[1])
 
 
-def merge_kernel(edges_ref, inner_ref, outer_ref, outer_more_ref, near_ref, taps_ref, first_ref, widen_ref, sent_ref,
-                 side_ref, held, sems):
+def merge_kernel(heads_ref, tails_ref, inner_ref, outer_ref, outer_more_ref, near_ref, taps_ref, first_ref, widen_ref,
+                 sent_ref, side_ref, held, sems):
     place = lax.axis_index("ctx")
     lower = lax.rem(place, 2) == 0
-    edges, inner = edges_ref[...].astype(F32), inner_ref[...].astype(F32)
+    chip = lax.div(place, 2)
+    opens, closes = lax.rem(chip, ROW) == 0, lax.rem(chip + 1, ROW) == 0
+    heads, tails, inner = heads_ref[...].astype(F32)[0:4], tails_ref[...].astype(F32)[0:4], inner_ref[...].astype(F32)
     outer, outer_more = outer_ref[...].astype(F32), outer_more_ref[...].astype(F32)
-    a0, a1 = product_rows(edges[6:10], outer[2:6], taps_ref)
-    b0, b1 = product_rows(
-        jnp.where(lower, inner[8:12], edges[6:10]), jnp.where(lower, edges[2:6], inner[10:14]), taps_ref
-    )
-    c0, c1 = product_rows(
-        jnp.where(lower, outer_more[0:4], outer[0:4]), jnp.where(lower, inner[12:16], edges[2:6]), taps_ref
-    )
+    tails_other, heads_other = inner[8:12], inner[16:20]
+    heads0, heads1 = jnp.where(lower, heads, heads_other), jnp.where(lower, heads_other, heads)
+    tails0, tails1 = jnp.where(lower, tails, tails_other), jnp.where(lower, tails_other, tails)
+    outer0, outer1 = jnp.where(lower, outer, outer_more), jnp.where(lower, outer_more, outer)
+    a0, a1 = product_rows(heads0, outer0[0:4], taps_ref)
+    b0, b1 = product_rows(heads1, tails0, taps_ref)
+    c0, c1 = (jnp.where(closes, 0.0, row) for row in product_rows(outer1[0:4], tails1, taps_ref))
     near, near_other = near_ref[...], inner[:RANK]
     first, last = first_ref[:RANK], first_ref[RANK:]
     near0 = jnp.where(lower, near, near_other)
+    near0 += jnp.where(opens, first[:, 0:1] * a0 + first[:, 1:2] * a1, 0.0)
     near1 = jnp.where(lower, near_other, near) + first[:, 0:1] * b0 + first[:, 1:2] * b1
     high, low = split(jnp.concatenate([near0, near1], 0))
-    whole = dot(widen_ref[...], jnp.concatenate([high, high, low, jnp.zeros_like(low)], 0))
+    widen = widen_ref[pl.ds(pl.multiple_of(jnp.where(closes, 0, 2 * RANK), 2 * RANK), 2 * RANK)]
+    whole = dot(widen, jnp.concatenate([high, high, low, jnp.zeros_like(low)], 0))[:RANK]
     whole += last[:, 0:1] * c0 + last[:, 1:2] * c1
     held[...] = jnp.concatenate([whole, whole], 0).astype(BF16)
     copies = [
@@ -215,19 +208,17 @@
     ]
     for copy in copies:
         copy.start()
-    start = jnp.where(place == 0, first[:, 2:3] * a0 + first[:, 3:4] * a1, 0.0)
-    side_ref[...] = jnp.concatenate(
-        [
-            jnp.where(lower, a0, b0),
-            jnp.where(lower, a1, b1),
-            jnp.where(lower, outer[0:2], inner[8:10]),
-            zeros(4, a0.shape[1]),
-            jnp.where(lower, start, near0),
-        ],
-        0,
-    )
+    rows = [jnp.where(lower, a0, b0), jnp.where(lower, a1, b1), jnp.where(lower, outer[4:6], inner[12:14])]
+    rows += [zeros(4, a0.shape[1]), jnp.where(lower, 0.0, near0)]
+    side_ref[...] = jnp.concatenate(rows, 0)
     for copy in copies:
         copy.wait()
+
+
+def spread_start(block):
+    place = lax.axis_index("ctx")
+    plain = jnp.logical_or(lax.rem(place, 2) == 1, lax.rem(lax.div(place, 2), ROW) == 0)
+    return pl.multiple_of(jnp.where(plain, block, 0), block)
 
 
 def local_kernel(side_ref, q_hbm, k_hbm, v_hbm, taps_hbm, skip_hbm, rates_hbm, residues_hbm, mix_hbm, toeplitz_hbm,
@@ -260,7 +251,7 @@
         queries.append(load(q_hbm.at[at], q_ref.at[at]))
 
     mid, half = log_range()
-    core = lax.rem(lax.axis_index("ctx"), 2)
+    kind = spread_start(block)
     row = lax.broadcasted_iota(jnp.int32, (block, width), 0)
     for copy in filters:
         copy.wait()
@@ -305,7 +296,7 @@
                 copy.wait()
         for part in range(width // 256):
             inner = slice(part * 256, part * 256 + 256)
-            total = dot(spread_ref[pl.ds(pl.multiple_of(core * block, block), block)], stacked[:, inner])
+            total = dot(spread_ref[pl.ds(kind, block)], stacked[:, inner])
             for k in range(RANK):
                 total += mixed[NODES + k : NODES + k + 1, inner] * dot(
                     toeplitz_ref[k * block : (k + 1) * block], twin[:, inner]
@@ -324,7 +315,7 @@
     place = lax.axis_index("ctx")
     carry = carry_ref[pl.ds(pl.multiple_of(place * 2 * NODES, 2 * NODES), 2 * NODES)]
     _, block, width = held.shape
-    spread = spread_ref[pl.ds(pl.multiple_of(lax.rem(place, 2) * block, block), block)]
+    spread = spread_ref[pl.ds(spread_start(block), block)]
     copies = []
     for step in range(held.shape[0]):
         cols = slice(step * width, (step + 1) * width)
@@ -361,45 +352,41 @@
     vmem = pl.BlockSpec(memory_space=pltpu.VMEM)
     params = pltpu.CompilerParams(vmem_limit_bytes=32 * MIB)
     keep = functools.partial(pltpu.with_memory_space_constraint, memory_space=pltpu.HBM)
+    key_plain, value_plain = key_proj, value_proj
     query_proj, key_proj, value_proj = keep(query_proj), keep(key_proj), keep(value_proj)
     swap = [(i, i ^ 1) for i in range(devices)]
 
-    edges, outer = pl.pallas_call(
+    heads, tails, outer = pl.pallas_call(
         edge_kernel,
         in_specs=[hbm, hbm, hbm],
-        out_specs=[vmem, vmem],
-        out_shape=[pltpu.VMEM((16, channels), BF16), pltpu.VMEM((8, channels), BF16)],
-        scratch_shapes=[pltpu.VMEM((5, 16, channels), BF16), pltpu.SemaphoreType.DMA((5,))],
+        out_specs=[vmem] * 3,
+        out_shape=[pltpu.VMEM((8, channels), BF16)] * 3,
+        scratch_shapes=[pltpu.VMEM((6, 16, channels), BF16), pltpu.SemaphoreType.DMA((6,))],
         compiler_params=params,
         name="edges",
     )(query_proj, key_proj, value_proj)
-    between = [(i, i + 1) for i in range(1, devices - 1, 2)]
-    outer = lax.ppermute(outer, "ctx", between + [(j, i) for i, j in between])
+    between = [(i - 1, i) for i in range(2, devices, 2)]
+    between += [(i, i - 1) for i in range(2, devices, 2) if shift_of(i // 2)]
+    outer = lax.ppermute(outer, "ctx", between)
 
     near_sums, inner = pl.pallas_call(
-        moment_kernel,
-        in_specs=[vmem, hbm, hbm, hbm, hbm],
+        functools.partial(moment_kernel, width=width),
+        in_specs=[vmem, vmem] + [vmem] * 4,
         out_specs=[vmem, vmem],
-        out_shape=[pltpu.VMEM((RANK, channels), F32), pltpu.VMEM((2 * RANK, channels), BF16)],
-        scratch_shapes=[
-            pltpu.VMEM((2, channels // width, block, width), BF16),
-            pltpu.VMEM(short_filter.shape, F32),
-            pltpu.VMEM(moment.shape, BF16),
-            pltpu.SemaphoreType.DMA((2 * (channels // width) + 2,)),
-        ],
+        out_shape=[pltpu.VMEM((RANK, channels), F32), pltpu.VMEM((4 * RANK, channels), BF16)],
         compiler_params=params,
         cost_estimate=pl.CostEstimate(
             flops=1, bytes_accessed=1, transcendentals=0
         ),
         name="moments",
-    )(edges, key_proj, value_proj, keep(short_filter), keep(moment))
+    )(heads, tails, key_plain, value_plain, short_filter, moment)
     inner, outer = lax.optimization_barrier((inner, outer))
     inner = lax.ppermute(inner, "ctx", swap)
     outer_more = lax.ppermute(outer, "ctx", swap)
 
     sent, side = pl.pallas_call(
         merge_kernel,
-        in_specs=[vmem] * 8,
+        in_specs=[vmem] * 9,
         out_specs=[hbm, vmem],
         out_shape=[
             pltpu.HBM((devices // 2 * RANK, channels), BF16),
@@ -408,7 +395,7 @@
         scratch_shapes=[pltpu.VMEM((16, channels), BF16), pltpu.SemaphoreType.DMA((devices // 2 * RANK // 16,))],
         compiler_params=params,
         name="merge",
-    )(edges, inner, outer, outer_more, near_sums, short_filter, first, widen)
+    )(heads, tails, inner, outer, outer_more, near_sums, short_filter, first, widen)
 
     groups = [[2 * chip + core for chip in chip_order(devices // 2)] for core in range(2)]
     got = lax.all_to_all(sent, "ctx", 0, 0, axis_index_groups=groups, tiled=True)

time: 29.5 us -> 28.5 us (0.966)
  Pallas kernels: 12.7 us -> 11.1 us
  starting transfers between devices: 13.6 us -> 14.7 us
  waiting for transfers between devices: 2.82 us -> 2.21 us
    pallas_call x3, Pallas kernels: 4.97 us -> 3.46 us  [the longest x1 1.24 us: on_device(): pl.pallas_call(merge_kernel, in_specs=[vmem] * 9, out_specs=[hbm, vmem],...]
    all_to_all x1, starting transfers between devices: 9.42 us -> 10.2 us  [on_device(): lax.all_to_all(sent, 'ctx', 0, 0, axis_index_groups=groups, tiled=True)]
    all_to_all x1, waiting for transfers between devices: 1.7 us -> 1 us  [on_device(): lax.all_to_all(sent, 'ctx', 0, 0, axis_index_groups=groups, tiled=True)]
    ppermute x1, starting transfers between devices: 3.44 us -> 3.85 us  [on_device(): inner = lax.ppermute(inner, 'ctx', swap)]
  transfers between devices with their start and end apart: 4 -> 4, of which waited for: 2 -> 2; matrix products, arithmetic and copies ran while one was open for 0% -> 0% of each run, Pallas kernels for 30% -> 25%
where the time goes in v4:
time: 28.5 us; the launch traced here: 28.2 us
  starting transfers between devices  14.7 us (52%)
  Pallas kernels  11.1 us (39%)
  waiting for transfers between devices  2.21 us (8%)
    all_to_all x1, starting transfers between devices, on_device(): lax.all_to_all(sent, 'ctx', 0, 0, axis_index_groups=groups, tiled=True)  10.2 us
    pallas_call x1, Pallas kernels, on_device(): pl.pallas_call(local_kernel, in_specs=[vmem] + [hbm] * len(local_args), o...  5.99 us
    ppermute x1, starting transfers between devices, on_device(): inner = lax.ppermute(inner, 'ctx', swap)  3.85 us
    pallas_call x1, Pallas kernels, on_device(): pl.pallas_call(out_kernel, in_specs=[vmem] * 7, out_specs=hbm, out_shape=...  1.69 us
    pallas_call x1, Pallas kernels, on_device(): pl.pallas_call(merge_kernel, in_specs=[vmem] * 9, out_specs=[hbm, vmem],...  1.24 us
    ppermute x1, waiting for transfers between devices, on_device(): outer_more = lax.ppermute(outer, 'ctx', swap)  1.2 us
    pallas_call x1, Pallas kernels, on_device(): pl.pallas_call(edge_kernel, in_specs=[hbm, hbm, hbm], out_specs=[vmem] *...  1.18 us
    pallas_call x1, Pallas kernels, on_device(): pl.pallas_call(functools.partial(moment_kernel, width=width), in_specs=[v...  1.03 us
  transfers between devices with their start and end apart: 4, of which 2 were waited for; matrix products, arithmetic and copies ran while one was open for 0% of the time, Pallas kernels for 25%

profile of v4, /device:TPU:0, one launch (start us, length us, event | category | flops | bytes accessed | tf_op | source)
XLA Modules:
  0.0 28.2 jit_solution(16640356241398805607)
XLA Ops:
  0.0 0.0 copy-start.1
  0.0 0.0 copy-start
  0.0 0.0 copy-start.2
  0.0 1.2 %edges.1 = (bf16[8,2048]{1,0:T(8,128)(2,1)S(1)}, bf16[8,2048]{1,0:T(8,128)(2,1)S(1)}, bf16[8,2048]{1,0:T(8,128)(2,1)S(1)}) custom-call(bf16[128,2048]{1,0:T(8,128)(2,1)} %q_hbm.1, bf16[128,2048]{1,0:T(8,128)(2,1)} %k_hbm.1, bf16[128,2048]{1,0:T(8,128)(2,1)} %v_hbm.1), custom_call_target="tpu_custom_call" | custom-call | tf_op jit(solution)/shard_map/edges/pallas_call | solution.py:359
  1.2 0.0 copy-start.7
  1.2 0.7 %collective-permute-start = (bf16[8,2048]{1,0:T(8,128)(2,1)S(1)}, bf16[8,2048]{1,0:T(8,128)(2,1)S(1)}, u32[]{:S(2)}, u32[]{:S(2)}) collective-permute-start(bf16[8,2048]{1,0:T(8,128)(2,1)S(1)} %get-tuple-element.21), channel_id=1, source_target_pairs={{4,8},{12,16},{20,24},{28,32},{36,40},{44,48},{52,56},{60,64},{68,... | collective-permute-start | bytes 98312 | tf_op jit(solution)/shard_map/ppermute | solution.py:370
  1.9 0.0 copy-done.1
  1.9 0.0 copy-done
  1.9 0.0 copy-done.2
  1.9 0.0 copy-done.7
  1.9 0.0 copy-start.5
  1.9 0.0 copy-start.6
  1.9 1.0 %moments.1 = (f32[8,2048]{1,0:T(8,128)S(1)}, bf16[32,2048]{1,0:T(8,128)(2,1)S(1)}) custom-call(bf16[8,2048]{1,0:T(8,128)(2,1)S(1)} %get-tuple-element.18.heads_ref, bf16[8,2048]{1,0:T(8,128)(2,1)S(1)} %get-tuple-element.19.tails_ref, bf16[128,2048]{1,0:T(8,128)(2,1)S(1)} %copy-done, bf16[128,2048]{1,0:T(8,128)(2,1)S(1)} %copy-done.1, ...), custom_call_target="tpu_custom_call" | custom-call | flops 1 | bytes 1 | tf_op jit(solution)/shard_map/moments/pallas_call | solution.py:372
  3.0 0.0 collective-permute-done.outer_ref
  3.0 3.8 %collective-permute-start.1 = (bf16[32,2048]{1,0:T(8,128)(2,1)S(1)}, bf16[32,2048]{1,0:T(8,128)(2,1)S(1)}, u32[]{:S(2)}, u32[]{:S(2)}) collective-permute-start(bf16[32,2048]{1,0:T(8,128)(2,1)S(1)} %get-tuple-element.22), channel_id=1, source_target_pairs={{0,4},{4,0},{8,12},{12,8},{16,20},{20,16},{24,28},{28,24},{32,36},... | collective-permute-start | bytes 393224 | tf_op jit(solution)/shard_map/ppermute | solution.py:384
  6.8 0.0 collective-permute-start.2
  6.8 1.2 %collective-permute-done.2.outer_more_ref = bf16[8,2048]{1,0:T(8,128)(2,1)S(1)} collective-permute-done((bf16[8,2048]{1,0:T(8,128)(2,1)S(1)}, bf16[8,2048]{1,0:T(8,128)(2,1)S(1)}, u32[]{:S(2)}, u32[]{:S(2)}) %collective-permute-start.2) | collective-permute-done | bytes 32800 | tf_op jit(solution)/shard_map/ppermute | solution.py:385
  8.0 0.0 collective-permute-done.1.inner_ref
  8.0 0.0 copy-done.5
  8.0 0.0 copy-done.6
  8.1 1.2 %merge.1 = (bf16[128,2048]{1,0:T(8,128)(2,1)}, f32[16,2048]{1,0:T(8,128)S(1)}) custom-call(bf16[8,2048]{1,0:T(8,128)(2,1)S(1)} %get-tuple-element.18.heads_ref, bf16[8,2048]{1,0:T(8,128)(2,1)S(1)} %get-tuple-element.19.tails_ref, bf16[32,2048]{1,0:T(8,128)(2,1)S(1)} %collective-permute-done.1.inner_ref, bf16[8,2048]{1,0:T(8,128)(2,1)S(1)} %collective-permute-done.outer_ref, ...), custom_call_target="tpu_custom_call" | custom-call | tf_op jit(solution)/shard_map/merge/pallas_call | solution.py:387
  9.3 10.2 %all-to-all-start = ((bf16[16,8,2048]{2,1,0:T(8,128)(2,1)}), bf16[16,8,2048]{2,1,0:T(8,128)(2,1)S(1)}, u32[]{:S(2)}, u32[]{:S(2)}) async-start(bf16[16,8,2048]{2,1,0:T(8,128)(2,1)} %bitcast.6), calls=%async_computation | async-start | bytes 1048576 | tf_op jit(solution)/shard_map/all_to_all | solution.py:401
  19.5 0.0 copy-start.3
  19.5 0.0 copy-start.4
  19.5 6.0 %local.1 = (bf16[128,2048]{1,0:T(8,128)(2,1)S(1)}, bf16[128,2048]{1,0:T(8,128)(2,1)S(1)}, f32[128,2048]{1,0:T(8,128)S(1)}, f32[32,2048]{1,0:T(8,128)S(1)}) custom-call(f32[16,2048]{1,0:T(8,128)S(1)} %get-tuple-element.25.side_ref, bf16[128,2048]{1,0:T(8,128)(2,1)} %q_hbm.1, bf16[128,2048]{1,0:T(8,128)(2,1)} %k_hbm.1, bf16[128,2048]{1,0:T(8,128)(2,1)} %v_hbm.1, ...), custom_call_target="tpu_custom_call" | custom-call | flops 4294967296 | bytes 4194304 | tf_op jit(solution)/shard_map/local/pallas_call | solution.py:408
  25.5 1.0 %all-to-all-done = bf16[16,8,2048]{2,1,0:T(8,128)(2,1)S(1)} async-done(((bf16[16,8,2048]{2,1,0:T(8,128)(2,1)}), bf16[16,8,2048]{2,1,0:T(8,128)(2,1)S(1)}, u32[]{:S(2)}, u32[]{:S(2)}) %all-to-all-start) | async-done | bytes 524320 | tf_op jit(solution)/shard_map/all_to_all | solution.py:401
  26.5 0.0 copy-done.3
  26.5 0.0 copy-done.4
  26.5 1.7 %output.1 = bf16[128,2048]{1,0:T(8,128)(2,1)} custom-call(bf16[128,2048]{1,0:T(8,128)(2,1)S(1)} %get-tuple-element.26.feat_ref, bf16[128,2048]{1,0:T(8,128)(2,1)S(1)} %get-tuple-element.27.full_ref, f32[128,2048]{1,0:T(8,128)S(1)} %get-tuple-element.28.local_ref, f32[32,2048]{1,0:T(8,128)S(1)} %get-tuple-element.29.weight_ref, ...), custom_call_target="tpu_custom_call" | custom-call | tf_op jit(solution)/shard_map/output/pallas_call | solution.py:427
Async XLA Ops:
  0.0 1.9 %copy-start.1 = (bf16[128,2048]{1,0:T(8,128)(2,1)S(1)}, bf16[128,2048]{1,0:T(8,128)(2,1)}, u32[]{:S(2)}) copy-start(bf16[128,2048]{1,0:T(8,128)(2,1)} %v_hbm.1) | copy-start | bytes 1572868
  0.0 1.9 %copy-start = (bf16[128,2048]{1,0:T(8,128)(2,1)S(1)}, bf16[128,2048]{1,0:T(8,128)(2,1)}, u32[]{:S(2)}) copy-start(bf16[128,2048]{1,0:T(8,128)(2,1)} %k_hbm.1) | copy-start | bytes 1572868
  0.0 1.9 %copy-start.2 = (f32[3,3,2048]{2,1,0:T(4,128)S(1)}, f32[3,3,2048]{2,1,0:T(4,128)}, u32[]{:S(2)}) copy-start(f32[3,3,2048]{2,1,0:T(4,128)} %taps_hbm.1) | copy-start | bytes 221188
  1.2 0.7 %copy-start.7 = (bf16[8,256]{1,0:T(8,128)(2,1)S(1)}, bf16[8,256]{1,0:T(8,128)(2,1)}, u32[]{:S(2)}) copy-start(bf16[8,256]{1,0:T(8,128)(2,1)} %constant.18.clone.moment_ref) | copy-start | bytes 12292
  1.2 1.8 %collective-permute-start = (bf16[8,2048]{1,0:T(8,128)(2,1)S(1)}, bf16[8,2048]{1,0:T(8,128)(2,1)S(1)}, u32[]{:S(2)}, u32[]{:S(2)}) collective-permute-start(bf16[8,2048]{1,0:T(8,128)(2,1)S(1)} %get-tuple-element.21), channel_id=1, source_target_pairs={{4,8},{12,16},{20,24},{28,32},{36,40},{44,48},{52,56},{60,64},{68,... | collective-permute-start | bytes 98312 | tf_op jit(solution)/shard_map/ppermute | solution.py:370
  1.9 6.1 %copy-start.5 = (bf16[32,64]{1,0:T(8,128)(2,1)S(1)}, bf16[32,64]{1,0:T(8,128)(2,1)}, u32[]{:S(2)}) copy-start(bf16[32,64]{1,0:T(8,128)(2,1)} %constant.20.clone.widen_ref) | copy-start | bytes 12292
  1.9 6.1 %copy-start.6 = (f32[16,128]{1,0:T(8,128)S(1)}, f32[16,128]{1,0:T(8,128)}, u32[]{:S(2)}) copy-start(f32[16,128]{1,0:T(8,128)} %constant.19.clone.first_ref) | copy-start | bytes 24580
  3.0 5.1 %collective-permute-start.1 = (bf16[32,2048]{1,0:T(8,128)(2,1)S(1)}, bf16[32,2048]{1,0:T(8,128)(2,1)S(1)}, u32[]{:S(2)}, u32[]{:S(2)}) collective-permute-start(bf16[32,2048]{1,0:T(8,128)(2,1)S(1)} %get-tuple-element.22), channel_id=1, source_target_pairs={{0,4},{4,0},{8,12},{12,8},{16,20},{20,16},{24,28},{28,24},{32,36},... | collective-permute-start | bytes 393224 | tf_op jit(solution)/shard_map/ppermute | solution.py:384
  6.8 1.2 %collective-permute-start.2 = (bf16[8,2048]{1,0:T(8,128)(2,1)S(1)}, bf16[8,2048]{1,0:T(8,128)(2,1)S(1)}, u32[]{:S(2)}, u32[]{:S(2)}) collective-permute-start(bf16[8,2048]{1,0:T(8,128)(2,1)S(1)} %collective-permute-done.outer_ref), channel_id=1, source_target_pairs={{0,4},{4,0},{8,12},{12,8},{16,20},{20,16},{24,28},{28,24},{32,36},... | collective-permute-start | bytes 98312 | tf_op jit(solution)/shard_map/ppermute | solution.py:385
  9.3 17.2 %all-to-all-start = ((bf16[16,8,2048]{2,1,0:T(8,128)(2,1)}), bf16[16,8,2048]{2,1,0:T(8,128)(2,1)S(1)}, u32[]{:S(2)}, u32[]{:S(2)}) async-start(bf16[16,8,2048]{2,1,0:T(8,128)(2,1)} %bitcast.6), calls=%async_computation | async-start | bytes 1048576 | tf_op jit(solution)/shard_map/all_to_all | solution.py:401
  19.5 7.0 %copy-start.3 = (bf16[1536,128]{1,0:T(8,128)(2,1)S(1)}, bf16[1536,128]{1,0:T(8,128)(2,1)}, u32[]{:S(2)}) copy-start(bf16[1536,128]{1,0:T(8,128)(2,1)} %constant.22.clone.carry_ref) | copy-start | bytes 1179652
  19.5 7.0 %copy-start.4 = (bf16[256,240]{1,0:T(8,128)(2,1)S(1)}, bf16[256,240]{1,0:T(8,128)(2,1)}, u32[]{:S(2)}) copy-start(bf16[256,240]{1,0:T(8,128)(2,1)} %constant.23.clone.spread_hbm.spread_ref) | copy-start | bytes 368644

commit v5 on v4

--- a/solution.py
+++ b/solution.py
@@ -225,7 +225,7 @@
                  near_hbm, spread_hbm, feat_ref, full_ref, local_ref, weight_ref, q_ref, k_ref, v_ref, taps_ref,
                  skip_ref, rates_ref, residues_ref, mix_ref, toeplitz_ref, near_ref, spread_ref, cheb_ref, sems):
     block, channels = q_ref.shape
-    width = cheb_ref.shape[1]
+    width = 512
     steps = channels // width
     count = 0
 
@@ -260,54 +260,57 @@
         x = (jnp.log(rates_ref[:, cols] + SHIFT) - mid) * (1.0 / half)
         before = residues_ref[:, cols]
         now = before * x
-        cheb_ref[0:1] = jnp.sum(before, 0, keepdims=True)
-        cheb_ref[1:2] = jnp.sum(now, 0, keepdims=True)
+        cheb_ref[0:1, cols] = jnp.sum(before, 0, keepdims=True)
+        cheb_ref[1:2, cols] = jnp.sum(now, 0, keepdims=True)
         twice = 2.0 * x
         for order in range(2, NODES):
             before, now = now, twice * now - before
-            cheb_ref[order : order + 1] = jnp.sum(now, 0, keepdims=True)
-        mixed = exact_dot(mix_ref[...], cheb_ref[...])
-        weight = mixed[:NODES]
-        weight_ref[:, cols] = jnp.concatenate([weight, skip_ref[:, cols], zeros(7, width)], 0)
-
-        if step == 0:
-            for copy in rows:
-                copy.wait()
-        side = side_ref[:, cols]
-        row0, row1, edge, moment = side[0:1], side[1:2], side[2:4], side[8:]
-        high, low = split(moment)
-        state = dot(near_ref[...], jnp.concatenate([high, high, low, jnp.zeros_like(low)], 0))
-        stacked = jnp.concatenate(
-            [weight * state, weight * row0, weight * row1, zeros(PAD - 3 * NODES, width)], 0
-        )
-        high, low = split(stacked)
-        stacked = jnp.concatenate([high, high, low], 0)
-
+            cheb_ref[order : order + 1, cols] = jnp.sum(now, 0, keepdims=True)
+    mixed = exact_dot(mix_ref[...], cheb_ref[...])
+    weight = mixed[:NODES]
+    weight_ref[...] = jnp.concatenate([weight, skip_ref[...], zeros(7, channels)], 0)
+    for copy in rows:
+        copy.wait()
+    side = side_ref[...]
+    row0, row1, edge = side[0:1], side[1:2], side[2:4]
+    high, low = split(side[8:])
+    state = dot(near_ref[...], jnp.concatenate([high, high, low, jnp.zeros_like(low)], 0))
+    stacked = jnp.concatenate(
+        [weight * state, weight * row0, weight * row1, zeros(PAD - 3 * NODES, channels)], 0
+    )
+    high, low = split(stacked)
+    stacked = jnp.concatenate([high, high, low], 0)
+    for copy in matrices:
+        copy.wait()
+    spread = spread_ref[pl.ds(kind, block)]
+
+    for step in range(steps):
+        cols = slice(step * width, (step + 1) * width)
         for copy in signals[step]:
             copy.wait()
         product = featurize(k_ref[:, cols].astype(F32), taps_ref[1, :, cols]) * featurize(
             v_ref[:, cols].astype(F32), taps_ref[2, :, cols]
         )
-        full_ref[:, cols] = jnp.where(row == 0, row0, jnp.where(row == 1, row1, product)).astype(BF16)
+        full_ref[:, cols] = jnp.where(
+            row == 0, row0[:, cols], jnp.where(row == 1, row1[:, cols], product)
+        ).astype(BF16)
         product = jnp.where(row < 2, 0.0, product).astype(BF16)
         twin = jnp.concatenate([product, product], 0)
-        if step == 0:
-            for copy in matrices:
-                copy.wait()
         for part in range(width // 256):
             inner = slice(part * 256, part * 256 + 256)
-            total = dot(spread_ref[pl.ds(kind, block)], stacked[:, inner])
+            outer = slice(step * width + part * 256, step * width + part * 256 + 256)
+            total = dot(spread, stacked[:, outer])
             for k in range(RANK):
-                total += mixed[NODES + k : NODES + k + 1, inner] * dot(
+                total += mixed[NODES + k : NODES + k + 1, outer] * dot(
                     toeplitz_ref[k * block : (k + 1) * block], twin[:, inner]
                 )
-            local_ref[:, step * width + part * 256 : step * width + part * 256 + 256] = total
+            local_ref[:, outer] = total
 
         queries[step].wait()
         values = q_ref[:, cols].astype(F32)
         taps = taps_ref[0, :, cols]
-        one = jnp.where(row == 0, edge[1:2], pltpu.roll(values, 1, 0))
-        two = jnp.where(row == 0, edge[0:1], jnp.where(row == 1, edge[1:2], pltpu.roll(values, 2, 0)))
+        one = jnp.where(row == 0, edge[1:2, cols], pltpu.roll(values, 1, 0))
+        two = jnp.where(row == 0, edge[0:1, cols], jnp.where(row == 1, edge[1:2, cols], pltpu.roll(values, 2, 0)))
         feat_ref[:, cols] = (taps[0:1] * values + taps[1:2] * one + taps[2:3] * two).astype(BF16)
 
 
@@ -316,13 +319,14 @@
     carry = carry_ref[pl.ds(pl.multiple_of(place * 2 * NODES, 2 * NODES), 2 * NODES)]
     _, block, width = held.shape
     spread = spread_ref[pl.ds(spread_start(block), block)]
+    state = dot(carry, got_ref[...])
+    state = weight_ref[:NODES] * (state[:NODES] + state[NODES:])
+    high, low = split(jnp.concatenate([state, zeros(PAD - NODES, state.shape[1])], 0))
+    stacked = jnp.concatenate([high, high, low], 0)
     copies = []
     for step in range(held.shape[0]):
         cols = slice(step * width, (step + 1) * width)
-        state = dot(carry, got_ref[:, cols])
-        state = weight_ref[:NODES, cols] * (state[:NODES] + state[NODES:])
-        high, low = split(jnp.concatenate([state, zeros(PAD - NODES, width)], 0))
-        convolved = local_ref[:, cols] + dot(spread, jnp.concatenate([high, high, low], 0))
+        convolved = local_ref[:, cols] + dot(spread, stacked[:, cols])
         skip = weight_ref[NODES : NODES + 1, cols]
         held[step] = (
             feat_ref[:, cols].astype(F32) * (rounded(convolved) + skip * full_ref[:, cols].astype(F32))
@@ -416,7 +420,7 @@
             pltpu.VMEM((NODES + 8, channels), F32),
         ],
         scratch_shapes=[pltpu.VMEM(arg.shape, arg.dtype) for arg in local_args]
-        + [pltpu.VMEM((NODES, width), F32), pltpu.SemaphoreType.DMA((9 + 3 * (channels // width),))],
+        + [pltpu.VMEM((NODES, channels), F32), pltpu.SemaphoreType.DMA((9 + 3 * (channels // width),))],
         compiler_params=params,
         cost_estimate=pl.CostEstimate(
             flops=8 * toeplitz.size * channels, bytes_accessed=16 * block * channels, transcendentals=0

time: 28.5 us -> 28 us (0.982)
  Pallas kernels: 11.1 us -> 9.97 us
  waiting for transfers between devices: 2.21 us -> 2.95 us
    pallas_call x1, Pallas kernels: 5.99 us -> 5.24 us  [on_device(): pl.pallas_call(local_kernel, in_specs=[vmem] + [hbm] * len(local_args), o...]
    all_to_all x1, waiting for transfers between devices: 1 us -> 1.74 us  [on_device(): lax.all_to_all(sent, 'ctx', 0, 0, axis_index_groups=groups, tiled=True)]
    pallas_call x1, Pallas kernels: 1.69 us -> 1.27 us  [on_device(): pl.pallas_call(out_kernel, in_specs=[vmem] * 7, out_specs=hbm, out_shape=...]
  transfers between devices with their start and end apart: 4 -> 4, of which waited for: 2 -> 2; matrix products, arithmetic and copies ran while one was open for 0% -> 0% of each run, Pallas kernels for 25% -> 23%
where the time goes in v5:
time: 28 us; the launch traced here: 27.8 us
  starting transfers between devices  14.7 us (52%)
  Pallas kernels  9.97 us (36%)
  waiting for transfers between devices  2.95 us (11%)
    all_to_all x1, starting transfers between devices, on_device(): lax.all_to_all(sent, 'ctx', 0, 0, axis_index_groups=groups, tiled=True)  10.2 us
    pallas_call x1, Pallas kernels, on_device(): pl.pallas_call(local_kernel, in_specs=[vmem] + [hbm] * len(local_args), o...  5.24 us
    ppermute x1, starting transfers between devices, on_device(): inner = lax.ppermute(inner, 'ctx', swap)  3.85 us
    all_to_all x1, waiting for transfers between devices, on_device(): lax.all_to_all(sent, 'ctx', 0, 0, axis_index_groups=groups, tiled=True)  1.74 us
    pallas_call x1, Pallas kernels, on_device(): pl.pallas_call(out_kernel, in_specs=[vmem] * 7, out_specs=hbm, out_shape=...  1.27 us
    pallas_call x1, Pallas kernels, on_device(): pl.pallas_call(merge_kernel, in_specs=[vmem] * 9, out_specs=[hbm, vmem],...  1.24 us
    ppermute x1, waiting for transfers between devices, on_device(): outer_more = lax.ppermute(outer, 'ctx', swap)  1.2 us
    pallas_call x1, Pallas kernels, on_device(): pl.pallas_call(edge_kernel, in_specs=[hbm, hbm, hbm], out_specs=[vmem] *...  1.18 us
  transfers between devices with their start and end apart: 4, of which 2 were waited for; matrix products, arithmetic and copies ran while one was open for 0% of the time, Pallas kernels for 23%

profile of v5, /device:TPU:0, one launch (start us, length us, event | category | flops | bytes accessed | tf_op | source)
XLA Modules:
  0.0 27.8 jit_solution(4131190430978537396)
XLA Ops:
  0.0 0.0 copy-start.1
  0.0 0.0 copy-start
  0.0 0.0 copy-start.2
  0.0 1.2 %edges.1 = (bf16[8,2048]{1,0:T(8,128)(2,1)S(1)}, bf16[8,2048]{1,0:T(8,128)(2,1)S(1)}, bf16[8,2048]{1,0:T(8,128)(2,1)S(1)}) custom-call(bf16[128,2048]{1,0:T(8,128)(2,1)} %q_hbm.1, bf16[128,2048]{1,0:T(8,128)(2,1)} %k_hbm.1, bf16[128,2048]{1,0:T(8,128)(2,1)} %v_hbm.1), custom_call_target="tpu_custom_call" | custom-call | tf_op jit(solution)/shard_map/edges/pallas_call | solution.py:363
  1.2 0.0 copy-start.7
  1.2 0.7 %collective-permute-start = (bf16[8,2048]{1,0:T(8,128)(2,1)S(1)}, bf16[8,2048]{1,0:T(8,128)(2,1)S(1)}, u32[]{:S(2)}, u32[]{:S(2)}) collective-permute-start(bf16[8,2048]{1,0:T(8,128)(2,1)S(1)} %get-tuple-element.21), channel_id=1, source_target_pairs={{4,8},{12,16},{20,24},{28,32},{36,40},{44,48},{52,56},{60,64},{68,... | collective-permute-start | bytes 98312 | tf_op jit(solution)/shard_map/ppermute | solution.py:374
  1.9 0.0 copy-done.1
  1.9 0.0 copy-done
  1.9 0.0 copy-done.2
  1.9 0.0 copy-done.7
  1.9 0.0 copy-start.5
  1.9 0.0 copy-start.6
  1.9 1.0 %moments.1 = (f32[8,2048]{1,0:T(8,128)S(1)}, bf16[32,2048]{1,0:T(8,128)(2,1)S(1)}) custom-call(bf16[8,2048]{1,0:T(8,128)(2,1)S(1)} %get-tuple-element.18.heads_ref, bf16[8,2048]{1,0:T(8,128)(2,1)S(1)} %get-tuple-element.19.tails_ref, bf16[128,2048]{1,0:T(8,128)(2,1)S(1)} %copy-done, bf16[128,2048]{1,0:T(8,128)(2,1)S(1)} %copy-done.1, ...), custom_call_target="tpu_custom_call" | custom-call | flops 1 | bytes 1 | tf_op jit(solution)/shard_map/moments/pallas_call | solution.py:376
  3.0 0.0 collective-permute-done.outer_ref
  3.0 3.8 %collective-permute-start.1 = (bf16[32,2048]{1,0:T(8,128)(2,1)S(1)}, bf16[32,2048]{1,0:T(8,128)(2,1)S(1)}, u32[]{:S(2)}, u32[]{:S(2)}) collective-permute-start(bf16[32,2048]{1,0:T(8,128)(2,1)S(1)} %get-tuple-element.22), channel_id=1, source_target_pairs={{0,4},{4,0},{8,12},{12,8},{16,20},{20,16},{24,28},{28,24},{32,36},... | collective-permute-start | bytes 393224 | tf_op jit(solution)/shard_map/ppermute | solution.py:388
  6.8 0.0 collective-permute-start.2
  6.8 1.2 %collective-permute-done.2.outer_more_ref = bf16[8,2048]{1,0:T(8,128)(2,1)S(1)} collective-permute-done((bf16[8,2048]{1,0:T(8,128)(2,1)S(1)}, bf16[8,2048]{1,0:T(8,128)(2,1)S(1)}, u32[]{:S(2)}, u32[]{:S(2)}) %collective-permute-start.2) | collective-permute-done | bytes 32800 | tf_op jit(solution)/shard_map/ppermute | solution.py:389
  8.0 0.0 collective-permute-done.1.inner_ref
  8.0 0.0 copy-done.5
  8.0 0.0 copy-done.6
  8.1 1.2 %merge.1 = (bf16[128,2048]{1,0:T(8,128)(2,1)}, f32[16,2048]{1,0:T(8,128)S(1)}) custom-call(bf16[8,2048]{1,0:T(8,128)(2,1)S(1)} %get-tuple-element.18.heads_ref, bf16[8,2048]{1,0:T(8,128)(2,1)S(1)} %get-tuple-element.19.tails_ref, bf16[32,2048]{1,0:T(8,128)(2,1)S(1)} %collective-permute-done.1.inner_ref, bf16[8,2048]{1,0:T(8,128)(2,1)S(1)} %collective-permute-done.outer_ref, ...), custom_call_target="tpu_custom_call" | custom-call | tf_op jit(solution)/shard_map/merge/pallas_call | solution.py:391
  9.3 10.2 %all-to-all-start = ((bf16[16,8,2048]{2,1,0:T(8,128)(2,1)}), bf16[16,8,2048]{2,1,0:T(8,128)(2,1)S(1)}, u32[]{:S(2)}, u32[]{:S(2)}) async-start(bf16[16,8,2048]{2,1,0:T(8,128)(2,1)} %bitcast.6), calls=%async_computation | async-start | bytes 1048576 | tf_op jit(solution)/shard_map/all_to_all | solution.py:405
  19.5 0.0 copy-start.3
  19.5 0.0 copy-start.4
  19.5 5.2 %local.1 = (bf16[128,2048]{1,0:T(8,128)(2,1)S(1)}, bf16[128,2048]{1,0:T(8,128)(2,1)S(1)}, f32[128,2048]{1,0:T(8,128)S(1)}, f32[32,2048]{1,0:T(8,128)S(1)}) custom-call(f32[16,2048]{1,0:T(8,128)S(1)} %get-tuple-element.25.side_ref, bf16[128,2048]{1,0:T(8,128)(2,1)} %q_hbm.1, bf16[128,2048]{1,0:T(8,128)(2,1)} %k_hbm.1, bf16[128,2048]{1,0:T(8,128)(2,1)} %v_hbm.1, ...), custom_call_target="tpu_custom_call" | custom-call | flops 4294967296 | bytes 4194304 | tf_op jit(solution)/shard_map/local/pallas_call | solution.py:412
  24.8 1.7 %all-to-all-done = bf16[16,8,2048]{2,1,0:T(8,128)(2,1)S(1)} async-done(((bf16[16,8,2048]{2,1,0:T(8,128)(2,1)}), bf16[16,8,2048]{2,1,0:T(8,128)(2,1)S(1)}, u32[]{:S(2)}, u32[]{:S(2)}) %all-to-all-start) | async-done | bytes 524320 | tf_op jit(solution)/shard_map/all_to_all | solution.py:405
  26.5 0.0 copy-done.3
  26.5 0.0 copy-done.4
  26.5 1.3 %output.1 = bf16[128,2048]{1,0:T(8,128)(2,1)} custom-call(bf16[128,2048]{1,0:T(8,128)(2,1)S(1)} %get-tuple-element.26.feat_ref, bf16[128,2048]{1,0:T(8,128)(2,1)S(1)} %get-tuple-element.27.full_ref, f32[128,2048]{1,0:T(8,128)S(1)} %get-tuple-element.28.local_ref, f32[32,2048]{1,0:T(8,128)S(1)} %get-tuple-element.29.weight_ref, ...), custom_call_target="tpu_custom_call" | custom-call | tf_op jit(solution)/shard_map/output/pallas_call | solution.py:431
Async XLA Ops:
  0.0 1.9 %copy-start.1 = (bf16[128,2048]{1,0:T(8,128)(2,1)S(1)}, bf16[128,2048]{1,0:T(8,128)(2,1)}, u32[]{:S(2)}) copy-start(bf16[128,2048]{1,0:T(8,128)(2,1)} %v_hbm.1) | copy-start | bytes 1572868
  0.0 1.9 %copy-start = (bf16[128,2048]{1,0:T(8,128)(2,1)S(1)}, bf16[128,2048]{1,0:T(8,128)(2,1)}, u32[]{:S(2)}) copy-start(bf16[128,2048]{1,0:T(8,128)(2,1)} %k_hbm.1) | copy-start | bytes 1572868
  0.0 1.9 %copy-start.2 = (f32[3,3,2048]{2,1,0:T(4,128)S(1)}, f32[3,3,2048]{2,1,0:T(4,128)}, u32[]{:S(2)}) copy-start(f32[3,3,2048]{2,1,0:T(4,128)} %taps_hbm.1) | copy-start | bytes 221188
  1.2 0.7 %copy-start.7 = (bf16[8,256]{1,0:T(8,128)(2,1)S(1)}, bf16[8,256]{1,0:T(8,128)(2,1)}, u32[]{:S(2)}) copy-start(bf16[8,256]{1,0:T(8,128)(2,1)} %constant.18.clone.moment_ref) | copy-start | bytes 12292
  1.2 1.8 %collective-permute-start = (bf16[8,2048]{1,0:T(8,128)(2,1)S(1)}, bf16[8,2048]{1,0:T(8,128)(2,1)S(1)}, u32[]{:S(2)}, u32[]{:S(2)}) collective-permute-start(bf16[8,2048]{1,0:T(8,128)(2,1)S(1)} %get-tuple-element.21), channel_id=1, source_target_pairs={{4,8},{12,16},{20,24},{28,32},{36,40},{44,48},{52,56},{60,64},{68,... | collective-permute-start | bytes 98312 | tf_op jit(solution)/shard_map/ppermute | solution.py:374
  1.9 6.1 %copy-start.5 = (bf16[32,64]{1,0:T(8,128)(2,1)S(1)}, bf16[32,64]{1,0:T(8,128)(2,1)}, u32[]{:S(2)}) copy-start(bf16[32,64]{1,0:T(8,128)(2,1)} %constant.20.clone.widen_ref) | copy-start | bytes 12292
  1.9 6.1 %copy-start.6 = (f32[16,128]{1,0:T(8,128)S(1)}, f32[16,128]{1,0:T(8,128)}, u32[]{:S(2)}) copy-start(f32[16,128]{1,0:T(8,128)} %constant.19.clone.first_ref) | copy-start | bytes 24580
  3.0 5.1 %collective-permute-start.1 = (bf16[32,2048]{1,0:T(8,128)(2,1)S(1)}, bf16[32,2048]{1,0:T(8,128)(2,1)S(1)}, u32[]{:S(2)}, u32[]{:S(2)}) collective-permute-start(bf16[32,2048]{1,0:T(8,128)(2,1)S(1)} %get-tuple-element.22), channel_id=1, source_target_pairs={{0,4},{4,0},{8,12},{12,8},{16,20},{20,16},{24,28},{28,24},{32,36},... | collective-permute-start | bytes 393224 | tf_op jit(solution)/shard_map/ppermute | solution.py:388
  6.8 1.2 %collective-permute-start.2 = (bf16[8,2048]{1,0:T(8,128)(2,1)S(1)}, bf16[8,2048]{1,0:T(8,128)(2,1)S(1)}, u32[]{:S(2)}, u32[]{:S(2)}) collective-permute-start(bf16[8,2048]{1,0:T(8,128)(2,1)S(1)} %collective-permute-done.outer_ref), channel_id=1, source_target_pairs={{0,4},{4,0},{8,12},{12,8},{16,20},{20,16},{24,28},{28,24},{32,36},... | collective-permute-start | bytes 98312 | tf_op jit(solution)/shard_map/ppermute | solution.py:389
  9.3 17.2 %all-to-all-start = ((bf16[16,8,2048]{2,1,0:T(8,128)(2,1)}), bf16[16,8,2048]{2,1,0:T(8,128)(2,1)S(1)}, u32[]{:S(2)}, u32[]{:S(2)}) async-start(bf16[16,8,2048]{2,1,0:T(8,128)(2,1)} %bitcast.6), calls=%async_computation | async-start | bytes 1048576 | tf_op jit(solution)/shard_map/all_to_all | solution.py:405
  19.5 7.0 %copy-start.3 = (bf16[1536,128]{1,0:T(8,128)(2,1)S(1)}, bf16[1536,128]{1,0:T(8,128)(2,1)}, u32[]{:S(2)}) copy-start(bf16[1536,128]{1,0:T(8,128)(2,1)} %constant.22.clone.carry_ref) | copy-start | bytes 1179652
  19.5 7.0 %copy-start.4 = (bf16[256,240]{1,0:T(8,128)(2,1)S(1)}, bf16[256,240]{1,0:T(8,128)(2,1)}, u32[]{:S(2)}) copy-start(bf16[256,240]{1,0:T(8,128)(2,1)} %constant.23.clone.spread_hbm.spread_ref) | copy-start | bytes 368644

commit v6 on v5

--- a/solution.py
+++ b/solution.py
@@ -161,7 +161,7 @@
         product = jnp.where(row < 2, 0.0, key_feat * value_feat).astype(BF16)
         near = dot(moment_ref[...], jnp.concatenate([product, product], 0))
         near_ref[:, cols] = near
-        rows = [tails_ref[:, cols].astype(F32), heads_ref[:, cols].astype(F32), zeros(8, width)]
+        rows = [ref[:, cols].astype(F32)[0:4] for ref in (tails_ref, heads_ref)]
         inner_ref[:, cols] = jnp.concatenate([near] + rows, 0).astype(BF16)
 
 
@@ -177,15 +177,15 @@
     return rounded(key[0] * value[0]), rounded(key[1] * value[1])
 
 
-def merge_kernel(heads_ref, tails_ref, inner_ref, outer_ref, outer_more_ref, near_ref, taps_ref, first_ref, widen_ref,
-                 sent_ref, side_ref, held, sems):
+def merge_kernel(heads_ref, tails_ref, tails_other_ref, inner_ref, outer_ref, outer_more_ref, near_ref, taps_ref,
+                 first_ref, widen_ref, sent_ref, side_ref, held, sems):
     place = lax.axis_index("ctx")
     lower = lax.rem(place, 2) == 0
     chip = lax.div(place, 2)
     opens, closes = lax.rem(chip, ROW) == 0, lax.rem(chip + 1, ROW) == 0
     heads, tails, inner = heads_ref[...].astype(F32)[0:4], tails_ref[...].astype(F32)[0:4], inner_ref[...].astype(F32)
     outer, outer_more = outer_ref[...].astype(F32), outer_more_ref[...].astype(F32)
-    tails_other, heads_other = inner[8:12], inner[16:20]
+    tails_other, heads_other = inner[8:12], inner[12:16]
     heads0, heads1 = jnp.where(lower, heads, heads_other), jnp.where(lower, heads_other, heads)
     tails0, tails1 = jnp.where(lower, tails, tails_other), jnp.where(lower, tails_other, tails)
     outer0, outer1 = jnp.where(lower, outer, outer_more), jnp.where(lower, outer_more, outer)
@@ -208,7 +208,7 @@
     ]
     for copy in copies:
         copy.start()
-    rows = [jnp.where(lower, a0, b0), jnp.where(lower, a1, b1), jnp.where(lower, outer[4:6], inner[12:14])]
+    rows = [jnp.where(lower, a0, b0), jnp.where(lower, a1, b1), jnp.where(lower, outer[4:6], tails_other_ref[...].astype(F32)[4:6])]
     rows += [zeros(4, a0.shape[1]), jnp.where(lower, 0.0, near0)]
     side_ref[...] = jnp.concatenate(rows, 0)
     for copy in copies:
@@ -377,20 +377,20 @@
         functools.partial(moment_kernel, width=width),
         in_specs=[vmem, vmem] + [vmem] * 4,
         out_specs=[vmem, vmem],
-        out_shape=[pltpu.VMEM((RANK, channels), F32), pltpu.VMEM((4 * RANK, channels), BF16)],
+        out_shape=[pltpu.VMEM((RANK, channels), F32), pltpu.VMEM((2 * RANK, channels), BF16)],
         compiler_params=params,
         cost_estimate=pl.CostEstimate(
             flops=1, bytes_accessed=1, transcendentals=0
         ),
         name="moments",
     )(heads, tails, key_plain, value_plain, short_filter, moment)
-    inner, outer = lax.optimization_barrier((inner, outer))
     inner = lax.ppermute(inner, "ctx", swap)
     outer_more = lax.ppermute(outer, "ctx", swap)
+    tails_other = lax.ppermute(tails, "ctx", swap)
 
     sent, side = pl.pallas_call(
         merge_kernel,
-        in_specs=[vmem] * 9,
+        in_specs=[vmem] * 10,
         out_specs=[hbm, vmem],
         out_shape=[
             pltpu.HBM((devices // 2 * RANK, channels), BF16),
@@ -399,7 +399,7 @@
         scratch_shapes=[pltpu.VMEM((16, channels), BF16), pltpu.SemaphoreType.DMA((devices // 2 * RANK // 16,))],
         compiler_params=params,
         name="merge",
-    )(heads, tails, inner, outer, outer_more, near_sums, short_filter, first, widen)
+    )(heads, tails, tails_other, inner, outer, outer_more, near_sums, short_filter, first, widen)
 
     groups = [[2 * chip + core for chip in chip_order(devices // 2)] for core in range(2)]
     got = lax.all_to_all(sent, "ctx", 0, 0, axis_index_groups=groups, tiled=True)

time: 28 us -> 27.7 us (0.989)
  waiting for transfers between devices: 2.95 us -> 2.46 us
    ppermute x1, waiting for transfers between devices: 1.2 us -> 0.17 us  [on_device(): outer_more = lax.ppermute(outer, 'ctx', swap)]
    ppermute x0 -> x1, waiting for transfers between devices: none -> 0.69 us  [on_device(): tails_other = lax.ppermute(tails, 'ctx', swap)]
    ppermute x1, starting transfers between devices: 3.85 us -> 3.37 us  [on_device(): inner = lax.ppermute(inner, 'ctx', swap)]
    ppermute x1, starting transfers between devices: 0.01 us -> 0.44 us  [on_device(): outer_more = lax.ppermute(outer, 'ctx', swap)]
  transfers between devices with their start and end apart: 4 -> 5, of which waited for: 2 -> 3; matrix products, arithmetic and copies ran while one was open for 0% -> 0% of each run, Pallas kernels for 23% -> 23%
where the time goes in v6:
time: 27.7 us; the launch traced here: 27.4 us
  starting transfers between devices  14.9 us (54%)
  Pallas kernels  9.97 us (36%)
  waiting for transfers between devices  2.46 us (9%)
    all_to_all x1, starting transfers between devices, on_device(): lax.all_to_all(sent, 'ctx', 0, 0, axis_index_groups=groups, tiled=True)  10.3 us
    pallas_call x1, Pallas kernels, on_device(): pl.pallas_call(local_kernel, in_specs=[vmem] + [hbm] * len(local_args), o...  5.25 us
    ppermute x1, starting transfers between devices, on_device(): inner = lax.ppermute(inner, 'ctx', swap)  3.37 us
    all_to_all x1, waiting for transfers between devices, on_device(): lax.all_to_all(sent, 'ctx', 0, 0, axis_index_groups=groups, tiled=True)  1.59 us
    pallas_call x1, Pallas kernels, on_device(): pl.pallas_call(out_kernel, in_specs=[vmem] * 7, out_specs=hbm, out_shape=...  1.27 us
    pallas_call x1, Pallas kernels, on_device(): pl.pallas_call(merge_kernel, in_specs=[vmem] * 10, out_specs=[hbm, vmem],...  1.24 us
    pallas_call x1, Pallas kernels, on_device(): pl.pallas_call(edge_kernel, in_specs=[hbm, hbm, hbm], out_specs=[vmem] *...  1.18 us
    pallas_call x1, Pallas kernels, on_device(): pl.pallas_call(functools.partial(moment_kernel, width=width), in_specs=[v...  1.03 us
  transfers between devices with their start and end apart: 5, of which 3 were waited for; matrix products, arithmetic and copies ran while one was open for 0% of the time, Pallas kernels for 23%

profile of v6, /device:TPU:0, one launch (start us, length us, event | category | flops | bytes accessed | tf_op | source)
XLA Modules:
  0.0 27.4 jit_solution(2064006530737354502)
XLA Ops:
  0.0 0.0 copy-start.1
  0.0 0.0 copy-start
  0.0 0.0 copy-start.2
  0.0 1.2 %edges.1 = (bf16[8,2048]{1,0:T(8,128)(2,1)S(1)}, bf16[8,2048]{1,0:T(8,128)(2,1)S(1)}, bf16[8,2048]{1,0:T(8,128)(2,1)S(1)}) custom-call(bf16[128,2048]{1,0:T(8,128)(2,1)} %q_hbm.1, bf16[128,2048]{1,0:T(8,128)(2,1)} %k_hbm.1, bf16[128,2048]{1,0:T(8,128)(2,1)} %v_hbm.1), custom_call_target="tpu_custom_call" | custom-call | tf_op jit(solution)/shard_map/edges/pallas_call | solution.py:363
  1.2 0.0 copy-start.7
  1.2 0.7 %collective-permute-start.2 = (bf16[8,2048]{1,0:T(8,128)(2,1)S(1)}, bf16[8,2048]{1,0:T(8,128)(2,1)S(1)}, u32[]{:S(2)}, u32[]{:S(2)}) collective-permute-start(bf16[8,2048]{1,0:T(8,128)(2,1)S(1)} %get-tuple-element.19), channel_id=1, source_target_pairs={{4,8},{12,16},{20,24},{28,32},{36,40},{44,48},{52,56},{60,64},{68,... | collective-permute-start | bytes 98312 | tf_op jit(solution)/shard_map/ppermute | solution.py:374
  1.9 0.0 copy-done.1
  1.9 0.0 copy-done
  1.9 0.0 copy-done.2
  1.9 0.0 copy-done.7
  1.9 0.0 copy-start.5
  1.9 0.0 copy-start.6
  1.9 1.0 %moments.1 = (f32[8,2048]{1,0:T(8,128)S(1)}, bf16[16,2048]{1,0:T(8,128)(2,1)S(1)}) custom-call(bf16[8,2048]{1,0:T(8,128)(2,1)S(1)} %get-tuple-element.16.heads_ref, bf16[8,2048]{1,0:T(8,128)(2,1)S(1)} %get-tuple-element.17.tails_ref, bf16[128,2048]{1,0:T(8,128)(2,1)S(1)} %copy-done, bf16[128,2048]{1,0:T(8,128)(2,1)S(1)} %copy-done.1, ...), custom_call_target="tpu_custom_call" | custom-call | flops 1 | bytes 1 | tf_op jit(solution)/shard_map/moments/pallas_call | solution.py:376
  3.0 3.4 %collective-permute-start.1 = (bf16[16,2048]{1,0:T(8,128)(2,1)S(1)}, bf16[16,2048]{1,0:T(8,128)(2,1)S(1)}, u32[]{:S(2)}, u32[]{:S(2)}) collective-permute-start(bf16[16,2048]{1,0:T(8,128)(2,1)S(1)} %get-tuple-element.18), channel_id=1, source_target_pairs={{0,4},{4,0},{8,12},{12,8},{16,20},{20,16},{24,28},{28,24},{32,36},... | collective-permute-start | bytes 196616 | tf_op jit(solution)/shard_map/ppermute | solution.py:387
  6.4 0.1 collective-permute-start
  6.4 0.0 collective-permute-done.2.outer_ref
  6.4 0.4 %collective-permute-start.3 = (bf16[8,2048]{1,0:T(8,128)(2,1)S(1)}, bf16[8,2048]{1,0:T(8,128)(2,1)S(1)}, u32[]{:S(2)}, u32[]{:S(2)}) collective-permute-start(bf16[8,2048]{1,0:T(8,128)(2,1)S(1)} %collective-permute-done.2.outer_ref), channel_id=1, source_target_pairs={{0,4},{4,0},{8,12},{12,8},{16,20},{20,16},{24,28},{28,24},{32,36},... | collective-permute-start | bytes 98312 | tf_op jit(solution)/shard_map/ppermute | solution.py:388
  6.9 0.7 %collective-permute-done.tails_other_ref = bf16[8,2048]{1,0:T(8,128)(2,1)S(1)} collective-permute-done((bf16[8,2048]{1,0:T(8,128)(2,1)S(1)}, bf16[8,2048]{1,0:T(8,128)(2,1)S(1)}, u32[]{:S(2)}, u32[]{:S(2)}) %collective-permute-start) | collective-permute-done | bytes 32800 | tf_op jit(solution)/shard_map/ppermute | solution.py:389
  7.6 0.2 collective-permute-done.3.outer_more_ref
  7.7 0.0 collective-permute-done.1.inner_ref
  7.7 0.0 copy-done.5
  7.7 0.0 copy-done.6
  7.7 1.2 %merge.1 = (bf16[128,2048]{1,0:T(8,128)(2,1)}, f32[16,2048]{1,0:T(8,128)S(1)}) custom-call(bf16[8,2048]{1,0:T(8,128)(2,1)S(1)} %get-tuple-element.16.heads_ref, bf16[8,2048]{1,0:T(8,128)(2,1)S(1)} %get-tuple-element.17.tails_ref, bf16[8,2048]{1,0:T(8,128)(2,1)S(1)} %collective-permute-done.tails_other_ref, ...), custom_call_target="tpu_custom_call" | custom-call | tf_op jit(solution)/shard_map/merge/pallas_call | solution.py:391
  9.0 10.3 %all-to-all-start = ((bf16[16,8,2048]{2,1,0:T(8,128)(2,1)}), bf16[16,8,2048]{2,1,0:T(8,128)(2,1)S(1)}, u32[]{:S(2)}, u32[]{:S(2)}) async-start(bf16[16,8,2048]{2,1,0:T(8,128)(2,1)} %bitcast.6), calls=%async_computation | async-start | bytes 1048576 | tf_op jit(solution)/shard_map/all_to_all | solution.py:405
  19.3 0.0 copy-start.3
  19.3 0.0 copy-start.4
  19.3 5.2 %local.1 = (bf16[128,2048]{1,0:T(8,128)(2,1)S(1)}, bf16[128,2048]{1,0:T(8,128)(2,1)S(1)}, f32[128,2048]{1,0:T(8,128)S(1)}, f32[32,2048]{1,0:T(8,128)S(1)}) custom-call(f32[16,2048]{1,0:T(8,128)S(1)} %get-tuple-element.21.side_ref, bf16[128,2048]{1,0:T(8,128)(2,1)} %q_hbm.1, bf16[128,2048]{1,0:T(8,128)(2,1)} %k_hbm.1, bf16[128,2048]{1,0:T(8,128)(2,1)} %v_hbm.1, ...), custom_call_target="tpu_custom_call" | custom-call | flops 4294967296 | bytes 4194304 | tf_op jit(solution)/shard_map/local/pallas_call | solution.py:412
  24.6 1.6 %all-to-all-done = bf16[16,8,2048]{2,1,0:T(8,128)(2,1)S(1)} async-done(((bf16[16,8,2048]{2,1,0:T(8,128)(2,1)}), bf16[16,8,2048]{2,1,0:T(8,128)(2,1)S(1)}, u32[]{:S(2)}, u32[]{:S(2)}) %all-to-all-start) | async-done | bytes 524320 | tf_op jit(solution)/shard_map/all_to_all | solution.py:405
  26.2 0.0 copy-done.3
  26.2 0.0 copy-done.4
  26.2 1.3 %output.1 = bf16[128,2048]{1,0:T(8,128)(2,1)} custom-call(bf16[128,2048]{1,0:T(8,128)(2,1)S(1)} %get-tuple-element.22.feat_ref, bf16[128,2048]{1,0:T(8,128)(2,1)S(1)} %get-tuple-element.23.full_ref, f32[128,2048]{1,0:T(8,128)S(1)} %get-tuple-element.24.local_ref, f32[32,2048]{1,0:T(8,128)S(1)} %get-tuple-element.25.weight_ref, ...), custom_call_target="tpu_custom_call" | custom-call | tf_op jit(solution)/shard_map/output/pallas_call | solution.py:431
Async XLA Ops:
  0.0 1.9 %copy-start.1 = (bf16[128,2048]{1,0:T(8,128)(2,1)S(1)}, bf16[128,2048]{1,0:T(8,128)(2,1)}, u32[]{:S(2)}) copy-start(bf16[128,2048]{1,0:T(8,128)(2,1)} %v_hbm.1) | copy-start | bytes 1572868
  0.0 1.9 %copy-start = (bf16[128,2048]{1,0:T(8,128)(2,1)S(1)}, bf16[128,2048]{1,0:T(8,128)(2,1)}, u32[]{:S(2)}) copy-start(bf16[128,2048]{1,0:T(8,128)(2,1)} %k_hbm.1) | copy-start | bytes 1572868
  0.0 1.9 %copy-start.2 = (f32[3,3,2048]{2,1,0:T(4,128)S(1)}, f32[3,3,2048]{2,1,0:T(4,128)}, u32[]{:S(2)}) copy-start(f32[3,3,2048]{2,1,0:T(4,128)} %taps_hbm.1) | copy-start | bytes 221188
  1.2 0.7 %copy-start.7 = (bf16[8,256]{1,0:T(8,128)(2,1)S(1)}, bf16[8,256]{1,0:T(8,128)(2,1)}, u32[]{:S(2)}) copy-start(bf16[8,256]{1,0:T(8,128)(2,1)} %constant.18.clone.moment_ref) | copy-start | bytes 12292
  1.2 5.2 %collective-permute-start.2 = (bf16[8,2048]{1,0:T(8,128)(2,1)S(1)}, bf16[8,2048]{1,0:T(8,128)(2,1)S(1)}, u32[]{:S(2)}, u32[]{:S(2)}) collective-permute-start(bf16[8,2048]{1,0:T(8,128)(2,1)S(1)} %get-tuple-element.19), channel_id=1, source_target_pairs={{4,8},{12,16},{20,24},{28,32},{36,40},{44,48},{52,56},{60,64},{68,... | collective-permute-start | bytes 98312 | tf_op jit(solution)/shard_map/ppermute | solution.py:374
  1.9 5.8 %copy-start.5 = (bf16[32,64]{1,0:T(8,128)(2,1)S(1)}, bf16[32,64]{1,0:T(8,128)(2,1)}, u32[]{:S(2)}) copy-start(bf16[32,64]{1,0:T(8,128)(2,1)} %constant.20.clone.widen_ref) | copy-start | bytes 12292
  1.9 5.8 %copy-start.6 = (f32[16,128]{1,0:T(8,128)S(1)}, f32[16,128]{1,0:T(8,128)}, u32[]{:S(2)}) copy-start(f32[16,128]{1,0:T(8,128)} %constant.19.clone.first_ref) | copy-start | bytes 24580
  3.0 4.8 %collective-permute-start.1 = (bf16[16,2048]{1,0:T(8,128)(2,1)S(1)}, bf16[16,2048]{1,0:T(8,128)(2,1)S(1)}, u32[]{:S(2)}, u32[]{:S(2)}) collective-permute-start(bf16[16,2048]{1,0:T(8,128)(2,1)S(1)} %get-tuple-element.18), channel_id=1, source_target_pairs={{0,4},{4,0},{8,12},{12,8},{16,20},{20,16},{24,28},{28,24},{32,36},... | collective-permute-start | bytes 196616 | tf_op jit(solution)/shard_map/ppermute | solution.py:387
  6.4 1.2 %collective-permute-start = (bf16[8,2048]{1,0:T(8,128)(2,1)S(1)}, bf16[8,2048]{1,0:T(8,128)(2,1)S(1)}, u32[]{:S(2)}, u32[]{:S(2)}) collective-permute-start(bf16[8,2048]{1,0:T(8,128)(2,1)S(1)} %get-tuple-element.17.tails_ref), channel_id=1, source_target_pairs={{0,4},{4,0},{8,12},{12,8},{16,20},{20,16},{24,28},{28,24},{32,36},... | collective-permute-start | bytes 98312 | tf_op jit(solution)/shard_map/ppermute | solution.py:389
  6.4 1.3 %collective-permute-start.3 = (bf16[8,2048]{1,0:T(8,128)(2,1)S(1)}, bf16[8,2048]{1,0:T(8,128)(2,1)S(1)}, u32[]{:S(2)}, u32[]{:S(2)}) collective-permute-start(bf16[8,2048]{1,0:T(8,128)(2,1)S(1)} %collective-permute-done.2.outer_ref), channel_id=1, source_target_pairs={{0,4},{4,0},{8,12},{12,8},{16,20},{20,16},{24,28},{28,24},{32,36},... | collective-permute-start | bytes 98312 | tf_op jit(solution)/shard_map/ppermute | solution.py:388
  9.0 17.2 %all-to-all-start = ((bf16[16,8,2048]{2,1,0:T(8,128)(2,1)}), bf16[16,8,2048]{2,1,0:T(8,128)(2,1)S(1)}, u32[]{:S(2)}, u32[]{:S(2)}) async-start(bf16[16,8,2048]{2,1,0:T(8,128)(2,1)} %bitcast.6), calls=%async_computation | async-start | bytes 1048576 | tf_op jit(solution)/shard_map/all_to_all | solution.py:405
  19.3 6.9 %copy-start.3 = (bf16[1536,128]{1,0:T(8,128)(2,1)S(1)}, bf16[1536,128]{1,0:T(8,128)(2,1)}, u32[]{:S(2)}) copy-start(bf16[1536,128]{1,0:T(8,128)(2,1)} %constant.22.clone.carry_ref) | copy-start | bytes 1179652
  19.3 6.9 %copy-start.4 = (bf16[256,240]{1,0:T(8,128)(2,1)S(1)}, bf16[256,240]{1,0:T(8,128)(2,1)}, u32[]{:S(2)}) copy-start(bf16[256,240]{1,0:T(8,128)(2,1)} %constant.23.clone.spread_hbm.spread_ref) | copy-start | bytes 368644

commit v7 on v6

--- a/solution.py
+++ b/solution.py
@@ -126,17 +126,19 @@
 
 def edge_kernel(q_ref, k_ref, v_ref, heads_ref, tails_ref, outer_ref, held, sems):
     block, columns = q_ref.shape
-    copies = []
-    for idx, ref in enumerate((k_ref, v_ref, q_ref)):
-        copies.append(pltpu.make_async_copy(ref.at[pl.ds(0, 16)], held.at[idx], sems.at[idx]))
-        copies.append(pltpu.make_async_copy(ref.at[pl.ds(block - 16, 16)], held.at[idx + 3], sems.at[idx + 3]))
+    copies = [
+        pltpu.make_async_copy(ref.at[pl.ds(start, 16)], held.at[idx], sems.at[idx])
+        for idx, (ref, start) in enumerate(
+            ((k_ref, 0), (v_ref, 0), (k_ref, block - 16), (v_ref, block - 16), (q_ref, block - 16))
+        )
+    ]
     for copy in copies:
         copy.start()
     for copy in copies:
         copy.wait()
-    heads = [held[idx].astype(F32)[0:2] for idx in range(3)]
-    tails = [held[idx + 3].astype(F32)[14:16] for idx in range(3)]
-    heads = jnp.concatenate(heads + [zeros(2, columns)], 0)
+    heads = [held[idx].astype(F32)[0:2] for idx in range(2)]
+    tails = [held[idx].astype(F32)[14:16] for idx in range(2, 5)]
+    heads = jnp.concatenate(heads + [zeros(4, columns)], 0)
     tails = jnp.concatenate(tails + [zeros(2, columns)], 0)
     heads_ref[...] = heads.astype(BF16)
     tails_ref[...] = tails.astype(BF16)
@@ -365,7 +367,7 @@
         in_specs=[hbm, hbm, hbm],
         out_specs=[vmem] * 3,
         out_shape=[pltpu.VMEM((8, channels), BF16)] * 3,
-        scratch_shapes=[pltpu.VMEM((6, 16, channels), BF16), pltpu.SemaphoreType.DMA((6,))],
+        scratch_shapes=[pltpu.VMEM((5, 16, channels), BF16), pltpu.SemaphoreType.DMA((5,))],
         compiler_params=params,
         name="edges",
     )(query_proj, key_proj, value_proj)

time: 27.7 us -> 27.7 us (level)
  no operation moved by 1% of the time
where the time goes in v7:
time: 27.7 us; the launch traced here: 27.4 us
  starting transfers between devices  14.9 us (54%)
  Pallas kernels  9.92 us (36%)
  waiting for transfers between devices  2.46 us (9%)
    all_to_all x1, starting transfers between devices, on_device(): lax.all_to_all(sent, 'ctx', 0, 0, axis_index_groups=groups, tiled=True)  10.3 us
    pallas_call x1, Pallas kernels, on_device(): pl.pallas_call(local_kernel, in_specs=[vmem] + [hbm] * len(local_args), o...  5.24 us
    ppermute x1, starting transfers between devices, on_device(): inner = lax.ppermute(inner, 'ctx', swap)  3.37 us
    all_to_all x1, waiting for transfers between devices, on_device(): lax.all_to_all(sent, 'ctx', 0, 0, axis_index_groups=groups, tiled=True)  1.6 us
    pallas_call x1, Pallas kernels, on_device(): pl.pallas_call(out_kernel, in_specs=[vmem] * 7, out_specs=hbm, out_shape=...  1.27 us
    pallas_call x1, Pallas kernels, on_device(): pl.pallas_call(merge_kernel, in_specs=[vmem] * 10, out_specs=[hbm, vmem],...  1.24 us
    pallas_call x1, Pallas kernels, on_device(): pl.pallas_call(edge_kernel, in_specs=[hbm, hbm, hbm], out_specs=[vmem] *...  1.14 us
    pallas_call x1, Pallas kernels, on_device(): pl.pallas_call(functools.partial(moment_kernel, width=width), in_specs=[v...  1.03 us
  transfers between devices with their start and end apart: 5, of which 3 were waited for; matrix products, arithmetic and copies ran while one was open for 0% of the time, Pallas kernels for 23%

profile of v7, /device:TPU:0, one launch (start us, length us, event | category | flops | bytes accessed | tf_op | source)
XLA Modules:
  0.0 27.4 jit_solution(127116256014592144)
XLA Ops:
  0.0 0.0 copy-start.1
  0.0 0.0 copy-start
  0.0 0.0 copy-start.2
  0.0 1.1 %edges.1 = (bf16[8,2048]{1,0:T(8,128)(2,1)S(1)}, bf16[8,2048]{1,0:T(8,128)(2,1)S(1)}, bf16[8,2048]{1,0:T(8,128)(2,1)S(1)}) custom-call(bf16[128,2048]{1,0:T(8,128)(2,1)} %q_hbm.1, bf16[128,2048]{1,0:T(8,128)(2,1)} %k_hbm.1, bf16[128,2048]{1,0:T(8,128)(2,1)} %v_hbm.1), custom_call_target="tpu_custom_call" | custom-call | tf_op jit(solution)/shard_map/edges/pallas_call | solution.py:365
  1.2 0.0 copy-start.7
  1.2 0.7 %collective-permute-start.2 = (bf16[8,2048]{1,0:T(8,128)(2,1)S(1)}, bf16[8,2048]{1,0:T(8,128)(2,1)S(1)}, u32[]{:S(2)}, u32[]{:S(2)}) collective-permute-start(bf16[8,2048]{1,0:T(8,128)(2,1)S(1)} %get-tuple-element.19), channel_id=1, source_target_pairs={{4,8},{12,16},{20,24},{28,32},{36,40},{44,48},{52,56},{60,64},{68,... | collective-permute-start | bytes 98312 | tf_op jit(solution)/shard_map/ppermute | solution.py:376
  1.8 0.0 copy-done.1
  1.8 0.0 copy-done
  1.9 0.0 copy-done.2
  1.9 0.0 copy-done.7
  1.9 0.0 copy-start.5
  1.9 0.0 copy-start.6
  1.9 1.0 %moments.1 = (f32[8,2048]{1,0:T(8,128)S(1)}, bf16[16,2048]{1,0:T(8,128)(2,1)S(1)}) custom-call(bf16[8,2048]{1,0:T(8,128)(2,1)S(1)} %get-tuple-element.16.heads_ref, bf16[8,2048]{1,0:T(8,128)(2,1)S(1)} %get-tuple-element.17.tails_ref, bf16[128,2048]{1,0:T(8,128)(2,1)S(1)} %copy-done, bf16[128,2048]{1,0:T(8,128)(2,1)S(1)} %copy-done.1, ...), custom_call_target="tpu_custom_call" | custom-call | flops 1 | bytes 1 | tf_op jit(solution)/shard_map/moments/pallas_call | solution.py:378
  2.9 3.4 %collective-permute-start.1 = (bf16[16,2048]{1,0:T(8,128)(2,1)S(1)}, bf16[16,2048]{1,0:T(8,128)(2,1)S(1)}, u32[]{:S(2)}, u32[]{:S(2)}) collective-permute-start(bf16[16,2048]{1,0:T(8,128)(2,1)S(1)} %get-tuple-element.18), channel_id=1, source_target_pairs={{0,4},{4,0},{8,12},{12,8},{16,20},{20,16},{24,28},{28,24},{32,36},... | collective-permute-start | bytes 196616 | tf_op jit(solution)/shard_map/ppermute | solution.py:389
  6.3 0.1 collective-permute-start
  6.4 0.0 collective-permute-done.2.outer_ref
  6.4 0.4 %collective-permute-start.3 = (bf16[8,2048]{1,0:T(8,128)(2,1)S(1)}, bf16[8,2048]{1,0:T(8,128)(2,1)S(1)}, u32[]{:S(2)}, u32[]{:S(2)}) collective-permute-start(bf16[8,2048]{1,0:T(8,128)(2,1)S(1)} %collective-permute-done.2.outer_ref), channel_id=1, source_target_pairs={{0,4},{4,0},{8,12},{12,8},{16,20},{20,16},{24,28},{28,24},{32,36},... | collective-permute-start | bytes 98312 | tf_op jit(solution)/shard_map/ppermute | solution.py:390
  6.8 0.7 %collective-permute-done.tails_other_ref = bf16[8,2048]{1,0:T(8,128)(2,1)S(1)} collective-permute-done((bf16[8,2048]{1,0:T(8,128)(2,1)S(1)}, bf16[8,2048]{1,0:T(8,128)(2,1)S(1)}, u32[]{:S(2)}, u32[]{:S(2)}) %collective-permute-start) | collective-permute-done | bytes 32800 | tf_op jit(solution)/shard_map/ppermute | solution.py:391
  7.5 0.2 collective-permute-done.3.outer_more_ref
  7.7 0.0 collective-permute-done.1.inner_ref
  7.7 0.0 copy-done.5
  7.7 0.0 copy-done.6
  7.7 1.2 %merge.1 = (bf16[128,2048]{1,0:T(8,128)(2,1)}, f32[16,2048]{1,0:T(8,128)S(1)}) custom-call(bf16[8,2048]{1,0:T(8,128)(2,1)S(1)} %get-tuple-element.16.heads_ref, bf16[8,2048]{1,0:T(8,128)(2,1)S(1)} %get-tuple-element.17.tails_ref, bf16[8,2048]{1,0:T(8,128)(2,1)S(1)} %collective-permute-done.tails_other_ref, ...), custom_call_target="tpu_custom_call" | custom-call | tf_op jit(solution)/shard_map/merge/pallas_call | solution.py:393
  8.9 10.3 %all-to-all-start = ((bf16[16,8,2048]{2,1,0:T(8,128)(2,1)}), bf16[16,8,2048]{2,1,0:T(8,128)(2,1)S(1)}, u32[]{:S(2)}, u32[]{:S(2)}) async-start(bf16[16,8,2048]{2,1,0:T(8,128)(2,1)} %bitcast.6), calls=%async_computation | async-start | bytes 1048576 | tf_op jit(solution)/shard_map/all_to_all | solution.py:407
  19.3 0.0 copy-start.3
  19.3 0.0 copy-start.4
  19.3 5.2 %local.1 = (bf16[128,2048]{1,0:T(8,128)(2,1)S(1)}, bf16[128,2048]{1,0:T(8,128)(2,1)S(1)}, f32[128,2048]{1,0:T(8,128)S(1)}, f32[32,2048]{1,0:T(8,128)S(1)}) custom-call(f32[16,2048]{1,0:T(8,128)S(1)} %get-tuple-element.21.side_ref, bf16[128,2048]{1,0:T(8,128)(2,1)} %q_hbm.1, bf16[128,2048]{1,0:T(8,128)(2,1)} %k_hbm.1, bf16[128,2048]{1,0:T(8,128)(2,1)} %v_hbm.1, ...), custom_call_target="tpu_custom_call" | custom-call | flops 4294967296 | bytes 4194304 | tf_op jit(solution)/shard_map/local/pallas_call | solution.py:414
  24.5 1.6 %all-to-all-done = bf16[16,8,2048]{2,1,0:T(8,128)(2,1)S(1)} async-done(((bf16[16,8,2048]{2,1,0:T(8,128)(2,1)}), bf16[16,8,2048]{2,1,0:T(8,128)(2,1)S(1)}, u32[]{:S(2)}, u32[]{:S(2)}) %all-to-all-start) | async-done | bytes 524320 | tf_op jit(solution)/shard_map/all_to_all | solution.py:407
  26.1 0.0 copy-done.3
  26.1 0.0 copy-done.4
  26.1 1.3 %output.1 = bf16[128,2048]{1,0:T(8,128)(2,1)} custom-call(bf16[128,2048]{1,0:T(8,128)(2,1)S(1)} %get-tuple-element.22.feat_ref, bf16[128,2048]{1,0:T(8,128)(2,1)S(1)} %get-tuple-element.23.full_ref, f32[128,2048]{1,0:T(8,128)S(1)} %get-tuple-element.24.local_ref, f32[32,2048]{1,0:T(8,128)S(1)} %get-tuple-element.25.weight_ref, ...), custom_call_target="tpu_custom_call" | custom-call | tf_op jit(solution)/shard_map/output/pallas_call | solution.py:433
Async XLA Ops:
  0.0 1.8 %copy-start.1 = (bf16[128,2048]{1,0:T(8,128)(2,1)S(1)}, bf16[128,2048]{1,0:T(8,128)(2,1)}, u32[]{:S(2)}) copy-start(bf16[128,2048]{1,0:T(8,128)(2,1)} %v_hbm.1) | copy-start | bytes 1572868
  0.0 1.8 %copy-start = (bf16[128,2048]{1,0:T(8,128)(2,1)S(1)}, bf16[128,2048]{1,0:T(8,128)(2,1)}, u32[]{:S(2)}) copy-start(bf16[128,2048]{1,0:T(8,128)(2,1)} %k_hbm.1) | copy-start | bytes 1572868
  0.0 1.9 %copy-start.2 = (f32[3,3,2048]{2,1,0:T(4,128)S(1)}, f32[3,3,2048]{2,1,0:T(4,128)}, u32[]{:S(2)}) copy-start(f32[3,3,2048]{2,1,0:T(4,128)} %taps_hbm.1) | copy-start | bytes 221188
  1.2 0.7 %copy-start.7 = (bf16[8,256]{1,0:T(8,128)(2,1)S(1)}, bf16[8,256]{1,0:T(8,128)(2,1)}, u32[]{:S(2)}) copy-start(bf16[8,256]{1,0:T(8,128)(2,1)} %constant.18.clone.moment_ref) | copy-start | bytes 12292
  1.2 5.2 %collective-permute-start.2 = (bf16[8,2048]{1,0:T(8,128)(2,1)S(1)}, bf16[8,2048]{1,0:T(8,128)(2,1)S(1)}, u32[]{:S(2)}, u32[]{:S(2)}) collective-permute-start(bf16[8,2048]{1,0:T(8,128)(2,1)S(1)} %get-tuple-element.19), channel_id=1, source_target_pairs={{4,8},{12,16},{20,24},{28,32},{36,40},{44,48},{52,56},{60,64},{68,... | collective-permute-start | bytes 98312 | tf_op jit(solution)/shard_map/ppermute | solution.py:376
  1.9 5.8 %copy-start.5 = (bf16[32,64]{1,0:T(8,128)(2,1)S(1)}, bf16[32,64]{1,0:T(8,128)(2,1)}, u32[]{:S(2)}) copy-start(bf16[32,64]{1,0:T(8,128)(2,1)} %constant.20.clone.widen_ref) | copy-start | bytes 12292
  1.9 5.8 %copy-start.6 = (f32[16,128]{1,0:T(8,128)S(1)}, f32[16,128]{1,0:T(8,128)}, u32[]{:S(2)}) copy-start(f32[16,128]{1,0:T(8,128)} %constant.19.clone.first_ref) | copy-start | bytes 24580
  2.9 4.8 %collective-permute-start.1 = (bf16[16,2048]{1,0:T(8,128)(2,1)S(1)}, bf16[16,2048]{1,0:T(8,128)(2,1)S(1)}, u32[]{:S(2)}, u32[]{:S(2)}) collective-permute-start(bf16[16,2048]{1,0:T(8,128)(2,1)S(1)} %get-tuple-element.18), channel_id=1, source_target_pairs={{0,4},{4,0},{8,12},{12,8},{16,20},{20,16},{24,28},{28,24},{32,36},... | collective-permute-start | bytes 196616 | tf_op jit(solution)/shard_map/ppermute | solution.py:389
  6.3 1.2 %collective-permute-start = (bf16[8,2048]{1,0:T(8,128)(2,1)S(1)}, bf16[8,2048]{1,0:T(8,128)(2,1)S(1)}, u32[]{:S(2)}, u32[]{:S(2)}) collective-permute-start(bf16[8,2048]{1,0:T(8,128)(2,1)S(1)} %get-tuple-element.17.tails_ref), channel_id=1, source_target_pairs={{0,4},{4,0},{8,12},{12,8},{16,20},{20,16},{24,28},{28,24},{32,36},... | collective-permute-start | bytes 98312 | tf_op jit(solution)/shard_map/ppermute | solution.py:391
  6.4 1.3 %collective-permute-start.3 = (bf16[8,2048]{1,0:T(8,128)(2,1)S(1)}, bf16[8,2048]{1,0:T(8,128)(2,1)S(1)}, u32[]{:S(2)}, u32[]{:S(2)}) collective-permute-start(bf16[8,2048]{1,0:T(8,128)(2,1)S(1)} %collective-permute-done.2.outer_ref), channel_id=1, source_target_pairs={{0,4},{4,0},{8,12},{12,8},{16,20},{20,16},{24,28},{28,24},{32,36},... | collective-permute-start | bytes 98312 | tf_op jit(solution)/shard_map/ppermute | solution.py:390
  8.9 17.2 %all-to-all-start = ((bf16[16,8,2048]{2,1,0:T(8,128)(2,1)}), bf16[16,8,2048]{2,1,0:T(8,128)(2,1)S(1)}, u32[]{:S(2)}, u32[]{:S(2)}) async-start(bf16[16,8,2048]{2,1,0:T(8,128)(2,1)} %bitcast.6), calls=%async_computation | async-start | bytes 1048576 | tf_op jit(solution)/shard_map/all_to_all | solution.py:407
  19.3 6.9 %copy-start.3 = (bf16[1536,128]{1,0:T(8,128)(2,1)S(1)}, bf16[1536,128]{1,0:T(8,128)(2,1)}, u32[]{:S(2)}) copy-start(bf16[1536,128]{1,0:T(8,128)(2,1)} %constant.22.clone.carry_ref) | copy-start | bytes 1179652
  19.3 6.9 %copy-start.4 = (bf16[256,240]{1,0:T(8,128)(2,1)S(1)}, bf16[256,240]{1,0:T(8,128)(2,1)}, u32[]{:S(2)}) copy-start(bf16[256,240]{1,0:T(8,128)(2,1)} %constant.23.clone.spread_hbm.spread_ref) | copy-start | bytes 368644

commit v8 on v7

--- a/solution.py
+++ b/solution.py
@@ -376,7 +376,7 @@
     outer = lax.ppermute(outer, "ctx", between)
 
     near_sums, inner = pl.pallas_call(
-        functools.partial(moment_kernel, width=width),
+        functools.partial(moment_kernel, width=channels // 2),
         in_specs=[vmem, vmem] + [vmem] * 4,
         out_specs=[vmem, vmem],
         out_shape=[pltpu.VMEM((RANK, channels), F32), pltpu.VMEM((2 * RANK, channels), BF16)],

time: 27.7 us -> 27.7 us (level)
  no operation moved by 1% of the time
where the time goes in v8:
time: 27.7 us; the launch traced here: 27.4 us
  starting transfers between devices  14.9 us (54%)
  Pallas kernels  9.92 us (36%)
  waiting for transfers between devices  2.46 us (9%)
    all_to_all x1, starting transfers between devices, on_device(): lax.all_to_all(sent, 'ctx', 0, 0, axis_index_groups=groups, tiled=True)  10.3 us
    pallas_call x1, Pallas kernels, on_device(): pl.pallas_call(local_kernel, in_specs=[vmem] + [hbm] * len(local_args), o...  5.24 us
    ppermute x1, starting transfers between devices, on_device(): inner = lax.ppermute(inner, 'ctx', swap)  3.37 us
    all_to_all x1, waiting for transfers between devices, on_device(): lax.all_to_all(sent, 'ctx', 0, 0, axis_index_groups=groups, tiled=True)  1.6 us
    pallas_call x1, Pallas kernels, on_device(): pl.pallas_call(out_kernel, in_specs=[vmem] * 7, out_specs=hbm, out_shape=...  1.27 us
    pallas_call x1, Pallas kernels, on_device(): pl.pallas_call(merge_kernel, in_specs=[vmem] * 10, out_specs=[hbm, vmem],...  1.24 us
    pallas_call x1, Pallas kernels, on_device(): pl.pallas_call(edge_kernel, in_specs=[hbm, hbm, hbm], out_specs=[vmem] *...  1.14 us
    pallas_call x1, Pallas kernels, on_device(): pl.pallas_call(functools.partial(moment_kernel, width=channels // 2), in_...  1.03 us
  transfers between devices with their start and end apart: 5, of which 3 were waited for; matrix products, arithmetic and copies ran while one was open for 0% of the time, Pallas kernels for 23%

profile of v8, /device:TPU:0, one launch (start us, length us, event | category | flops | bytes accessed | tf_op | source)
XLA Modules:
  0.0 27.4 jit_solution(2340035861261022668)
XLA Ops:
  0.0 0.0 copy-start.1
  0.0 0.0 copy-start
  0.0 0.0 copy-start.2
  0.0 1.1 %edges.1 = (bf16[8,2048]{1,0:T(8,128)(2,1)S(1)}, bf16[8,2048]{1,0:T(8,128)(2,1)S(1)}, bf16[8,2048]{1,0:T(8,128)(2,1)S(1)}) custom-call(bf16[128,2048]{1,0:T(8,128)(2,1)} %q_hbm.1, bf16[128,2048]{1,0:T(8,128)(2,1)} %k_hbm.1, bf16[128,2048]{1,0:T(8,128)(2,1)} %v_hbm.1), custom_call_target="tpu_custom_call" | custom-call | tf_op jit(solution)/shard_map/edges/pallas_call | solution.py:365
  1.2 0.0 copy-start.7
  1.2 0.7 %collective-permute-start.2 = (bf16[8,2048]{1,0:T(8,128)(2,1)S(1)}, bf16[8,2048]{1,0:T(8,128)(2,1)S(1)}, u32[]{:S(2)}, u32[]{:S(2)}) collective-permute-start(bf16[8,2048]{1,0:T(8,128)(2,1)S(1)} %get-tuple-element.19), channel_id=1, source_target_pairs={{4,8},{12,16},{20,24},{28,32},{36,40},{44,48},{52,56},{60,64},{68,... | collective-permute-start | bytes 98312 | tf_op jit(solution)/shard_map/ppermute | solution.py:376
  1.8 0.0 copy-done.1
  1.8 0.0 copy-done
  1.9 0.0 copy-done.2
  1.9 0.0 copy-done.7
  1.9 0.0 copy-start.5
  1.9 0.0 copy-start.6
  1.9 1.0 %moments.1 = (f32[8,2048]{1,0:T(8,128)S(1)}, bf16[16,2048]{1,0:T(8,128)(2,1)S(1)}) custom-call(bf16[8,2048]{1,0:T(8,128)(2,1)S(1)} %get-tuple-element.16.heads_ref, bf16[8,2048]{1,0:T(8,128)(2,1)S(1)} %get-tuple-element.17.tails_ref, bf16[128,2048]{1,0:T(8,128)(2,1)S(1)} %copy-done, bf16[128,2048]{1,0:T(8,128)(2,1)S(1)} %copy-done.1, ...), custom_call_target="tpu_custom_call" | custom-call | flops 1 | bytes 1 | tf_op jit(solution)/shard_map/moments/pallas_call | solution.py:378
  2.9 3.4 %collective-permute-start.1 = (bf16[16,2048]{1,0:T(8,128)(2,1)S(1)}, bf16[16,2048]{1,0:T(8,128)(2,1)S(1)}, u32[]{:S(2)}, u32[]{:S(2)}) collective-permute-start(bf16[16,2048]{1,0:T(8,128)(2,1)S(1)} %get-tuple-element.18), channel_id=1, source_target_pairs={{0,4},{4,0},{8,12},{12,8},{16,20},{20,16},{24,28},{28,24},{32,36},... | collective-permute-start | bytes 196616 | tf_op jit(solution)/shard_map/ppermute | solution.py:389
  6.3 0.1 collective-permute-start
  6.4 0.0 collective-permute-done.2.outer_ref
  6.4 0.4 %collective-permute-start.3 = (bf16[8,2048]{1,0:T(8,128)(2,1)S(1)}, bf16[8,2048]{1,0:T(8,128)(2,1)S(1)}, u32[]{:S(2)}, u32[]{:S(2)}) collective-permute-start(bf16[8,2048]{1,0:T(8,128)(2,1)S(1)} %collective-permute-done.2.outer_ref), channel_id=1, source_target_pairs={{0,4},{4,0},{8,12},{12,8},{16,20},{20,16},{24,28},{28,24},{32,36},... | collective-permute-start | bytes 98312 | tf_op jit(solution)/shard_map/ppermute | solution.py:390
  6.8 0.7 %collective-permute-done.tails_other_ref = bf16[8,2048]{1,0:T(8,128)(2,1)S(1)} collective-permute-done((bf16[8,2048]{1,0:T(8,128)(2,1)S(1)}, bf16[8,2048]{1,0:T(8,128)(2,1)S(1)}, u32[]{:S(2)}, u32[]{:S(2)}) %collective-permute-start) | collective-permute-done | bytes 32800 | tf_op jit(solution)/shard_map/ppermute | solution.py:391
  7.5 0.2 collective-permute-done.3.outer_more_ref
  7.7 0.0 collective-permute-done.1.inner_ref
  7.7 0.0 copy-done.5
  7.7 0.0 copy-done.6
  7.7 1.2 %merge.1 = (bf16[128,2048]{1,0:T(8,128)(2,1)}, f32[16,2048]{1,0:T(8,128)S(1)}) custom-call(bf16[8,2048]{1,0:T(8,128)(2,1)S(1)} %get-tuple-element.16.heads_ref, bf16[8,2048]{1,0:T(8,128)(2,1)S(1)} %get-tuple-element.17.tails_ref, bf16[8,2048]{1,0:T(8,128)(2,1)S(1)} %collective-permute-done.tails_other_ref, ...), custom_call_target="tpu_custom_call" | custom-call | tf_op jit(solution)/shard_map/merge/pallas_call | solution.py:393
  8.9 10.3 %all-to-all-start = ((bf16[16,8,2048]{2,1,0:T(8,128)(2,1)}), bf16[16,8,2048]{2,1,0:T(8,128)(2,1)S(1)}, u32[]{:S(2)}, u32[]{:S(2)}) async-start(bf16[16,8,2048]{2,1,0:T(8,128)(2,1)} %bitcast.6), calls=%async_computation | async-start | bytes 1048576 | tf_op jit(solution)/shard_map/all_to_all | solution.py:407
  19.3 0.0 copy-start.3
  19.3 0.0 copy-start.4
  19.3 5.2 %local.1 = (bf16[128,2048]{1,0:T(8,128)(2,1)S(1)}, bf16[128,2048]{1,0:T(8,128)(2,1)S(1)}, f32[128,2048]{1,0:T(8,128)S(1)}, f32[32,2048]{1,0:T(8,128)S(1)}) custom-call(f32[16,2048]{1,0:T(8,128)S(1)} %get-tuple-element.21.side_ref, bf16[128,2048]{1,0:T(8,128)(2,1)} %q_hbm.1, bf16[128,2048]{1,0:T(8,128)(2,1)} %k_hbm.1, bf16[128,2048]{1,0:T(8,128)(2,1)} %v_hbm.1, ...), custom_call_target="tpu_custom_call" | custom-call | flops 4294967296 | bytes 4194304 | tf_op jit(solution)/shard_map/local/pallas_call | solution.py:414
  24.5 1.6 %all-to-all-done = bf16[16,8,2048]{2,1,0:T(8,128)(2,1)S(1)} async-done(((bf16[16,8,2048]{2,1,0:T(8,128)(2,1)}), bf16[16,8,2048]{2,1,0:T(8,128)(2,1)S(1)}, u32[]{:S(2)}, u32[]{:S(2)}) %all-to-all-start) | async-done | bytes 524320 | tf_op jit(solution)/shard_map/all_to_all | solution.py:407
  26.1 0.0 copy-done.3
  26.1 0.0 copy-done.4
  26.1 1.3 %output.1 = bf16[128,2048]{1,0:T(8,128)(2,1)} custom-call(bf16[128,2048]{1,0:T(8,128)(2,1)S(1)} %get-tuple-element.22.feat_ref, bf16[128,2048]{1,0:T(8,128)(2,1)S(1)} %get-tuple-element.23.full_ref, f32[128,2048]{1,0:T(8,128)S(1)} %get-tuple-element.24.local_ref, f32[32,2048]{1,0:T(8,128)S(1)} %get-tuple-element.25.weight_ref, ...), custom_call_target="tpu_custom_call" | custom-call | tf_op jit(solution)/shard_map/output/pallas_call | solution.py:433
Async XLA Ops:
  0.0 1.8 %copy-start.1 = (bf16[128,2048]{1,0:T(8,128)(2,1)S(1)}, bf16[128,2048]{1,0:T(8,128)(2,1)}, u32[]{:S(2)}) copy-start(bf16[128,2048]{1,0:T(8,128)(2,1)} %v_hbm.1) | copy-start | bytes 1572868
  0.0 1.8 %copy-start = (bf16[128,2048]{1,0:T(8,128)(2,1)S(1)}, bf16[128,2048]{1,0:T(8,128)(2,1)}, u32[]{:S(2)}) copy-start(bf16[128,2048]{1,0:T(8,128)(2,1)} %k_hbm.1) | copy-start | bytes 1572868
  0.0 1.9 %copy-start.2 = (f32[3,3,2048]{2,1,0:T(4,128)S(1)}, f32[3,3,2048]{2,1,0:T(4,128)}, u32[]{:S(2)}) copy-start(f32[3,3,2048]{2,1,0:T(4,128)} %taps_hbm.1) | copy-start | bytes 221188
  1.2 0.7 %copy-start.7 = (bf16[8,256]{1,0:T(8,128)(2,1)S(1)}, bf16[8,256]{1,0:T(8,128)(2,1)}, u32[]{:S(2)}) copy-start(bf16[8,256]{1,0:T(8,128)(2,1)} %constant.18.clone.moment_ref) | copy-start | bytes 12292
  1.2 5.2 %collective-permute-start.2 = (bf16[8,2048]{1,0:T(8,128)(2,1)S(1)}, bf16[8,2048]{1,0:T(8,128)(2,1)S(1)}, u32[]{:S(2)}, u32[]{:S(2)}) collective-permute-start(bf16[8,2048]{1,0:T(8,128)(2,1)S(1)} %get-tuple-element.19), channel_id=1, source_target_pairs={{4,8},{12,16},{20,24},{28,32},{36,40},{44,48},{52,56},{60,64},{68,... | collective-permute-start | bytes 98312 | tf_op jit(solution)/shard_map/ppermute | solution.py:376
  1.9 5.8 %copy-start.5 = (bf16[32,64]{1,0:T(8,128)(2,1)S(1)}, bf16[32,64]{1,0:T(8,128)(2,1)}, u32[]{:S(2)}) copy-start(bf16[32,64]{1,0:T(8,128)(2,1)} %constant.20.clone.widen_ref) | copy-start | bytes 12292
  1.9 5.8 %copy-start.6 = (f32[16,128]{1,0:T(8,128)S(1)}, f32[16,128]{1,0:T(8,128)}, u32[]{:S(2)}) copy-start(f32[16,128]{1,0:T(8,128)} %constant.19.clone.first_ref) | copy-start | bytes 24580
  2.9 4.8 %collective-permute-start.1 = (bf16[16,2048]{1,0:T(8,128)(2,1)S(1)}, bf16[16,2048]{1,0:T(8,128)(2,1)S(1)}, u32[]{:S(2)}, u32[]{:S(2)}) collective-permute-start(bf16[16,2048]{1,0:T(8,128)(2,1)S(1)} %get-tuple-element.18), channel_id=1, source_target_pairs={{0,4},{4,0},{8,12},{12,8},{16,20},{20,16},{24,28},{28,24},{32,36},... | collective-permute-start | bytes 196616 | tf_op jit(solution)/shard_map/ppermute | solution.py:389
  6.3 1.2 %collective-permute-start = (bf16[8,2048]{1,0:T(8,128)(2,1)S(1)}, bf16[8,2048]{1,0:T(8,128)(2,1)S(1)}, u32[]{:S(2)}, u32[]{:S(2)}) collective-permute-start(bf16[8,2048]{1,0:T(8,128)(2,1)S(1)} %get-tuple-element.17.tails_ref), channel_id=1, source_target_pairs={{0,4},{4,0},{8,12},{12,8},{16,20},{20,16},{24,28},{28,24},{32,36},... | collective-permute-start | bytes 98312 | tf_op jit(solution)/shard_map/ppermute | solution.py:391
  6.4 1.3 %collective-permute-start.3 = (bf16[8,2048]{1,0:T(8,128)(2,1)S(1)}, bf16[8,2048]{1,0:T(8,128)(2,1)S(1)}, u32[]{:S(2)}, u32[]{:S(2)}) collective-permute-start(bf16[8,2048]{1,0:T(8,128)(2,1)S(1)} %collective-permute-done.2.outer_ref), channel_id=1, source_target_pairs={{0,4},{4,0},{8,12},{12,8},{16,20},{20,16},{24,28},{28,24},{32,36},... | collective-permute-start | bytes 98312 | tf_op jit(solution)/shard_map/ppermute | solution.py:390
  8.9 17.2 %all-to-all-start = ((bf16[16,8,2048]{2,1,0:T(8,128)(2,1)}), bf16[16,8,2048]{2,1,0:T(8,128)(2,1)S(1)}, u32[]{:S(2)}, u32[]{:S(2)}) async-start(bf16[16,8,2048]{2,1,0:T(8,128)(2,1)} %bitcast.6), calls=%async_computation | async-start | bytes 1048576 | tf_op jit(solution)/shard_map/all_to_all | solution.py:407
  19.3 6.9 %copy-start.3 = (bf16[1536,128]{1,0:T(8,128)(2,1)S(1)}, bf16[1536,128]{1,0:T(8,128)(2,1)}, u32[]{:S(2)}) copy-start(bf16[1536,128]{1,0:T(8,128)(2,1)} %constant.22.clone.carry_ref) | copy-start | bytes 1179652
  19.3 6.9 %copy-start.4 = (bf16[256,240]{1,0:T(8,128)(2,1)S(1)}, bf16[256,240]{1,0:T(8,128)(2,1)}, u32[]{:S(2)}) copy-start(bf16[256,240]{1,0:T(8,128)(2,1)} %constant.23.clone.spread_hbm.spread_ref) | copy-start | bytes 368644
